TPU v7x, 512 devices: a whole 4x4x16 slice. The times are simulated.
512 devices in a mesh: group: 8 (over x, core), dom: 64 (over z, y).
Axes of the slice: x: 4, y: 4, z: 16, core: 2. Of those that a mesh axis runs over, the one named last changes fastest.
Arguments:
- node_feats: bfloat16 [131072, 512], P(('group', 'dom')), may hold values from -40 to 40
- queries: bfloat16 [131072, 512], P(('group', 'dom')), may hold values from -240 to 240
- keys: bfloat16 [131072, 512], P(('group', 'dom')), may hold values from -6.5 to 6.5
- values: bfloat16 [131072, 512], P(('group', 'dom')), may hold values from -6 to 6
- out_weight: bfloat16 [512, 512], replicated, may hold values from -0.25 to 0.25
- up_weight: bfloat16 [512, 2048], P(None, 'group'), may hold values from -0.25 to 0.25
- down_weight: bfloat16 [512, 2048], P(None, 'group'), may hold values from -0.125 to 0.125
- norm_gain: float32 [512], replicated, may hold values from 0.5 to 1.5
- tile_lists: int32 [1024, 6], P(('group', 'dom')), may hold values from -1 to 1023, as said below
- virtual_of: int32 [131072], P(('group', 'dom')), may hold values from 0 to 63
Outputs:
- layer_out: bfloat16 [131072, 512], P(('group', 'dom'))
Inputs may be any that keep to these rules, and one draw needn't show every extreme that they name: Row b of tile_lists starts with b itself, then names distinct other blocks, then -1 up to the end. Every named block c lies in the same group as b, in a partition c // 2 at most 2 away along dom from b // 2. In every draw some partitions have all of their rows full.
All inputs are finite; a program needn't handle non-finite values.
Results may differ from a plain program's by a relative error of at most 0.0095.
Values may be sent and summed in bfloat16 or wider, within the bound.
No kernel may reach another device: no remote copies, remote signals or barrier semaphores. Data moves between devices by JAX's collectives and lax.ppermute only.
A program may use at most 64 MiB of HBM per device.

v0:
```python
import math

import jax
import jax.numpy as jnp
from jax import lax
from jax.sharding import PartitionSpec as P

HEADS = 8
BLOCK = 128
VIRTUAL = 64
REACH = 2


def passed_along(shard, axis, by):
    length = lax.axis_size(axis)
    pairs = [(i, i + by) for i in range(length) if 0 <= i + by < length]
    return lax.ppermute(shard, axis, pairs)


def layer_finish(node_feats, attended, out_weight, norm_gain):
    residual = node_feats.astype(jnp.float32) + jnp.dot(
        attended, out_weight, preferred_element_type=jnp.float32
    )
    row_mean = jnp.mean(residual, axis=-1, keepdims=True)
    centered = residual - row_mean
    variance = jnp.mean(centered * centered, axis=-1, keepdims=True)
    normed = (centered * lax.rsqrt(variance + 1e-05) * norm_gain).astype(jnp.bfloat16)
    return (residual, normed)


def local(
    node_feats,
    queries,
    keys,
    values,
    out_weight,
    up_weight,
    down_weight,
    norm_gain,
    tile_lists,
    virtual_of,
):
    node_rows, feat_width = queries.shape
    head_count = HEADS
    head_dim = feat_width // head_count
    block_len = BLOCK
    block_count = node_rows // block_len
    reach = REACH
    score_scale = 1.0 / math.sqrt(head_dim)
    dom_size = lax.axis_size("dom")
    device_pos = lax.axis_index("group") * dom_size + lax.axis_index("dom")
    members = (virtual_of[None, :] == jnp.arange(VIRTUAL, dtype=jnp.int32)[:, None]).astype(
        jnp.bfloat16
    )
    key_pooled = jnp.dot(members, keys, preferred_element_type=jnp.float32)
    value_pooled = jnp.dot(members, values, preferred_element_type=jnp.float32)
    key_total, value_total = lax.psum((key_pooled, value_pooled), ("group", "dom"))
    pool_scale = math.sqrt(VIRTUAL / (node_rows * lax.axis_size("group") * dom_size))
    virtual_keys = (
        (key_total * pool_scale).astype(jnp.bfloat16).reshape(VIRTUAL, head_count, head_dim)
    )
    virtual_values = (
        (value_total * pool_scale).astype(jnp.bfloat16).reshape(VIRTUAL, head_count, head_dim)
    )
    key_value = jnp.stack([keys, values], axis=0)
    pieces = {0: key_value}
    shift_list = []
    for distance in range(1, reach + 1):
        shift_list.append(distance)
        shift_list.append(-distance)
    for shift_by in shift_list:
        pieces[-shift_by] = passed_along(key_value, "dom", shift_by)
    window = jnp.stack([pieces[offset] for offset in range(-reach, reach + 1)], axis=1)
    window_blocks = (2 * reach + 1) * block_count
    window = window.reshape(2, window_blocks, block_len, feat_width)
    present = tile_lists >= 0
    window_index = jnp.where(present, tile_lists - (device_pos - reach) * block_count, 0)
    block_mask = jnp.any(
        (window_index[:, :, None] == jnp.arange(window_blocks, dtype=jnp.int32)[None, None, :])
        & present[:, :, None],
        axis=1,
    )
    row_mask = jnp.repeat(jnp.repeat(block_mask, block_len, axis=0), block_len, axis=1)
    allowed = jnp.concatenate([row_mask, jnp.ones((node_rows, VIRTUAL), dtype=bool)], axis=1)
    all_keys = jnp.concatenate(
        [window[0].reshape(window_blocks * block_len, head_count, head_dim), virtual_keys], axis=0
    )
    all_values = jnp.concatenate(
        [window[1].reshape(window_blocks * block_len, head_count, head_dim), virtual_values], axis=0
    )
    keys_by_head = jnp.transpose(all_keys, (1, 0, 2))
    values_by_head = jnp.transpose(all_values, (1, 0, 2))
    queries_by_head = jnp.transpose(queries.reshape(node_rows, head_count, head_dim), (1, 0, 2))

    def attend_head(inputs):
        head_queries, head_keys, head_values = inputs
        head_scores = (
            lax.dot_general(
                head_queries,
                head_keys,
                (((1,), (1,)), ((), ())),
                preferred_element_type=jnp.float32,
            )
            * score_scale
        )
        head_scores = jnp.where(allowed, head_scores, -jnp.inf)
        row_max = jnp.max(head_scores, axis=-1, keepdims=True)
        exponent = jnp.exp(head_scores - row_max)
        denominator = jnp.sum(exponent, axis=-1, keepdims=True)
        numerator = jnp.dot(
            exponent.astype(jnp.bfloat16), head_values, preferred_element_type=jnp.float32
        )
        return numerator / denominator

    per_head = lax.map(attend_head, (queries_by_head, keys_by_head, values_by_head))
    attended = (
        jnp.transpose(per_head, (1, 0, 2)).reshape(node_rows, feat_width).astype(jnp.bfloat16)
    )
    residual, normed = layer_finish(node_feats, attended, out_weight, norm_gain)
    up_piece = lax.all_gather(up_weight, "group", axis=1, tiled=True)
    down_piece = lax.all_gather(down_weight, "group", axis=1, tiled=True)
    hidden = jax.nn.relu(jnp.dot(normed, up_piece, preferred_element_type=jnp.float32)).astype(
        jnp.bfloat16
    )
    ffn_out = lax.dot_general(
        hidden, down_piece, (((1,), (1,)), ((), ())), preferred_element_type=jnp.float32
    )
    return (residual + ffn_out).astype(jnp.bfloat16)


def solution(mesh):
    placed = (
        P(("group", "dom"), None),
        P(("group", "dom"), None),
        P(("group", "dom"), None),
        P(("group", "dom"), None),
        P(),
        P(None, "group"),
        P(None, "group"),
        P(),
        P(("group", "dom"), None),
        P(("group", "dom")),
    )
    return jax.shard_map(
        local, mesh=mesh, in_specs=placed, out_specs=P(("group", "dom"), None), check_vma=False
    )
```

profile of v0, /device:TPU:1, one launch (start us, length us, event | category | flops | bytes accessed | tf_op | source)
XLA Modules:
  0.0 539.0 jit_solution(6679021699994924783)
XLA Ops:
  7.4 1.9 fusion.24
  9.2 1.8 fusion.25
  11.0 0.0 all-reduce.4.cloned.1.call-update
  11.1 0.0 all-gather.3.cloned.1.call-start
  11.1 0.5 all-gather.3.cloned.1.call-update
  11.6 0.0 all-gather.5.cloned.1.call-start
  11.7 1.1 pad_maximum_fusion
  12.8 6.5 %collective-permute-start = (bf16[2,256,512]{2,1,0:T(8,128)(2,1)S(1)}, bf16[2,256,512]{2,1,0:T(8,128)(2,1)}, u32[]{:S(2)}, u32[]{:S(2)}) collective-permute-start(bf16[2,256,512]{2,1,0:T(8,128)(2,1)S(1)} %pad_maximum_fusion), channel_id=1, source_target_pairs={{0,2},{1,3},{2,4},{3,5},{4,6},{5,7},{6,8},{7,9},{8,10},{9,11},{10,... | collective-permute-start | bytes 1572872 | tf_op jit(solution)/shard_map/ppermute | solution.py:17
  19.2 3.1 collective-permute-start.1
  22.3 1.3 collective-permute-start.2
  23.6 1.3 collective-permute-start.3
  24.9 0.0 all-gather.5.cloned.1.call-update
  25.0 0.1 fusion.29
  25.1 0.1 copy.24
  25.2 0.1 broadcast_bitcast_fusion
  25.3 0.0 copy-start.3
  25.3 0.1 copy.21
  25.5 0.1 broadcast_in_dim.20
  25.6 0.3 concatenate.10
  25.9 465.4 %all-reduce.4.cloned.1.call-done = (f32[64,512]{1,0:T(8,128)}, f32[64,512]{1,0:T(8,128)}) async-done(((f32[64,512]{1,0:T(8,128)}, f32[64,512]{1,0:T(8,128)}), (f32[64,512]{1,0:T(8,128)}, f32[64,512]{1,0:T(8,128)})) %all-reduce.4.cloned.1.call-update) | async-done | bytes 262160 | tf_op jit(solution)/shard_map/psum | solution.py:57
  491.3 1.0 multiply_convert_fusion.3
  492.3 0.1 copy.31
  492.4 0.1 copy.30
  492.6 1.1 bitcast_dynamic-update-slice_fusion.4
  493.6 1.1 bitcast_dynamic-update-slice_fusion.3
  494.9 1.7 fusion.32
  496.6 3.2 copy.25
  499.7 2.3 reshape_squeeze.7
  502.0 3.2 copy.22
  505.2 2.3 reshape_squeeze.6
  507.5 1.5 maximum_bitcast_fusion.1
  509.1 0.0 copy-start.6
  509.1 0.2 copy-done.1
  509.3 1.3 maximum_bitcast_fusion
  510.5 16.0 %while.10 = (s32[]{:T(128)}, bf16[8,256,64]{1,2,0:T(8,128)(2,1)S(1)}, bf16[8,256,64]{1,2,0:T(8,128)(2,1)S(1)}, bf16[8,1344,64]{1,2,0:T(8,128)(2,1)}, pred[256,13...) while((s32[]{:T(128)}, bf16[8,256,64]{1,2,0:T(8,128)(2,1)S(1)}, ...), condition=%wide.region_6.7_spmd, body=%wide.region_3.6_spmd.sunk | while | flops 90504704 | bytes 4938829 | solution.py:115
  510.5 1.4 fusion.47
  511.9 0.3 fusion.48
  512.2 0.3 fusion.49
  512.6 1.4 fusion.47
  513.9 0.3 fusion.48
  514.2 0.3 fusion.49
  514.6 1.4 fusion.47
  515.9 0.3 fusion.48
  516.2 0.3 fusion.49
  516.6 1.4 fusion.47
  518.0 0.3 fusion.48
  518.2 0.3 fusion.49
  518.6 1.4 fusion.47
  520.0 0.3 fusion.48
  520.2 0.3 fusion.49
  520.6 1.4 fusion.47
  522.0 0.3 fusion.48
  522.2 0.3 fusion.49
  522.6 1.4 fusion.47
  524.0 0.3 fusion.48
  524.2 0.3 fusion.49
  524.6 1.4 fusion.47
  526.0 0.3 fusion.48
  526.2 0.3 fusion.49
  526.6 0.4 fusion.33
  527.0 0.2 multiply_reduce_fusion
  527.3 0.0 all-gather.3.cloned.1.call-done
  527.3 0.0 all-gather.5.cloned.1.call-done
  527.3 4.2 fusion.16
  (30 shorter events, 0.2 us)
Async XLA Ops:
  7.4 519.2 %copy-start = (bf16[512,512]{1,0:T(8,128)(2,1)S(1)}, bf16[512,512]{1,0:T(8,128)(2,1)}, u32[]{:S(2)}) copy-start(bf16[512,512]{1,0:T(8,128)(2,1)} %param.16) | copy-start | bytes 1572868
  7.4 17.6 %copy-start.7 = (s32[2,6]{1,0:T(2,128)S(1)}, s32[2,6]{1,0:T(2,128)}, u32[]{:S(2)}) copy-start(s32[2,6]{1,0:T(2,128)} %param.20) | copy-start | bytes 148
  7.4 17.9 %copy-start.4 = (bf16[256,512]{1,0:T(8,128)(2,1)S(1)}, bf16[256,512]{1,0:T(8,128)(2,1)}, u32[]{:S(2)}) copy-start(bf16[256,512]{1,0:T(8,128)(2,1)} %param.13) | copy-start | bytes 786436
  7.4 483.9 %all-reduce.4.cloned.1.call-start = ((), (), s32[]{:S(2)}) async-start(), calls=%async_computation.2 | async-start | bytes 524288 | tf_op jit(solution)/shard_map/psum | solution.py:57
  11.1 516.2 %all-gather.3.cloned.1.call-start = ((), (), s32[]{:S(2)}) async-start(), calls=%async_computation | async-start | bytes 2359296 | tf_op jit(solution)/shard_map/all_gather | solution.py:120
  11.6 515.7 %all-gather.5.cloned.1.call-start = ((), (), s32[]{:S(2)}) async-start(), calls=%async_computation.1 | async-start | bytes 2359296 | tf_op jit(solution)/shard_map/all_gather | solution.py:121
  12.8 479.8 %collective-permute-start = (bf16[2,256,512]{2,1,0:T(8,128)(2,1)S(1)}, bf16[2,256,512]{2,1,0:T(8,128)(2,1)}, u32[]{:S(2)}, u32[]{:S(2)}) collective-permute-start(bf16[2,256,512]{2,1,0:T(8,128)(2,1)S(1)} %pad_maximum_fusion), channel_id=1, source_target_pairs={{0,2},{1,3},{2,4},{3,5},{4,6},{5,7},{6,8},{7,9},{8,10},{9,11},{10,... | collective-permute-start | bytes 1572872 | tf_op jit(solution)/shard_map/ppermute | solution.py:17
  19.2 474.4 %collective-permute-start.1 = (bf16[2,256,512]{2,1,0:T(8,128)(2,1)S(1)}, bf16[2,256,512]{2,1,0:T(8,128)(2,1)}, u32[]{:S(2)}, u32[]{:S(2)}) collective-permute-start(bf16[2,256,512]{2,1,0:T(8,128)(2,1)S(1)} %pad_maximum_fusion), channel_id=1, source_target_pairs={{0,1},{1,2},{2,3},{3,4},{4,5},{5,6},{6,7},{7,8},{8,9},{9,10},{10,1... | collective-permute-start | bytes 1572872 | tf_op jit(solution)/shard_map/ppermute | solution.py:17
  22.3 472.5 %collective-permute-start.2 = (bf16[2,256,512]{2,1,0:T(8,128)(2,1)S(1)}, bf16[2,256,512]{2,1,0:T(8,128)(2,1)S(1)}, u32[]{:S(2)}, u32[]{:S(2)}) collective-permute-start(bf16[2,256,512]{2,1,0:T(8,128)(2,1)S(1)} %pad_maximum_fusion), channel_id=1, source_target_pairs={{1,0},{2,1},{3,2},{4,3},{5,4},{6,5},{7,6},{8,7},{9,8},{10,9},{11,1... | collective-permute-start | bytes 1572872 | tf_op jit(solution)/shard_map/ppermute | solution.py:17
  23.6 471.2 %collective-permute-start.3 = (bf16[2,256,512]{2,1,0:T(8,128)(2,1)S(1)}, bf16[2,256,512]{2,1,0:T(8,128)(2,1)S(1)}, u32[]{:S(2)}, u32[]{:S(2)}) collective-permute-start(bf16[2,256,512]{2,1,0:T(8,128)(2,1)S(1)} %pad_maximum_fusion), channel_id=1, source_target_pairs={{2,0},{3,1},{4,2},{5,3},{6,4},{7,5},{8,6},{9,7},{10,8},{11,9},{12,... | collective-permute-start | bytes 1572872 | tf_op jit(solution)/shard_map/ppermute | solution.py:17
  25.3 469.4 %copy-start.2 = (bf16[256,512]{1,0:T(8,128)(2,1)S(1)}, bf16[256,512]{1,0:T(8,128)(2,1)}, u32[]{:S(2)}) copy-start(bf16[256,512]{1,0:T(8,128)(2,1)} %param.14) | copy-start | bytes 786436
  25.3 469.4 %copy-start.3 = (bf16[256,512]{1,0:T(8,128)(2,1)S(1)}, bf16[256,512]{1,0:T(8,128)(2,1)}, u32[]{:S(2)}) copy-start(bf16[256,512]{1,0:T(8,128)(2,1)} %param.15) | copy-start | bytes 786436
  507.5 1.7 copy-start.1
  509.1 1.4 copy-start.6
  510.5 16.1 %copy-start.5 = (bf16[256,512]{1,0:T(8,128)(2,1)S(1)}, bf16[256,512]{1,0:T(8,128)(2,1)}, u32[]{:S(2)}) copy-start(bf16[256,512]{1,0:T(8,128)(2,1)} %param.12) | copy-start | bytes 786436
  526.6 0.7 copy-start.8
Sparse Core Ops, SparseCore 0:
  13.7 477.5 all-reduce.3
Sparse Core Ops, SparseCore 1:
  13.9 40.5 all-gather.2
  56.6 35.5 all-gather.4
where the time goes:
time: 540 us; the launch traced here: 539 us
  waiting for transfers between devices  466 us (86%)
  matrix products  22 us (4%)
  local copies, waits for them, and re-layouts  16.1 us (3%)
  between operations  15.2 us (3%)
  starting transfers between devices  12.2 us (2%)
  other arithmetic  7.39 us (1%)
    psum x1, waiting for transfers between devices, local(): lax.psum((key_pooled, value_pooled), ('group', 'dom'))  465 us
    ppermute x4, starting transfers between devices, passed_along(): return lax.ppermute(shard, axis, pairs)  12.1 us
    dot_general x8, matrix products, attend_head(): lax.dot_general(head_queries, head_keys, (((1,), (1,)), ((), ())), prefer...  11 us
  transfers between devices with their start and end apart: 7, of which 1 were waited for; matrix products, arithmetic and copies ran while one was open for 7% of the time, Pallas kernels for 0%

commit v1 on v0

v1 whole, which is shorter than its diff:
```python
import math

import jax
import jax.numpy as jnp
from jax import lax
from jax.experimental import pallas as pl
from jax.experimental.pallas import tpu as pltpu
from jax.sharding import Mesh
from jax.sharding import PartitionSpec as P

HEADS = 8
BLOCK = 128
VIRTUAL = 64
REACH = 2
TMAX = 6
LANES = 128
LOG2E = 1.4426950408889634
AXES = ("x", "c", "z", "y")
DOM = ("z", "y")
PLANE = ("x", "c", "y")
VMEM = pltpu.VMEM
F32 = jnp.float32
BF16 = jnp.bfloat16


def pool_kernel(virtual_of, keys, values, up, down, sums, key_value, weights):
    node_rows, feat_width = keys.shape
    ids = lax.broadcasted_iota(jnp.int32, (VIRTUAL, node_rows), 0)
    members = jnp.where(virtual_of[...] == ids, 1.0, 0.0).astype(BF16)
    per_part = sums.shape[1]
    lane_parts = feat_width // LANES
    rows_parts = VIRTUAL // per_part
    for which, source in enumerate((keys, values)):
        pooled = jnp.dot(members, source[...], preferred_element_type=F32)
        for row in range(rows_parts):
            for lane in range(lane_parts):
                sums[(which * rows_parts + row) * lane_parts + lane] = pooled[
                    row * per_part : (row + 1) * per_part, lane * LANES : (lane + 1) * LANES
                ]
        key_value[which] = source[...]
    weights[0] = up[...]
    weights[1] = down[...]


def layer_kernel(
    tile_lists,
    queries,
    node_feats,
    out_weight,
    norm_gain,
    virtual_kv,
    kv_m2,
    kv_m1,
    kv_0,
    kv_p1,
    kv_p2,
    w_0,
    w_1,
    w_2,
    w_3,
    w_far,
    layer_out,
    window,
    weights,
    kv_sem,
    w_sem,
    attended,
):
    feat_width = queries.shape[1]
    head_dim = feat_width // HEADS
    pieces = (kv_m2, kv_m1, kv_0, kv_p1, kv_p2)
    rows = kv_0.shape[1]
    copies = [
        pltpu.make_async_copy(piece, window.at[:, pl.ds(i * rows, rows)], kv_sem.at[i])
        for i, piece in enumerate(pieces)
    ]
    near = (w_0, w_1, w_2, w_3)
    w_copies = [
        pltpu.make_async_copy(piece, weights.at[i], w_sem.at[i]) for i, piece in enumerate(near)
    ]
    w_copies.append(
        pltpu.make_async_copy(w_far, weights.at[pl.ds(len(near), len(near))], w_sem.at[len(near)])
    )
    for copy in copies:
        copy.start()
    for copy in w_copies:
        copy.start()
    for copy in copies:
        copy.wait()

    first_block = tile_lists[0, 0] - REACH * (rows // BLOCK)
    scale = LOG2E / math.sqrt(head_dim)
    lane_parts = feat_width // LANES
    per_part = virtual_kv.shape[1]
    rows_parts = VIRTUAL // per_part
    low = lax.broadcasted_iota(jnp.int32, (BLOCK, LANES), 1) < head_dim
    for block in range(rows // BLOCK):
        own = tile_lists[block, 0]
        starts = []
        shown = []
        for slot in range(TMAX):
            tile = tile_lists[block, slot]
            there = tile >= 0
            place = jnp.where(there, tile, own) - first_block
            starts.append(pl.multiple_of(place * BLOCK, BLOCK))
            shown.append(jnp.where(there, 1.0, 0.0))
        for part in range(lane_parts):
            lanes = slice(part * LANES, (part + 1) * LANES)
            pair = queries[block * BLOCK : (block + 1) * BLOCK, lanes]
            zero = jnp.zeros_like(pair)
            both = jnp.concatenate([jnp.where(low, pair, zero), jnp.where(low, zero, pair)], axis=0)
            all_keys = jnp.concatenate(
                [window[0, pl.ds(s, BLOCK), lanes] for s in starts]
                + [virtual_kv[r * lane_parts + part] for r in range(rows_parts)],
                axis=0,
            )
            scores = lax.dot_general(
                both, all_keys, (((1,), (1,)), ((), ())), preferred_element_type=F32
            )
            row_max = jnp.max(scores, axis=-1, keepdims=True)
            exponent = jnp.exp2(scores * scale - row_max * scale).astype(BF16)
            value_rows = [window[1, pl.ds(s, BLOCK), lanes] for s in starts]
            ones = [jnp.full((BLOCK, LANES), there, F32).astype(BF16) for there in shown]
            value_rows = [v * o for v, o in zip(value_rows, ones)]
            value_rows += [
                virtual_kv[(rows_parts + r) * lane_parts + part] for r in range(rows_parts)
            ]
            ones.append(jnp.ones((VIRTUAL, LANES), BF16))
            right = jnp.concatenate(
                [jnp.concatenate(value_rows, axis=0), jnp.concatenate(ones, axis=0)], axis=1
            )
            summed = jnp.dot(exponent, right, preferred_element_type=F32)
            result = summed[:, :LANES] / summed[:, LANES:]
            attended[block * BLOCK : (block + 1) * BLOCK, lanes] = jnp.where(
                low, result[:BLOCK], result[BLOCK:]
            ).astype(BF16)

    residual = node_feats[...].astype(F32) + jnp.dot(
        attended[...], out_weight[...], preferred_element_type=F32
    )
    row_mean = jnp.mean(residual, axis=-1, keepdims=True)
    centered = residual - row_mean
    variance = jnp.mean(centered * centered, axis=-1, keepdims=True)
    normed = (centered * lax.rsqrt(variance + 1e-05) * norm_gain[...]).astype(BF16)
    for copy in w_copies:
        copy.wait()
    total = residual
    for shard in range(2 * len(near)):
        hidden = jnp.dot(normed, weights[shard, 0], preferred_element_type=F32)
        hidden = jnp.maximum(hidden, 0.0).astype(BF16)
        total = total + lax.dot_general(
            hidden, weights[shard, 1], (((1,), (1,)), ((), ())), preferred_element_type=F32
        )
    layer_out[...] = total.astype(BF16)


def along_dom(shard, by):
    length = lax.axis_size(DOM)
    pairs = [(i, i + by) for i in range(length) if 0 <= i + by < length]
    return lax.ppermute(shard, DOM, pairs)


def around(shard, axis, by):
    length = lax.axis_size(axis)
    return lax.ppermute(shard, axis, [(i, (i + by) % length) for i in range(length)])


def exchanged(parts, axes):
    return lax.all_to_all(parts, axes, 0, 0, tiled=True)


def local(
    node_feats,
    queries,
    keys,
    values,
    out_weight,
    up_weight,
    down_weight,
    norm_gain,
    tile_lists,
    virtual_of,
):
    node_rows, feat_width = queries.shape
    plane = lax.axis_size(PLANE)
    depth = lax.axis_size("z")
    per_part = 2 * VIRTUAL * feat_width // LANES // plane
    own_hidden = up_weight.shape[1]
    in_vmem = pl.BlockSpec(memory_space=VMEM)
    anywhere = pl.BlockSpec(memory_space=pl.ANY)
    sums, key_value, w_0 = pl.pallas_call(
        pool_kernel,
        out_shape=(
            jax.ShapeDtypeStruct((plane, per_part, LANES), F32),
            jax.ShapeDtypeStruct((2, node_rows, feat_width), BF16),
            jax.ShapeDtypeStruct((2, feat_width, own_hidden), BF16),
        ),
        in_specs=[in_vmem] * 5,
        out_specs=(in_vmem,) * 3,
        name="pool",
    )(virtual_of.reshape(1, node_rows), keys, values, up_weight, down_weight)

    pieces = {offset: along_dom(key_value, -offset) for offset in (-1, 1, -2, 2)}
    w_1 = around(w_0, "x", 1)
    w_2 = around(w_0, "x", -1)
    w_3 = around(w_0, "x", 2)
    w_far = around(jnp.stack([w_0, w_1, w_2, w_3]), "c", 1)

    plane_sum = jnp.sum(exchanged(sums, PLANE), axis=0, keepdims=True)
    everywhere = exchanged(jnp.broadcast_to(plane_sum, (depth, per_part, LANES)), "z")
    pool_scale = math.sqrt(VIRTUAL / (node_rows * lax.axis_size(AXES)))
    pooled = (jnp.sum(everywhere, axis=0, keepdims=True) * pool_scale).astype(BF16)
    virtual_kv = exchanged(jnp.broadcast_to(pooled, (plane, per_part, LANES)), PLANE)

    return pl.pallas_call(
        layer_kernel,
        out_shape=jax.ShapeDtypeStruct((node_rows, feat_width), BF16),
        in_specs=[pl.BlockSpec(memory_space=pltpu.SMEM)] + [in_vmem] * 5 + [anywhere] * 10,
        out_specs=in_vmem,
        scratch_shapes=[
            VMEM((2, (2 * REACH + 1) * node_rows, feat_width), BF16),
            VMEM((8, 2, feat_width, own_hidden), BF16),
            pltpu.SemaphoreType.DMA((2 * REACH + 1,)),
            pltpu.SemaphoreType.DMA((5,)),
            VMEM((node_rows, feat_width), BF16),
        ],
        compiler_params=pltpu.CompilerParams(vmem_limit_bytes=32 * 1024 * 1024),
        name="layer",
    )(
        tile_lists,
        queries,
        node_feats,
        out_weight,
        norm_gain.reshape(1, feat_width),
        virtual_kv,
        pieces[-2],
        pieces[-1],
        key_value,
        pieces[1],
        pieces[2],
        w_0,
        w_1,
        w_2,
        w_3,
        w_far,
    )


def solution(mesh):
    group, dom = mesh.devices.shape
    fine = Mesh(mesh.devices.reshape(group // 2, 2, dom // 4, 4), AXES)
    placed = (
        P(AXES, None),
        P(AXES, None),
        P(AXES, None),
        P(AXES, None),
        P(),
        P(None, ("x", "c")),
        P(None, ("x", "c")),
        P(),
        P(AXES, None),
        P(AXES),
    )
    return jax.shard_map(
        local, mesh=fine, in_specs=placed, out_specs=P(AXES, None), check_vma=False
    )
```

time: 540 us -> 136 us (0.25)
  waiting for transfers between devices: 466 us -> 50.2 us
  starting transfers between devices: 12.2 us -> 47.4 us
  matrix products: 22 us -> 0 us
  blocking collectives: 0 us -> 15.9 us
  between operations: 15.2 us -> 0.15 us
  Pallas kernels: 0 us -> 10.8 us
  local copies, waits for them, and re-layouts: 16.1 us -> 6.48 us
    psum x1 -> x0, waiting for transfers between devices: 465 us -> none  [local(): lax.psum((key_pooled, value_pooled), ('group', 'dom'))]
    ppermute x4 -> x8, waiting for transfers between devices: 0.01 us -> 45.9 us  [the longest x4 28.1 us: along_dom(): return lax.ppermute(shard, DOM, pairs)]
    all_to_all x0 -> x2, starting transfers between devices: none -> 22.2 us  [exchanged(): return lax.all_to_all(parts, axes, 0, 0, tiled=True)]
    dot_general x20 -> x0, matrix products: 22 us -> none  [the longest x8 11 us: attend_head(): lax.dot_general(head_queries, head_keys, (((1,), (1,)), ((), ())), prefer...]
    all_to_all x0 -> x1, blocking collectives: none -> 15.9 us  [exchanged(): return lax.all_to_all(parts, axes, 0, 0, tiled=True)]
    ppermute x4 -> x8, starting transfers between devices: 12.1 us -> 25.3 us  [the longest x4 15.9 us: around(): lax.ppermute(shard, axis, [(i, (i + by) % length) for i in range(length)])]
    pallas_call x0 -> x2, Pallas kernels: none -> 10.8 us  [the longest x1 8.45 us: local(): pl.pallas_call(layer_kernel, out_shape=jax.ShapeDtypeStruct((node_rows, f...]
    slice x3 -> x0, local copies, waits for them, and re-layouts: 8 us -> none  [the longest x2 4.83 us: local(): window[1].reshape(window_blocks * block_len, head_count, head_dim)]
  transfers between devices with their start and end apart: 7 -> 10, of which waited for: 1 -> 7; matrix products, arithmetic and copies ran while one was open for 7% -> 2% of each run, Pallas kernels for 0% -> 0%
where the time goes in v1:
time: 136 us; the launch traced here: 135 us
  waiting for transfers between devices  50.2 us (37%)
  starting transfers between devices  47.4 us (35%)
  blocking collectives  15.9 us (12%)
  Pallas kernels  10.8 us (8%)
  local copies, waits for them, and re-layouts  6.48 us (5%)
  other arithmetic  3.86 us (3%)
    ppermute x4, waiting for transfers between devices, along_dom(): return lax.ppermute(shard, DOM, pairs)  28.1 us
    all_to_all x2, starting transfers between devices, exchanged(): return lax.all_to_all(parts, axes, 0, 0, tiled=True)  22.2 us
    ppermute x4, waiting for transfers between devices, around(): lax.ppermute(shard, axis, [(i, (i + by) % length) for i in range(length)])  17.8 us
    ppermute x4, starting transfers between devices, around(): lax.ppermute(shard, axis, [(i, (i + by) % length) for i in range(length)])  15.9 us
    all_to_all x1, blocking collectives, exchanged(): return lax.all_to_all(parts, axes, 0, 0, tiled=True)  15.9 us
    ppermute x4, starting transfers between devices, along_dom(): return lax.ppermute(shard, DOM, pairs)  9.4 us
    pallas_call x1, Pallas kernels, local(): pl.pallas_call(layer_kernel, out_shape=jax.ShapeDtypeStruct((node_rows, f...  8.45 us
    unnamed x24, local copies, waits for them, and re-layouts  5.14 us
  transfers between devices with their start and end apart: 10, of which 7 were waited for; matrix products, arithmetic and copies ran while one was open for 2% of the time, Pallas kernels for 0%

profile of v1, /device:TPU:1, one launch (start us, length us, event | category | flops | bytes accessed | tf_op | source)
XLA Modules:
  0.0 134.8 jit_solution(4344233504255368936)
XLA Ops:
  0.0 2.3 %pool.1 = (f32[32,16,128]{2,1,0:T(8,128)}, bf16[2,256,512]{2,1,0:T(8,128)(2,1)}, bf16[2,512,256]{2,1,0:T(8,128)(2,1)}) custom-call(s32[1,256]{1,0:T(1,128)} %bitcast.11, bf16[256,512]{1,0:T(8,128)(2,1)} %keys.1, bf16[256,512]{1,0:T(8,128)(2,1)} %values.1, bf16[512,256]{1,0:T(8,128)(2,1)} %up.1, bf16[512,256]{1,0:T(8,128)(2,1)} %down.1), custom_call_target="tpu_custom_call" | custom-call | tf_op jit(solution)/shard_map/pool/pallas_call | solution.py:191
  2.3 3.9 %collective-permute-start.4 = (bf16[2,512,256]{2,1,0:T(8,128)(2,1)}, bf16[2,512,256]{2,1,0:T(8,128)(2,1)S(1)}, u32[]{:S(2)}, u32[]{:S(2)}) collective-permute-start(bf16[2,512,256]{2,1,0:T(8,128)(2,1)} %get-tuple-element.10.w_0), channel_id=1, source_target_pairs={{0,128},{128,256},{256,384},{384,0},{1,129},{129,257},{257,385},{3... | collective-permute-start | bytes 1572872 | tf_op jit(solution)/shard_map/ppermute | solution.py:165
  6.3 3.2 %collective-permute-start.5 = (bf16[2,512,256]{2,1,0:T(8,128)(2,1)}, bf16[2,512,256]{2,1,0:T(8,128)(2,1)S(1)}, u32[]{:S(2)}, u32[]{:S(2)}) collective-permute-start(bf16[2,512,256]{2,1,0:T(8,128)(2,1)} %get-tuple-element.10.w_0), channel_id=1, source_target_pairs={{0,384},{128,0},{256,128},{384,256},{1,385},{129,1},{257,129},{385... | collective-permute-start | bytes 1572872 | tf_op jit(solution)/shard_map/ppermute | solution.py:165
  9.5 3.6 %collective-permute-start.6 = (bf16[2,512,256]{2,1,0:T(8,128)(2,1)}, bf16[2,512,256]{2,1,0:T(8,128)(2,1)S(1)}, u32[]{:S(2)}, u32[]{:S(2)}) collective-permute-start(bf16[2,512,256]{2,1,0:T(8,128)(2,1)} %get-tuple-element.10.w_0), channel_id=1, source_target_pairs={{0,256},{128,384},{256,0},{384,128},{1,257},{129,385},{257,1},{385... | collective-permute-start | bytes 1572872 | tf_op jit(solution)/shard_map/ppermute | solution.py:165
  13.1 1.2 collective-permute-done.4.w_1
  14.3 2.6 %collective-permute-done.5.w_2 = bf16[2,512,256]{2,1,0:T(8,128)(2,1)S(1)} collective-permute-done((bf16[2,512,256]{2,1,0:T(8,128)(2,1)}, bf16[2,512,256]{2,1,0:T(8,128)(2,1)S(1)}, u32[]{:S(2)}, u32[]{:S(2)}) %collective-permute-start.5) | collective-permute-done | bytes 524320 | tf_op jit(solution)/shard_map/ppermute | solution.py:165
  17.0 0.0 copy-start.1
  17.0 14.0 %collective-permute-done.6.w_3 = bf16[2,512,256]{2,1,0:T(8,128)(2,1)S(1)} collective-permute-done((bf16[2,512,256]{2,1,0:T(8,128)(2,1)}, bf16[2,512,256]{2,1,0:T(8,128)(2,1)S(1)}, u32[]{:S(2)}, u32[]{:S(2)}) %collective-permute-start.6) | collective-permute-done | bytes 524320 | tf_op jit(solution)/shard_map/ppermute | solution.py:165
  30.9 0.0 copy-start.3
  30.9 0.0 copy-start.11
  30.9 0.0 copy-start
  30.9 0.0 copy-start.7
  30.9 0.0 copy-start.9
  30.9 0.0 copy-start.10
  31.0 2.9 %pad_maximum_fusion = bf16[4,2,512,256]{3,2,1,0:T(8,128)(2,1)} fusion(bf16[1,2,512,256]{3,2,1,0:T(8,128)(2,1)S(1)} %bitcast.9, bf16[1,2,512,256]{3,2,1,0:T(8,128)(2,1)S(1)} %bitcast.8, bf16[1,2,512,256]{3,2,1,0:T(8,128)(2,1)S(1)} %bitcast.7, bf16[1,2,512,256]{3,2,1,0:T(8,128)(2,1)} %bitcast.6), kind=kLoop, calls=%fused_computation | loop fusion | flops 3145728 | bytes 4194304 | tf_op jit(solution)/shard_map/stack | solution.py:207
  33.8 0.0 copy-done.1
  33.8 0.0 copy-done.3
  33.8 5.1 %collective-permute-start.7 = (bf16[4,2,512,256]{3,2,1,0:T(8,128)(2,1)}, bf16[4,2,512,256]{3,2,1,0:T(8,128)(2,1)S(1)}, u32[]{:S(2)}, u32[]{:S(2)}) collective-permute-start(bf16[4,2,512,256]{3,2,1,0:T(8,128)(2,1)} %pad_maximum_fusion), channel_id=1, source_target_pairs={{0,64},{64,0},{1,65},{65,1},{2,66},{66,2},{3,67},{67,3},{4,68},{68... | collective-permute-start | bytes 6291464 | tf_op jit(solution)/shard_map/ppermute | solution.py:165
  39.0 0.0 copy-done.11
  39.0 15.9 %all_to_all.15 = f32[32,16,128]{2,1,0:T(8,128)} all-to-all(f32[32,16,128]{2,1,0:T(8,128)S(1)} %copy-done.11), channel_id=1, replica_groups=mesh['x'=4,'c'=2,'z'=16,'y'=4] {'x','c','y'}, dimensions={0} | all-to-all | bytes 524288 | tf_op jit(solution)/shard_map/all_to_all | solution.py:169
  54.8 1.0 reduce_sum.18
  55.8 0.7 broadcast_in_dim.4
  56.5 14.9 %all-to-all-start.1 = ((f32[16,16,128]{2,1,0:T(8,128)}), f32[16,16,128]{2,1,0:T(8,128)S(1)}, u32[]{:S(2)}, u32[]{:S(2)}) async-start(f32[16,16,128]{2,1,0:T(8,128)} %broadcast_in_dim.4), calls=%async_computation.1 | async-start | bytes 262144 | tf_op jit(solution)/shard_map/all_to_all | solution.py:169
  71.4 3.5 %collective-permute-start = (bf16[2,256,512]{2,1,0:T(8,128)(2,1)}, bf16[2,256,512]{2,1,0:T(8,128)(2,1)}, u32[]{:S(2)}, u32[]{:S(2)}) collective-permute-start(bf16[2,256,512]{2,1,0:T(8,128)(2,1)} %get-tuple-element.9.kv_0), channel_id=1, source_target_pairs={{0,2},{1,3},{2,4},{3,5},{4,6},{5,7},{6,8},{7,9},{8,10},{9,11},{10,... | collective-permute-start | bytes 1572872 | tf_op jit(solution)/shard_map/ppermute | solution.py:160
  75.0 3.3 %collective-permute-start.1 = (bf16[2,256,512]{2,1,0:T(8,128)(2,1)}, bf16[2,256,512]{2,1,0:T(8,128)(2,1)}, u32[]{:S(2)}, u32[]{:S(2)}) collective-permute-start(bf16[2,256,512]{2,1,0:T(8,128)(2,1)} %get-tuple-element.9.kv_0), channel_id=1, source_target_pairs={{0,1},{1,2},{2,3},{3,4},{4,5},{5,6},{6,7},{7,8},{8,9},{9,10},{10,1... | collective-permute-start | bytes 1572872 | tf_op jit(solution)/shard_map/ppermute | solution.py:160
  78.2 1.3 collective-permute-start.2
  79.5 1.3 collective-permute-start.3
  80.8 2.6 %all-to-all-done.1 = f32[16,16,128]{2,1,0:T(8,128)S(1)} async-done(((f32[16,16,128]{2,1,0:T(8,128)}), f32[16,16,128]{2,1,0:T(8,128)S(1)}, u32[]{:S(2)}, u32[]{:S(2)}) %all-to-all-start.1) | async-done | bytes 131104 | tf_op jit(solution)/shard_map/all_to_all | solution.py:169
  83.5 0.7 broadcast_in_dim.5
  84.1 7.2 %all-to-all-start.2 = ((bf16[32,16,128]{2,1,0:T(8,128)(2,1)}), bf16[32,16,128]{2,1,0:T(8,128)(2,1)S(1)}, u32[]{:S(2)}, u32[]{:S(2)}) async-start(bf16[32,16,128]{2,1,0:T(8,128)(2,1)} %broadcast_in_dim.5), calls=%async_computation.2 | async-start | bytes 262144 | tf_op jit(solution)/shard_map/all_to_all | solution.py:169
  91.4 0.0 collective-permute-done.kv_m2
  91.4 5.9 %collective-permute-done.1.kv_m1 = bf16[2,256,512]{2,1,0:T(8,128)(2,1)} collective-permute-done((bf16[2,256,512]{2,1,0:T(8,128)(2,1)}, bf16[2,256,512]{2,1,0:T(8,128)(2,1)}, u32[]{:S(2)}, u32[]{:S(2)}) %collective-permute-start.1) | collective-permute-done | bytes 524320 | tf_op jit(solution)/shard_map/ppermute | solution.py:160
  97.3 22.2 %collective-permute-done.2.kv_p1 = bf16[2,256,512]{2,1,0:T(8,128)(2,1)} collective-permute-done((bf16[2,256,512]{2,1,0:T(8,128)(2,1)}, bf16[2,256,512]{2,1,0:T(8,128)(2,1)}, u32[]{:S(2)}, u32[]{:S(2)}) %collective-permute-start.2) | collective-permute-done | bytes 524320 | tf_op jit(solution)/shard_map/ppermute | solution.py:160
  119.5 0.0 collective-permute-done.3.kv_p2
  119.5 1.7 %all-to-all-done.2.virtual_kv = bf16[32,16,128]{2,1,0:T(8,128)(2,1)S(1)} async-done(((bf16[32,16,128]{2,1,0:T(8,128)(2,1)}), bf16[32,16,128]{2,1,0:T(8,128)(2,1)S(1)}, u32[]{:S(2)}, u32[]{:S(2)}) %all-to-all-start.2) | async-done | bytes 131104 | tf_op jit(solution)/shard_map/all_to_all | solution.py:169
  121.2 0.0 collective-permute-done.7.w_far
  121.2 0.0 copy-done
  121.3 0.0 copy-done.7
  121.3 0.0 copy-done.9
  121.3 0.0 copy-done.10
  121.3 0.0 copy-start.2
  121.3 1.0 copy-done.2
  122.3 0.0 copy-start.4
  122.3 1.0 copy-done.4
  123.4 0.0 copy-start.5
  123.4 1.0 copy-done.5
  124.4 0.0 copy-start.6
  124.4 1.0 copy-done.6
  125.4 0.0 copy-start.8
  125.4 0.9 copy-done.8
  126.4 8.4 %layer.1 = bf16[256,512]{1,0:T(8,128)(2,1)} custom-call(s32[2,6]{1,0:T(2,128)S(1)} %copy-done.10, bf16[256,512]{1,0:T(8,128)(2,1)S(1)} %copy-done.7, bf16[256,512]{1,0:T(8,128)(2,1)S(1)} %copy-done.8, bf16[512,512]{1,0:T(8,128)(2,1)S(1)} %copy-done.5, f32[1,512]{1,0:T(1,128)S(1)} %bitcast.10, bf16[32,16,128]{2,1,0:T(8,128)(2,1)S(1)} %all-to-all-done.2.virtual_kv, ...), custom_call_target="tpu_custom_call" | custom-call | tf_op jit(solution)/shard_map/layer/pallas_call | solution.py:215
  (2 shorter events, 0.0 us)
Async XLA Ops:
  2.3 12.0 %collective-permute-start.4 = (bf16[2,512,256]{2,1,0:T(8,128)(2,1)}, bf16[2,512,256]{2,1,0:T(8,128)(2,1)S(1)}, u32[]{:S(2)}, u32[]{:S(2)}) collective-permute-start(bf16[2,512,256]{2,1,0:T(8,128)(2,1)} %get-tuple-element.10.w_0), channel_id=1, source_target_pairs={{0,128},{128,256},{256,384},{384,0},{1,129},{129,257},{257,385},{3... | collective-permute-start | bytes 1572872 | tf_op jit(solution)/shard_map/ppermute | solution.py:165
  6.3 10.7 %collective-permute-start.5 = (bf16[2,512,256]{2,1,0:T(8,128)(2,1)}, bf16[2,512,256]{2,1,0:T(8,128)(2,1)S(1)}, u32[]{:S(2)}, u32[]{:S(2)}) collective-permute-start(bf16[2,512,256]{2,1,0:T(8,128)(2,1)} %get-tuple-element.10.w_0), channel_id=1, source_target_pairs={{0,384},{128,0},{256,128},{384,256},{1,385},{129,1},{257,129},{385... | collective-permute-start | bytes 1572872 | tf_op jit(solution)/shard_map/ppermute | solution.py:165
  9.5 21.4 %collective-permute-start.6 = (bf16[2,512,256]{2,1,0:T(8,128)(2,1)}, bf16[2,512,256]{2,1,0:T(8,128)(2,1)S(1)}, u32[]{:S(2)}, u32[]{:S(2)}) collective-permute-start(bf16[2,512,256]{2,1,0:T(8,128)(2,1)} %get-tuple-element.10.w_0), channel_id=1, source_target_pairs={{0,256},{128,384},{256,0},{384,128},{1,257},{129,385},{257,1},{385... | collective-permute-start | bytes 1572872 | tf_op jit(solution)/shard_map/ppermute | solution.py:165
  17.0 16.9 %copy-start.1 = (bf16[2,512,256]{2,1,0:T(8,128)(2,1)}, bf16[2,512,256]{2,1,0:T(8,128)(2,1)S(1)}, u32[]{:S(2)}) copy-start(bf16[2,512,256]{2,1,0:T(8,128)(2,1)S(1)} %collective-permute-done.5.w_2) | copy-start | bytes 1572868
  30.9 2.9 %copy-start.3 = (bf16[2,512,256]{2,1,0:T(8,128)(2,1)}, bf16[2,512,256]{2,1,0:T(8,128)(2,1)S(1)}, u32[]{:S(2)}) copy-start(bf16[2,512,256]{2,1,0:T(8,128)(2,1)S(1)} %collective-permute-done.6.w_3) | copy-start | bytes 1572868
  30.9 8.0 %copy-start.11 = (f32[32,16,128]{2,1,0:T(8,128)S(1)}, f32[32,16,128]{2,1,0:T(8,128)}, u32[]{:S(2)}) copy-start(f32[32,16,128]{2,1,0:T(8,128)} %get-tuple-element.8) | copy-start | bytes 786436
  30.9 90.3 %copy-start = (bf16[2,512,256]{2,1,0:T(8,128)(2,1)S(1)}, bf16[2,512,256]{2,1,0:T(8,128)(2,1)}, u32[]{:S(2)}) copy-start(bf16[2,512,256]{2,1,0:T(8,128)(2,1)} %get-tuple-element.10.w_0) | copy-start | bytes 1572868
  30.9 90.3 %copy-start.7 = (bf16[256,512]{1,0:T(8,128)(2,1)S(1)}, bf16[256,512]{1,0:T(8,128)(2,1)}, u32[]{:S(2)}) copy-start(bf16[256,512]{1,0:T(8,128)(2,1)} %queries.1) | copy-start | bytes 786436
  30.9 90.3 %copy-start.9 = (f32[512]{0:T(512)S(1)}, f32[512]{0:T(512)}, u32[]{:S(2)}) copy-start(f32[512]{0:T(512)} %param.17) | copy-start | bytes 6148
  30.9 90.3 %copy-start.10 = (s32[2,6]{1,0:T(2,128)S(1)}, s32[2,6]{1,0:T(2,128)}, u32[]{:S(2)}) copy-start(s32[2,6]{1,0:T(2,128)} %tile_lists.1) | copy-start | bytes 148
  33.8 87.4 %collective-permute-start.7 = (bf16[4,2,512,256]{3,2,1,0:T(8,128)(2,1)}, bf16[4,2,512,256]{3,2,1,0:T(8,128)(2,1)S(1)}, u32[]{:S(2)}, u32[]{:S(2)}) collective-permute-start(bf16[4,2,512,256]{3,2,1,0:T(8,128)(2,1)} %pad_maximum_fusion), channel_id=1, source_target_pairs={{0,64},{64,0},{1,65},{65,1},{2,66},{66,2},{3,67},{67,3},{4,68},{68... | collective-permute-start | bytes 6291464 | tf_op jit(solution)/shard_map/ppermute | solution.py:165
  56.5 26.9 %all-to-all-start.1 = ((f32[16,16,128]{2,1,0:T(8,128)}), f32[16,16,128]{2,1,0:T(8,128)S(1)}, u32[]{:S(2)}, u32[]{:S(2)}) async-start(f32[16,16,128]{2,1,0:T(8,128)} %broadcast_in_dim.4), calls=%async_computation.1 | async-start | bytes 262144 | tf_op jit(solution)/shard_map/all_to_all | solution.py:169
  71.4 20.0 %collective-permute-start = (bf16[2,256,512]{2,1,0:T(8,128)(2,1)}, bf16[2,256,512]{2,1,0:T(8,128)(2,1)}, u32[]{:S(2)}, u32[]{:S(2)}) collective-permute-start(bf16[2,256,512]{2,1,0:T(8,128)(2,1)} %get-tuple-element.9.kv_0), channel_id=1, source_target_pairs={{0,2},{1,3},{2,4},{3,5},{4,6},{5,7},{6,8},{7,9},{8,10},{9,11},{10,... | collective-permute-start | bytes 1572872 | tf_op jit(solution)/shard_map/ppermute | solution.py:160
  75.0 22.3 %collective-permute-start.1 = (bf16[2,256,512]{2,1,0:T(8,128)(2,1)}, bf16[2,256,512]{2,1,0:T(8,128)(2,1)}, u32[]{:S(2)}, u32[]{:S(2)}) collective-permute-start(bf16[2,256,512]{2,1,0:T(8,128)(2,1)} %get-tuple-element.9.kv_0), channel_id=1, source_target_pairs={{0,1},{1,2},{2,3},{3,4},{4,5},{5,6},{6,7},{7,8},{8,9},{9,10},{10,1... | collective-permute-start | bytes 1572872 | tf_op jit(solution)/shard_map/ppermute | solution.py:160
  78.2 41.3 %collective-permute-start.2 = (bf16[2,256,512]{2,1,0:T(8,128)(2,1)}, bf16[2,256,512]{2,1,0:T(8,128)(2,1)}, u32[]{:S(2)}, u32[]{:S(2)}) collective-permute-start(bf16[2,256,512]{2,1,0:T(8,128)(2,1)} %get-tuple-element.9.kv_0), channel_id=1, source_target_pairs={{1,0},{2,1},{3,2},{4,3},{5,4},{6,5},{7,6},{8,7},{9,8},{10,9},{11,1... | collective-permute-start | bytes 1572872 | tf_op jit(solution)/shard_map/ppermute | solution.py:160
  79.5 40.0 %collective-permute-start.3 = (bf16[2,256,512]{2,1,0:T(8,128)(2,1)}, bf16[2,256,512]{2,1,0:T(8,128)(2,1)}, u32[]{:S(2)}, u32[]{:S(2)}) collective-permute-start(bf16[2,256,512]{2,1,0:T(8,128)(2,1)} %get-tuple-element.9.kv_0), channel_id=1, source_target_pairs={{2,0},{3,1},{4,2},{5,3},{6,4},{7,5},{8,6},{9,7},{10,8},{11,9},{12,... | collective-permute-start | bytes 1572872 | tf_op jit(solution)/shard_map/ppermute | solution.py:160
  84.1 37.1 %all-to-all-start.2 = ((bf16[32,16,128]{2,1,0:T(8,128)(2,1)}), bf16[32,16,128]{2,1,0:T(8,128)(2,1)S(1)}, u32[]{:S(2)}, u32[]{:S(2)}) async-start(bf16[32,16,128]{2,1,0:T(8,128)(2,1)} %broadcast_in_dim.5), calls=%async_computation.2 | async-start | bytes 262144 | tf_op jit(solution)/shard_map/all_to_all | solution.py:169
  121.3 1.0 copy-start.2
  122.3 1.0 copy-start.4
  123.4 1.0 copy-start.5
  124.4 1.0 copy-start.6
  125.4 0.9 copy-start.8

commit v2 on v1

v2 whole, which is shorter than its diff:
```python
import functools
import math

import jax
import jax.numpy as jnp
from jax import lax
from jax.experimental import pallas as pl
from jax.experimental.pallas import tpu as pltpu
from jax.sharding import Mesh
from jax.sharding import PartitionSpec as P

HEADS = 8
BLOCK = 128
VIRTUAL = 64
REACH = 2
TMAX = 6
LANES = 128
LOG2E = 1.4426950408889634
AXES = ("x", "c", "z", "y")
DOM = ("z", "y")
PLANE = ("x", "c", "y")
VMEM = pltpu.VMEM
F32 = jnp.float32
BF16 = jnp.bfloat16


def pool_kernel(
    virtual_of_in, keys_in, values_in, up_in, down_in, sums, key_value, weights, virtual_of, sem
):
    copies = [
        pltpu.make_async_copy(source, target, sem.at[i])
        for i, (source, target) in enumerate(
            (
                (virtual_of_in, virtual_of),
                (keys_in, key_value.at[0]),
                (values_in, key_value.at[1]),
                (up_in, weights.at[0]),
                (down_in, weights.at[1]),
            )
        )
    ]
    for copy in copies:
        copy.start()
    for copy in copies[:3]:
        copy.wait()
    node_rows, feat_width = key_value.shape[1:]
    ids = lax.broadcasted_iota(jnp.int32, (VIRTUAL, node_rows), 0)
    members = jnp.where(virtual_of[...] == ids, 1.0, 0.0).astype(BF16)
    per_part = sums.shape[1]
    lane_parts = feat_width // LANES
    rows_parts = VIRTUAL // per_part
    for which in range(2):
        pooled = jnp.dot(members, key_value[which], preferred_element_type=F32)
        for row in range(rows_parts):
            for lane in range(lane_parts):
                sums[(which * rows_parts + row) * lane_parts + lane] = pooled[
                    row * per_part : (row + 1) * per_part, lane * LANES : (lane + 1) * LANES
                ]
    for copy in copies[3:]:
        copy.wait()


def plane_sum_kernel(parts, total):
    total[...] = jnp.broadcast_to(jnp.sum(parts[...], axis=0, keepdims=True), total.shape)


def pooled_kernel(scale, parts, after, pooled):
    mean = (jnp.sum(parts[...], axis=0, keepdims=True) * scale).astype(BF16)
    pooled[...] = jnp.broadcast_to(mean, pooled.shape)


def stack_kernel(after, w_0, w_1, w_2, w_3, stacked):
    for i, piece in enumerate((w_0, w_1, w_2, w_3)):
        stacked[i] = piece[...]


def head_pair(queries, block, lanes, low):
    pair = queries[block * BLOCK : (block + 1) * BLOCK, lanes]
    zero = jnp.zeros_like(pair)
    return jnp.concatenate([jnp.where(low, pair, zero), jnp.where(low, zero, pair)], axis=0)


def attend(both, keys, values, ones, bias, scale, low):
    scores = lax.dot_general(both, keys, (((1,), (1,)), ((), ())), preferred_element_type=F32)
    scores = scores * scale
    if bias is not None:
        scores = scores + bias
    row_max = jnp.max(scores, axis=-1, keepdims=True)
    exponent = jnp.exp2(scores - row_max).astype(BF16)
    right = jnp.concatenate([values, ones], axis=1)
    summed = jnp.dot(exponent, right, preferred_element_type=F32)
    top, bottom = summed[:BLOCK], summed[BLOCK:]
    numerator = jnp.where(low, top[:, :LANES], bottom[:, :LANES])
    denominator = jnp.where(low, top[:, LANES:], bottom[:, LANES:])
    return numerator, denominator, jnp.where(low, row_max[:BLOCK], row_max[BLOCK:])


def named(tile_lists, block, place, first_block):
    wanted = first_block + place
    found = tile_lists[block, 0] == wanted
    for slot in range(1, TMAX):
        found = jnp.logical_or(found, tile_lists[block, slot] == wanted)
    return jnp.logical_and(found, wanted >= 0)


def near_kernel(
    tile_lists,
    after,
    queries_in,
    keys,
    values,
    kv_m1,
    kv_p1,
    numerators,
    denominators,
    maxima,
    queries,
    window,
    sem,
):
    rows, feat_width = queries.shape
    head_dim = feat_width // HEADS
    copies = [
        pltpu.make_async_copy(queries_in, queries, sem.at[0]),
        pltpu.make_async_copy(keys, window.at[0, pl.ds(rows, rows)], sem.at[1]),
        pltpu.make_async_copy(values, window.at[1, pl.ds(rows, rows)], sem.at[2]),
        pltpu.make_async_copy(kv_m1, window.at[:, pl.ds(0, rows)], sem.at[3]),
        pltpu.make_async_copy(kv_p1, window.at[:, pl.ds(2 * rows, rows)], sem.at[4]),
    ]
    for copy in copies:
        copy.start()
    for copy in copies:
        copy.wait()
    blocks = rows // BLOCK
    first_block = tile_lists[0, 0] - blocks
    scale = LOG2E / math.sqrt(head_dim)
    low = lax.broadcasted_iota(jnp.int32, (BLOCK, LANES), 1) < head_dim
    for block in range(blocks):
        own = tile_lists[block, 0] - first_block
        starts = []
        shown = []
        for place in range(3 * blocks):
            there = named(tile_lists, block, place, first_block)
            starts.append(pl.multiple_of(jnp.where(there, place, own) * BLOCK, BLOCK))
            shown.append(jnp.full((BLOCK, LANES), jnp.where(there, 1.0, 0.0), F32).astype(BF16))
        for part in range(feat_width // LANES):
            lanes = slice(part * LANES, (part + 1) * LANES)
            keys_here = [window[0, pl.ds(s, BLOCK), lanes] for s in starts]
            values_here = [window[1, pl.ds(s, BLOCK), lanes] * o for s, o in zip(starts, shown)]
            numerator, denominator, row_max = attend(
                head_pair(queries, block, lanes, low),
                jnp.concatenate(keys_here, axis=0),
                jnp.concatenate(values_here, axis=0),
                jnp.concatenate(shown, axis=0),
                None,
                scale,
                low,
            )
            here = slice(block * BLOCK, (block + 1) * BLOCK)
            numerators[here, lanes] = numerator
            denominators[here, lanes] = denominator
            maxima[here, lanes] = row_max


def layer_kernel(
    tile_lists,
    virtual_kv,
    numerators_in,
    denominators_in,
    maxima_in,
    queries_in,
    node_feats_in,
    out_weight_in,
    norm_gain_in,
    kv_m2,
    kv_p2,
    w_near_in,
    partial_out,
    normed_out,
    window,
    numerators,
    denominators,
    maxima,
    queries,
    node_feats,
    out_weight,
    norm_gain,
    w_near,
    attended,
    sem,
):
    rows, feat_width = queries.shape
    copies = [
        pltpu.make_async_copy(source, target, sem.at[i])
        for i, (source, target) in enumerate(
            (
                (queries_in, queries),
                (kv_m2, window.at[:, pl.ds(0, rows)]),
                (kv_p2, window.at[:, pl.ds(rows, rows)]),
                (numerators_in, numerators),
                (denominators_in, denominators),
                (maxima_in, maxima),
                (out_weight_in, out_weight),
                (node_feats_in, node_feats),
                (norm_gain_in, norm_gain),
                (w_near_in, w_near),
            )
        )
    ]
    for copy in copies:
        copy.start()
    for copy in copies[:6]:
        copy.wait()
    head_dim = feat_width // HEADS
    scale = LOG2E / math.sqrt(head_dim)
    lane_parts = feat_width // LANES
    rows_parts = VIRTUAL // virtual_kv.shape[1]
    blocks = rows // BLOCK
    far_blocks = 2 * blocks
    low = lax.broadcasted_iota(jnp.int32, (BLOCK, LANES), 1) < head_dim
    ones = jnp.ones((far_blocks * BLOCK + VIRTUAL, LANES), BF16)
    first_block = tile_lists[0, 0] - 2 * blocks
    for block in range(blocks):
        here = slice(block * BLOCK, (block + 1) * BLOCK)
        bias = [
            jnp.full(
                (1, BLOCK),
                jnp.where(
                    named(tile_lists, block, place + (3 * blocks if place >= blocks else 0), first_block),
                    0.0,
                    -jnp.inf,
                ),
                F32,
            )
            for place in range(far_blocks)
        ]
        bias = jnp.concatenate(bias + [jnp.zeros((1, VIRTUAL), F32)], axis=1)
        for part in range(lane_parts):
            lanes = slice(part * LANES, (part + 1) * LANES)
            pooled = [virtual_kv[r * lane_parts + part] for r in range(2 * rows_parts)]
            numerator, denominator, row_max = attend(
                head_pair(queries, block, lanes, low),
                jnp.concatenate([window[0, :, lanes]] + pooled[:rows_parts], axis=0),
                jnp.concatenate([window[1, :, lanes]] + pooled[rows_parts:], axis=0),
                ones,
                bias,
                scale,
                low,
            )
            near_max = maxima[here, lanes]
            top = jnp.maximum(near_max, row_max)
            keep = jnp.exp2(near_max - top)
            add = jnp.exp2(row_max - top)
            attended[here, lanes] = (
                (numerators[here, lanes] * keep + numerator * add)
                / (denominators[here, lanes] * keep + denominator * add)
            ).astype(BF16)

    for copy in copies[6:9]:
        copy.wait()
    residual = node_feats[...].astype(F32) + jnp.dot(
        attended[...], out_weight[...], preferred_element_type=F32
    )
    row_mean = jnp.mean(residual, axis=-1, keepdims=True)
    centered = residual - row_mean
    variance = jnp.mean(centered * centered, axis=-1, keepdims=True)
    normed = (centered * lax.rsqrt(variance + 1e-05) * norm_gain[...]).astype(BF16)
    normed_out[...] = normed
    copies[9].wait()
    partial_out[...] = residual + hidden_sum(normed, w_near)


def hidden_sum(normed, weights):
    total = 0.0
    for shard in range(weights.shape[0]):
        hidden = jnp.dot(normed, weights[shard, 0], preferred_element_type=F32)
        hidden = jnp.maximum(hidden, 0.0).astype(BF16)
        total = total + lax.dot_general(
            hidden, weights[shard, 1], (((1,), (1,)), ((), ())), preferred_element_type=F32
        )
    return total


def finish_kernel(partial, normed, weights, layer_out):
    layer_out[...] = (partial[...] + hidden_sum(normed[...], weights)).astype(BF16)


def along_dom(shard, by):
    length = lax.axis_size(DOM)
    pairs = [(i, i + by) for i in range(length) if 0 <= i + by < length]
    return lax.ppermute(shard, DOM, pairs)


def around(shard, axis, by):
    length = lax.axis_size(axis)
    return lax.ppermute(shard, axis, [(i, (i + by) % length) for i in range(length)])


def exchanged(parts, axes):
    return lax.all_to_all(parts, axes, 0, 0, tiled=True)


def local(
    node_feats,
    queries,
    keys,
    values,
    out_weight,
    up_weight,
    down_weight,
    norm_gain,
    tile_lists,
    virtual_of,
):
    node_rows, feat_width = queries.shape
    plane = lax.axis_size(PLANE)
    depth = lax.axis_size("z")
    near = lax.axis_size("x")
    per_part = 2 * VIRTUAL * feat_width // LANES // plane
    own_hidden = up_weight.shape[1]
    in_vmem = pl.BlockSpec(memory_space=VMEM)
    in_smem = pl.BlockSpec(memory_space=pltpu.SMEM)
    anywhere = pl.BlockSpec(memory_space=pl.ANY)
    shape = jax.ShapeDtypeStruct

    def grant(mib):
        return pltpu.CompilerParams(vmem_limit_bytes=mib * 1024 * 1024)

    def hbm(array):
        return pltpu.with_memory_space_constraint(array, pltpu.HBM)

    def dma(count):
        return pltpu.SemaphoreType.DMA((count,))

    kv_shape = (2, node_rows, feat_width)
    w_shape = (2, feat_width, own_hidden)
    sums, key_value, w_0 = pl.pallas_call(
        pool_kernel,
        out_shape=(
            shape((plane, per_part, LANES), F32),
            pltpu.HBM(kv_shape, BF16),
            pltpu.HBM(w_shape, BF16),
        ),
        in_specs=[anywhere] * 5,
        out_specs=(in_vmem,) * 3,
        scratch_shapes=[VMEM((1, node_rows), jnp.int32), dma(5)],
        compiler_params=grant(6),
        name="pool",
    )(
        hbm(virtual_of.reshape(1, node_rows)),
        hbm(keys),
        hbm(values),
        hbm(up_weight),
        hbm(down_weight),
    )
    parts = exchanged(sums, PLANE)
    kv_m1 = along_dom(key_value, 1)
    kv_p1 = along_dom(key_value, -1)
    w_1 = around(w_0, "x", 1)
    w_2 = around(w_0, "x", -1)
    w_3 = around(w_0, "x", 2)

    plane_sum = pl.pallas_call(
        plane_sum_kernel,
        out_shape=shape((depth, per_part, LANES), F32),
        in_specs=[in_vmem],
        out_specs=in_vmem,
        compiler_params=grant(2),
        name="plane_sum",
    )(parts)

    parts = exchanged(plane_sum, "z")
    kv_m2 = along_dom(kv_m1, 1)
    kv_p2 = along_dom(kv_p1, -1)
    wide = pltpu.HBM((node_rows, feat_width), F32)
    nears = pl.pallas_call(
        near_kernel,
        out_shape=(wide, wide, wide),
        in_specs=[in_smem] + [anywhere] * 6,
        out_specs=(in_vmem,) * 3,
        scratch_shapes=[
            VMEM((node_rows, feat_width), BF16),
            VMEM((2, 3 * node_rows, feat_width), BF16),
            dma(5),
        ],
        compiler_params=grant(12),
        cost_estimate=pl.CostEstimate(
            flops=4_000_000_000, bytes_accessed=6_000_000, transcendentals=2_000_000
        ),
        name="near",
    )(tile_lists, plane_sum, hbm(queries), hbm(keys), hbm(values), kv_m1, kv_p1)

    pool_scale = math.sqrt(VIRTUAL / (node_rows * lax.axis_size(AXES)))
    pooled = pl.pallas_call(
        functools.partial(pooled_kernel, pool_scale),
        out_shape=shape((plane, per_part, LANES), BF16),
        in_specs=[in_vmem, anywhere],
        out_specs=in_vmem,
        compiler_params=grant(2),
        name="pooled",
    )(parts, hbm(nears[2]))

    virtual_kv = exchanged(pooled, PLANE)
    w_near = pl.pallas_call(
        stack_kernel,
        out_shape=pltpu.HBM((near, *w_shape), BF16),
        in_specs=[anywhere] + [in_vmem] * near,
        out_specs=in_vmem,
        compiler_params=grant(6),
        name="stack",
    )(pooled, hbm(w_0), w_1, w_2, w_3)
    w_far = around(w_near, "c", 1)

    partial, normed = pl.pallas_call(
        layer_kernel,
        out_shape=(wide, shape((node_rows, feat_width), BF16)),
        in_specs=[in_smem, in_vmem] + [anywhere] * 10,
        out_specs=(in_vmem,) * 2,
        scratch_shapes=[
            VMEM((2, 2 * node_rows, feat_width), BF16),
            VMEM((node_rows, feat_width), F32),
            VMEM((node_rows, feat_width), F32),
            VMEM((node_rows, feat_width), F32),
            VMEM((node_rows, feat_width), BF16),
            VMEM((node_rows, feat_width), BF16),
            VMEM(out_weight.shape, BF16),
            VMEM((1, feat_width), F32),
            VMEM((near, *w_shape), BF16),
            VMEM((node_rows, feat_width), BF16),
            dma(10),
        ],
        compiler_params=grant(20),
        cost_estimate=pl.CostEstimate(
            flops=400_000_000_000, bytes_accessed=6_000_000, transcendentals=2_000_000
        ),
        name="layer",
    )(
        tile_lists,
        virtual_kv,
        *[hbm(part) for part in nears],
        hbm(queries),
        hbm(node_feats),
        hbm(out_weight),
        hbm(norm_gain.reshape(1, feat_width)),
        kv_m2,
        kv_p2,
        hbm(w_near),
    )
    return pl.pallas_call(
        finish_kernel,
        out_shape=shape((node_rows, feat_width), BF16),
        in_specs=[in_vmem] * 3,
        out_specs=in_vmem,
        compiler_params=grant(10),
        name="finish",
    )(hbm(partial), normed, w_far)


def solution(mesh):
    group, dom = mesh.devices.shape
    fine = Mesh(mesh.devices.reshape(group // 2, 2, dom // 4, 4), AXES)
    placed = (
        P(AXES, None),
        P(AXES, None),
        P(AXES, None),
        P(AXES, None),
        P(),
        P(None, ("x", "c")),
        P(None, ("x", "c")),
        P(),
        P(AXES, None),
        P(AXES),
    )
    return jax.shard_map(
        local, mesh=fine, in_specs=placed, out_specs=P(AXES, None), check_vma=False
    )
```

time: 136 us -> 93.3 us (0.69)
  waiting for transfers between devices: 50.2 us -> 2.91 us
  Pallas kernels: 10.8 us -> 22.4 us
  local copies, waits for them, and re-layouts: 6.48 us -> 0.01 us
  other arithmetic: 3.86 us -> 0 us
  blocking collectives: 15.9 us -> 19 us
    ppermute x4, waiting for transfers between devices: 28.1 us -> 0.01 us  [along_dom(): return lax.ppermute(shard, DOM, pairs)]
    ppermute x4, waiting for transfers between devices: 17.8 us -> 0.01 us  [around(): lax.ppermute(shard, axis, [(i, (i + by) % length) for i in range(length)])]
    pallas_call x2 -> x7, Pallas kernels: 10.8 us -> 22.4 us  [the longest x1 7.32 us: local(): pl.pallas_call(layer_kernel, out_shape=(wide, shape((node_rows, feat_widt...]
    unnamed x24 -> x2, local copies, waits for them, and re-layouts: 5.14 us -> 0.01 us
    ppermute x4, starting transfers between devices: 15.9 us -> 12.1 us  [around(): lax.ppermute(shard, axis, [(i, (i + by) % length) for i in range(length)])]
    all_to_all x1, blocking collectives: 15.9 us -> 19 us  [exchanged(): return lax.all_to_all(parts, axes, 0, 0, tiled=True)]
    another operation x1 -> x0, other arithmetic: 2.85 us -> none  [local(): w_far = around(jnp.stack([w_0, w_1, w_2, w_3]), 'c', 1)]
    ppermute x4, starting transfers between devices: 9.4 us -> 12.1 us  [along_dom(): return lax.ppermute(shard, DOM, pairs)]
  transfers between devices with their start and end apart: 10 -> 10, of which waited for: 7 -> 1; matrix products, arithmetic and copies ran while one was open for 2% -> 0% of each run, Pallas kernels for 0% -> 18%
where the time goes in v2:
time: 93.3 us; the launch traced here: 92.7 us
  starting transfers between devices  48.3 us (52%)
  Pallas kernels  22.4 us (24%)
  blocking collectives  19 us (20%)
  waiting for transfers between devices  2.91 us (3%)
    all_to_all x2, starting transfers between devices, exchanged(): return lax.all_to_all(parts, axes, 0, 0, tiled=True)  24.2 us
    all_to_all x1, blocking collectives, exchanged(): return lax.all_to_all(parts, axes, 0, 0, tiled=True)  19 us
    ppermute x4, starting transfers between devices, along_dom(): return lax.ppermute(shard, DOM, pairs)  12.1 us
    ppermute x4, starting transfers between devices, around(): lax.ppermute(shard, axis, [(i, (i + by) % length) for i in range(length)])  12.1 us
    pallas_call x1, Pallas kernels, local(): pl.pallas_call(layer_kernel, out_shape=(wide, shape((node_rows, feat_widt...  7.32 us
    pallas_call x1, Pallas kernels, local(): pl.pallas_call(near_kernel, out_shape=(wide, wide, wide), in_specs=[in_sm...  5.29 us
    pallas_call x1, Pallas kernels, local(): pl.pallas_call(finish_kernel, out_shape=shape((node_rows, feat_width), BF...  3.55 us
    all_to_all x2, waiting for transfers between devices, exchanged(): return lax.all_to_all(parts, axes, 0, 0, tiled=True)  2.89 us
  transfers between devices with their start and end apart: 10, of which 1 were waited for; matrix products, arithmetic and copies ran while one was open for 0% of the time, Pallas kernels for 18%

profile of v2, /device:TPU:1, one launch (start us, length us, event | category | flops | bytes accessed | tf_op | source)
XLA Modules:
  0.0 92.7 jit_solution(16275793085781456051)
XLA Ops:
  0.0 0.0 copy-start
  0.0 2.3 %pool.1 = (f32[32,16,128]{2,1,0:T(8,128)S(1)}, bf16[2,256,512]{2,1,0:T(8,128)(2,1)}, bf16[2,512,256]{2,1,0:T(8,128)(2,1)}) custom-call(s32[1,256]{1,0:T(1,128)} %bitcast.2, bf16[256,512]{1,0:T(8,128)(2,1)} %keys.1, bf16[256,512]{1,0:T(8,128)(2,1)} %values.1, bf16[512,256]{1,0:T(8,128)(2,1)} %up_in.1, bf16[512,256]{1,0:T(8,128)(2,1)} %down_in.1), custom_call_target="tpu_custom_call" | custom-call | tf_op jit(solution)/shard_map/pool/pallas_call | solution.py:337
  2.3 1.3 %collective-permute-start.1 = (bf16[2,256,512]{2,1,0:T(8,128)(2,1)}, bf16[2,256,512]{2,1,0:T(8,128)(2,1)S(1)}, u32[]{:S(2)}, u32[]{:S(2)}) collective-permute-start(bf16[2,256,512]{2,1,0:T(8,128)(2,1)} %get-tuple-element.14), channel_id=1, source_target_pairs={{1,0},{2,1},{3,2},{4,3},{5,4},{6,5},{7,6},{8,7},{9,8},{10,9},{11,1... | collective-permute-start | bytes 1572872 | tf_op jit(solution)/shard_map/ppermute | solution.py:291
  3.6 4.7 %collective-permute-start = (bf16[2,256,512]{2,1,0:T(8,128)(2,1)}, bf16[2,256,512]{2,1,0:T(8,128)(2,1)S(1)}, u32[]{:S(2)}, u32[]{:S(2)}) collective-permute-start(bf16[2,256,512]{2,1,0:T(8,128)(2,1)} %get-tuple-element.14), channel_id=1, source_target_pairs={{0,1},{1,2},{2,3},{3,4},{4,5},{5,6},{6,7},{7,8},{8,9},{9,10},{10,1... | collective-permute-start | bytes 1572872 | tf_op jit(solution)/shard_map/ppermute | solution.py:291
  8.3 19.0 %all_to_all.15.parts = f32[32,16,128]{2,1,0:T(8,128)S(1)} all-to-all(f32[32,16,128]{2,1,0:T(8,128)S(1)} %get-tuple-element.13), channel_id=1, replica_groups=mesh['x'=4,'c'=2,'z'=16,'y'=4] {'x','c','y'}, dimensions={0} | all-to-all | bytes 524288 | tf_op jit(solution)/shard_map/all_to_all | solution.py:300
  27.3 0.7 plane_sum.1.after
  28.0 17.1 %all-to-all-start.1 = ((f32[16,16,128]{2,1,0:T(8,128)}), f32[16,16,128]{2,1,0:T(8,128)S(1)}, u32[]{:S(2)}, u32[]{:S(2)}) async-start(f32[16,16,128]{2,1,0:T(8,128)} %plane_sum.1.after), calls=%async_computation.1 | async-start | bytes 262144 | tf_op jit(solution)/shard_map/all_to_all | solution.py:300
  45.1 4.7 %collective-permute-start.6 = (bf16[2,512,256]{2,1,0:T(8,128)(2,1)}, bf16[2,512,256]{2,1,0:T(8,128)(2,1)S(1)}, u32[]{:S(2)}, u32[]{:S(2)}) collective-permute-start(bf16[2,512,256]{2,1,0:T(8,128)(2,1)} %get-tuple-element.18.w_0), channel_id=1, source_target_pairs={{0,256},{128,384},{256,0},{384,128},{1,257},{129,385},{257,1},{385... | collective-permute-start | bytes 1572872 | tf_op jit(solution)/shard_map/ppermute | solution.py:296
  49.7 2.8 %collective-permute-start.5 = (bf16[2,512,256]{2,1,0:T(8,128)(2,1)}, bf16[2,512,256]{2,1,0:T(8,128)(2,1)S(1)}, u32[]{:S(2)}, u32[]{:S(2)}) collective-permute-start(bf16[2,512,256]{2,1,0:T(8,128)(2,1)} %get-tuple-element.18.w_0), channel_id=1, source_target_pairs={{0,384},{128,0},{256,128},{384,256},{1,385},{129,1},{257,129},{385... | collective-permute-start | bytes 1572872 | tf_op jit(solution)/shard_map/ppermute | solution.py:296
  52.5 2.5 %collective-permute-start.4 = (bf16[2,512,256]{2,1,0:T(8,128)(2,1)}, bf16[2,512,256]{2,1,0:T(8,128)(2,1)S(1)}, u32[]{:S(2)}, u32[]{:S(2)}) collective-permute-start(bf16[2,512,256]{2,1,0:T(8,128)(2,1)} %get-tuple-element.18.w_0), channel_id=1, source_target_pairs={{0,128},{128,256},{256,384},{384,0},{1,129},{129,257},{257,385},{3... | collective-permute-start | bytes 1572872 | tf_op jit(solution)/shard_map/ppermute | solution.py:296
  55.0 0.0 collective-permute-done.1.kv_p1
  55.1 1.3 %collective-permute-start.3 = (bf16[2,256,512]{2,1,0:T(8,128)(2,1)S(1)}, bf16[2,256,512]{2,1,0:T(8,128)(2,1)S(1)}, u32[]{:S(2)}, u32[]{:S(2)}) collective-permute-start(bf16[2,256,512]{2,1,0:T(8,128)(2,1)S(1)} %collective-permute-done.1.kv_p1), channel_id=1, source_target_pairs={{1,0},{2,1},{3,2},{4,3},{5,4},{6,5},{7,6},{8,7},{9,8},{10,9},{11,1... | collective-permute-start | bytes 1572872 | tf_op jit(solution)/shard_map/ppermute | solution.py:291
  56.4 0.0 collective-permute-done.kv_m1
  56.4 4.8 %collective-permute-start.2 = (bf16[2,256,512]{2,1,0:T(8,128)(2,1)S(1)}, bf16[2,256,512]{2,1,0:T(8,128)(2,1)}, u32[]{:S(2)}, u32[]{:S(2)}) collective-permute-start(bf16[2,256,512]{2,1,0:T(8,128)(2,1)S(1)} %collective-permute-done.kv_m1), channel_id=1, source_target_pairs={{0,1},{1,2},{2,3},{3,4},{4,5},{5,6},{6,7},{7,8},{8,9},{9,10},{10,1... | collective-permute-start | bytes 1572872 | tf_op jit(solution)/shard_map/ppermute | solution.py:291
  61.2 0.0 copy-done
  61.2 5.3 %near.1 = (f32[256,512]{1,0:T(8,128)}, f32[256,512]{1,0:T(8,128)}, f32[256,512]{1,0:T(8,128)}) custom-call(s32[2,6]{1,0:T(2,128)S(1)} %copy-done, f32[16,16,128]{2,1,0:T(8,128)} %plane_sum.1.after, bf16[256,512]{1,0:T(8,128)(2,1)} %queries_in.3, bf16[256,512]{1,0:T(8,128)(2,1)} %keys.1, bf16[256,512]{1,0:T(8,128)(2,1)} %values.1, ...), custom_call_target="tpu_custom_call" | custom-call | flops 4000000000 | bytes 6000000 | tf_op jit(solution)/shard_map/near/pallas_call | solution.py:376
  66.5 0.0 all-to-all-done.1.parts
  66.5 0.7 pooled.1.after
  67.2 7.1 %all-to-all-start.2 = ((bf16[32,16,128]{2,1,0:T(8,128)(2,1)}), bf16[32,16,128]{2,1,0:T(8,128)(2,1)S(1)}, u32[]{:S(2)}, u32[]{:S(2)}) async-start(bf16[32,16,128]{2,1,0:T(8,128)(2,1)} %pooled.1.after), calls=%async_computation.2 | async-start | bytes 262144 | tf_op jit(solution)/shard_map/all_to_all | solution.py:300
  74.2 0.0 collective-permute-done.6.w_3
  74.3 0.0 collective-permute-done.5.w_2
  74.3 0.0 collective-permute-done.4.w_1
  74.3 2.5 %stack.1.w_near_in = bf16[4,2,512,256]{3,2,1,0:T(8,128)(2,1)} custom-call(bf16[32,16,128]{2,1,0:T(8,128)(2,1)} %pooled.1.after, bf16[2,512,256]{2,1,0:T(8,128)(2,1)} %get-tuple-element.18.w_0, bf16[2,512,256]{2,1,0:T(8,128)(2,1)S(1)} %collective-permute-done.4.w_1, bf16[2,512,256]{2,1,0:T(8,128)(2,1)S(1)} %collective-permute-done.5.w_2, ...), custom_call_target="tpu_custom_call" | custom-call | tf_op jit(solution)/shard_map/stack/pallas_call | solution.py:404
  76.8 2.1 %collective-permute-start.7 = (bf16[4,2,512,256]{3,2,1,0:T(8,128)(2,1)}, bf16[4,2,512,256]{3,2,1,0:T(8,128)(2,1)}, u32[]{:S(2)}, u32[]{:S(2)}) collective-permute-start(bf16[4,2,512,256]{3,2,1,0:T(8,128)(2,1)} %stack.1.w_near_in), channel_id=1, source_target_pairs={{0,64},{64,0},{1,65},{65,1},{2,66},{66,2},{3,67},{67,3},{4,68},{68... | collective-permute-start | bytes 6291464 | tf_op jit(solution)/shard_map/ppermute | solution.py:296
  78.9 2.9 %all-to-all-done.2.virtual_kv = bf16[32,16,128]{2,1,0:T(8,128)(2,1)S(1)} async-done(((bf16[32,16,128]{2,1,0:T(8,128)(2,1)}), bf16[32,16,128]{2,1,0:T(8,128)(2,1)S(1)}, u32[]{:S(2)}, u32[]{:S(2)}) %all-to-all-start.2) | async-done | bytes 131104 | tf_op jit(solution)/shard_map/all_to_all | solution.py:300
  81.8 0.0 collective-permute-done.3.kv_p2
  81.8 0.0 collective-permute-done.2.kv_m2
  81.8 7.3 %layer.1 = (f32[256,512]{1,0:T(8,128)}, bf16[256,512]{1,0:T(8,128)(2,1)S(1)}) custom-call(s32[2,6]{1,0:T(2,128)S(1)} %copy-done, bf16[32,16,128]{2,1,0:T(8,128)(2,1)S(1)} %all-to-all-done.2.virtual_kv, f32[256,512]{1,0:T(8,128)} %get-tuple-element.16.numerators_in, f32[256,512]{1,0:T(8,128)} %get-tuple-element.17.denominators_in, ...), custom_call_target="tpu_custom_call" | custom-call | flops 399999991808 | bytes 6000000 | tf_op jit(solution)/shard_map/layer/pallas_call | solution.py:414
  89.2 0.0 collective-permute-done.7.weights
  89.2 3.6 %finish.1 = bf16[256,512]{1,0:T(8,128)(2,1)} custom-call(f32[256,512]{1,0:T(8,128)} %get-tuple-element.19.partial, bf16[256,512]{1,0:T(8,128)(2,1)S(1)} %get-tuple-element.20.normed, bf16[4,2,512,256]{3,2,1,0:T(8,128)(2,1)} %collective-permute-done.7.weights), custom_call_target="tpu_custom_call" | custom-call | tf_op jit(solution)/shard_map/finish/pallas_call | solution.py:449
Async XLA Ops:
  0.0 61.2 %copy-start = (s32[2,6]{1,0:T(2,128)S(1)}, s32[2,6]{1,0:T(2,128)}, u32[]{:S(2)}) copy-start(s32[2,6]{1,0:T(2,128)} %tile_lists.3) | copy-start | bytes 148
  2.3 52.7 %collective-permute-start.1 = (bf16[2,256,512]{2,1,0:T(8,128)(2,1)}, bf16[2,256,512]{2,1,0:T(8,128)(2,1)S(1)}, u32[]{:S(2)}, u32[]{:S(2)}) collective-permute-start(bf16[2,256,512]{2,1,0:T(8,128)(2,1)} %get-tuple-element.14), channel_id=1, source_target_pairs={{1,0},{2,1},{3,2},{4,3},{5,4},{6,5},{7,6},{8,7},{9,8},{10,9},{11,1... | collective-permute-start | bytes 1572872 | tf_op jit(solution)/shard_map/ppermute | solution.py:291
  3.6 52.7 %collective-permute-start = (bf16[2,256,512]{2,1,0:T(8,128)(2,1)}, bf16[2,256,512]{2,1,0:T(8,128)(2,1)S(1)}, u32[]{:S(2)}, u32[]{:S(2)}) collective-permute-start(bf16[2,256,512]{2,1,0:T(8,128)(2,1)} %get-tuple-element.14), channel_id=1, source_target_pairs={{0,1},{1,2},{2,3},{3,4},{4,5},{5,6},{6,7},{7,8},{8,9},{9,10},{10,1... | collective-permute-start | bytes 1572872 | tf_op jit(solution)/shard_map/ppermute | solution.py:291
  28.0 38.5 %all-to-all-start.1 = ((f32[16,16,128]{2,1,0:T(8,128)}), f32[16,16,128]{2,1,0:T(8,128)S(1)}, u32[]{:S(2)}, u32[]{:S(2)}) async-start(f32[16,16,128]{2,1,0:T(8,128)} %plane_sum.1.after), calls=%async_computation.1 | async-start | bytes 262144 | tf_op jit(solution)/shard_map/all_to_all | solution.py:300
  45.1 29.2 %collective-permute-start.6 = (bf16[2,512,256]{2,1,0:T(8,128)(2,1)}, bf16[2,512,256]{2,1,0:T(8,128)(2,1)S(1)}, u32[]{:S(2)}, u32[]{:S(2)}) collective-permute-start(bf16[2,512,256]{2,1,0:T(8,128)(2,1)} %get-tuple-element.18.w_0), channel_id=1, source_target_pairs={{0,256},{128,384},{256,0},{384,128},{1,257},{129,385},{257,1},{385... | collective-permute-start | bytes 1572872 | tf_op jit(solution)/shard_map/ppermute | solution.py:296
  49.7 24.5 %collective-permute-start.5 = (bf16[2,512,256]{2,1,0:T(8,128)(2,1)}, bf16[2,512,256]{2,1,0:T(8,128)(2,1)S(1)}, u32[]{:S(2)}, u32[]{:S(2)}) collective-permute-start(bf16[2,512,256]{2,1,0:T(8,128)(2,1)} %get-tuple-element.18.w_0), channel_id=1, source_target_pairs={{0,384},{128,0},{256,128},{384,256},{1,385},{129,1},{257,129},{385... | collective-permute-start | bytes 1572872 | tf_op jit(solution)/shard_map/ppermute | solution.py:296
  52.5 21.7 %collective-permute-start.4 = (bf16[2,512,256]{2,1,0:T(8,128)(2,1)}, bf16[2,512,256]{2,1,0:T(8,128)(2,1)S(1)}, u32[]{:S(2)}, u32[]{:S(2)}) collective-permute-start(bf16[2,512,256]{2,1,0:T(8,128)(2,1)} %get-tuple-element.18.w_0), channel_id=1, source_target_pairs={{0,128},{128,256},{256,384},{384,0},{1,129},{129,257},{257,385},{3... | collective-permute-start | bytes 1572872 | tf_op jit(solution)/shard_map/ppermute | solution.py:296
  55.1 26.8 %collective-permute-start.3 = (bf16[2,256,512]{2,1,0:T(8,128)(2,1)S(1)}, bf16[2,256,512]{2,1,0:T(8,128)(2,1)S(1)}, u32[]{:S(2)}, u32[]{:S(2)}) collective-permute-start(bf16[2,256,512]{2,1,0:T(8,128)(2,1)S(1)} %collective-permute-done.1.kv_p1), channel_id=1, source_target_pairs={{1,0},{2,1},{3,2},{4,3},{5,4},{6,5},{7,6},{8,7},{9,8},{10,9},{11,1... | collective-permute-start | bytes 1572872 | tf_op jit(solution)/shard_map/ppermute | solution.py:291
  56.4 25.5 %collective-permute-start.2 = (bf16[2,256,512]{2,1,0:T(8,128)(2,1)S(1)}, bf16[2,256,512]{2,1,0:T(8,128)(2,1)}, u32[]{:S(2)}, u32[]{:S(2)}) collective-permute-start(bf16[2,256,512]{2,1,0:T(8,128)(2,1)S(1)} %collective-permute-done.kv_m1), channel_id=1, source_target_pairs={{0,1},{1,2},{2,3},{3,4},{4,5},{5,6},{6,7},{7,8},{8,9},{9,10},{10,1... | collective-permute-start | bytes 1572872 | tf_op jit(solution)/shard_map/ppermute | solution.py:291
  67.2 14.7 %all-to-all-start.2 = ((bf16[32,16,128]{2,1,0:T(8,128)(2,1)}), bf16[32,16,128]{2,1,0:T(8,128)(2,1)S(1)}, u32[]{:S(2)}, u32[]{:S(2)}) async-start(bf16[32,16,128]{2,1,0:T(8,128)(2,1)} %pooled.1.after), calls=%async_computation.2 | async-start | bytes 262144 | tf_op jit(solution)/shard_map/all_to_all | solution.py:300
  76.8 12.4 %collective-permute-start.7 = (bf16[4,2,512,256]{3,2,1,0:T(8,128)(2,1)}, bf16[4,2,512,256]{3,2,1,0:T(8,128)(2,1)}, u32[]{:S(2)}, u32[]{:S(2)}) collective-permute-start(bf16[4,2,512,256]{3,2,1,0:T(8,128)(2,1)} %stack.1.w_near_in), channel_id=1, source_target_pairs={{0,64},{64,0},{1,65},{65,1},{2,66},{66,2},{3,67},{67,3},{4,68},{68... | collective-permute-start | bytes 6291464 | tf_op jit(solution)/shard_map/ppermute | solution.py:296

commit v3 on v2

--- a/solution.py
+++ b/solution.py
@@ -64,7 +64,7 @@
     total[...] = jnp.broadcast_to(jnp.sum(parts[...], axis=0, keepdims=True), total.shape)
 
 
-def pooled_kernel(scale, parts, after, pooled):
+def pooled_kernel(scale, parts, after, after_1, after_2, after_3, pooled):
     mean = (jnp.sum(parts[...], axis=0, keepdims=True) * scale).astype(BF16)
     pooled[...] = jnp.broadcast_to(mean, pooled.shape)
 
@@ -394,11 +394,11 @@
     pooled = pl.pallas_call(
         functools.partial(pooled_kernel, pool_scale),
         out_shape=shape((plane, per_part, LANES), BF16),
-        in_specs=[in_vmem, anywhere],
+        in_specs=[in_vmem] + [anywhere] * 4,
         out_specs=in_vmem,
         compiler_params=grant(2),
         name="pooled",
-    )(parts, hbm(nears[2]))
+    )(parts, hbm(nears[2]), w_1, w_2, w_3)
 
     virtual_kv = exchanged(pooled, PLANE)
     w_near = pl.pallas_call(

time: 93.3 us -> 86.1 us (0.923)
  blocking collectives: 19 us -> 0 us
  starting transfers between devices: 48.3 us -> 59.4 us
    all_to_all x1 -> x0, blocking collectives: 19 us -> none  [exchanged(): return lax.all_to_all(parts, axes, 0, 0, tiled=True)]
    all_to_all x2 -> x3, starting transfers between devices: 24.2 us -> 35.1 us  [exchanged(): return lax.all_to_all(parts, axes, 0, 0, tiled=True)]
    all_to_all x2 -> x3, waiting for transfers between devices: 2.89 us -> 3.47 us  [exchanged(): return lax.all_to_all(parts, axes, 0, 0, tiled=True)]
  transfers between devices with their start and end apart: 10 -> 11, of which waited for: 1 -> 2; matrix products, arithmetic and copies ran while one was open for 0% -> 0% of each run, Pallas kernels for 18% -> 19%
where the time goes in v3:
time: 86.1 us; the launch traced here: 85.5 us
  starting transfers between devices  59.4 us (69%)
  Pallas kernels  22.4 us (26%)
  waiting for transfers between devices  3.49 us (4%)
    all_to_all x3, starting transfers between devices, exchanged(): return lax.all_to_all(parts, axes, 0, 0, tiled=True)  35.1 us
    ppermute x4, starting transfers between devices, around(): lax.ppermute(shard, axis, [(i, (i + by) % length) for i in range(length)])  12.2 us
    ppermute x4, starting transfers between devices, along_dom(): return lax.ppermute(shard, DOM, pairs)  12.1 us
    pallas_call x1, Pallas kernels, local(): pl.pallas_call(layer_kernel, out_shape=(wide, shape((node_rows, feat_widt...  7.32 us
    pallas_call x1, Pallas kernels, local(): pl.pallas_call(near_kernel, out_shape=(wide, wide, wide), in_specs=[in_sm...  5.3 us
    pallas_call x1, Pallas kernels, local(): pl.pallas_call(finish_kernel, out_shape=shape((node_rows, feat_width), BF...  3.55 us
    all_to_all x3, waiting for transfers between devices, exchanged(): return lax.all_to_all(parts, axes, 0, 0, tiled=True)  3.47 us
    pallas_call x1, Pallas kernels, local(): pl.pallas_call(stack_kernel, out_shape=pltpu.HBM((near, *w_shape), BF16),...  2.52 us
  transfers between devices with their start and end apart: 11, of which 2 were waited for; matrix products, arithmetic and copies ran while one was open for 0% of the time, Pallas kernels for 19%

profile of v3, /device:TPU:1, one launch (start us, length us, event | category | flops | bytes accessed | tf_op | source)
XLA Modules:
  0.0 85.5 jit_solution(10957248391711265695)
XLA Ops:
  0.0 0.0 copy-start
  0.0 2.4 %pool.1 = (f32[32,16,128]{2,1,0:T(8,128)}, bf16[2,256,512]{2,1,0:T(8,128)(2,1)}, bf16[2,512,256]{2,1,0:T(8,128)(2,1)}) custom-call(s32[1,256]{1,0:T(1,128)} %bitcast.2, bf16[256,512]{1,0:T(8,128)(2,1)} %keys.1, bf16[256,512]{1,0:T(8,128)(2,1)} %values.1, bf16[512,256]{1,0:T(8,128)(2,1)} %up_in.1, bf16[512,256]{1,0:T(8,128)(2,1)} %down_in.1), custom_call_target="tpu_custom_call" | custom-call | tf_op jit(solution)/shard_map/pool/pallas_call | solution.py:337
  2.4 1.3 %collective-permute-start.1 = (bf16[2,256,512]{2,1,0:T(8,128)(2,1)}, bf16[2,256,512]{2,1,0:T(8,128)(2,1)S(1)}, u32[]{:S(2)}, u32[]{:S(2)}) collective-permute-start(bf16[2,256,512]{2,1,0:T(8,128)(2,1)} %get-tuple-element.14), channel_id=1, source_target_pairs={{1,0},{2,1},{3,2},{4,3},{5,4},{6,5},{7,6},{8,7},{9,8},{10,9},{11,1... | collective-permute-start | bytes 1572872 | tf_op jit(solution)/shard_map/ppermute | solution.py:291
  3.7 4.7 %collective-permute-start = (bf16[2,256,512]{2,1,0:T(8,128)(2,1)}, bf16[2,256,512]{2,1,0:T(8,128)(2,1)S(1)}, u32[]{:S(2)}, u32[]{:S(2)}) collective-permute-start(bf16[2,256,512]{2,1,0:T(8,128)(2,1)} %get-tuple-element.14), channel_id=1, source_target_pairs={{0,1},{1,2},{2,3},{3,4},{4,5},{5,6},{6,7},{7,8},{8,9},{9,10},{10,1... | collective-permute-start | bytes 1572872 | tf_op jit(solution)/shard_map/ppermute | solution.py:291
  8.4 10.4 %all-to-all-start = ((f32[32,16,128]{2,1,0:T(8,128)}), f32[32,16,128]{2,1,0:T(8,128)S(1)}, u32[]{:S(2)}, u32[]{:S(2)}) async-start(f32[32,16,128]{2,1,0:T(8,128)} %get-tuple-element.13), calls=%async_computation | async-start | bytes 524288 | tf_op jit(solution)/shard_map/all_to_all | solution.py:300
  18.8 4.8 %collective-permute-start.4 = (bf16[2,512,256]{2,1,0:T(8,128)(2,1)}, bf16[2,512,256]{2,1,0:T(8,128)(2,1)S(1)}, u32[]{:S(2)}, u32[]{:S(2)}) collective-permute-start(bf16[2,512,256]{2,1,0:T(8,128)(2,1)} %get-tuple-element.16.w_0), channel_id=1, source_target_pairs={{0,256},{128,384},{256,0},{384,128},{1,257},{129,385},{257,1},{385... | collective-permute-start | bytes 1572872 | tf_op jit(solution)/shard_map/ppermute | solution.py:296
  23.6 2.8 %collective-permute-start.3 = (bf16[2,512,256]{2,1,0:T(8,128)(2,1)}, bf16[2,512,256]{2,1,0:T(8,128)(2,1)S(1)}, u32[]{:S(2)}, u32[]{:S(2)}) collective-permute-start(bf16[2,512,256]{2,1,0:T(8,128)(2,1)} %get-tuple-element.16.w_0), channel_id=1, source_target_pairs={{0,384},{128,0},{256,128},{384,256},{1,385},{129,1},{257,129},{385... | collective-permute-start | bytes 1572872 | tf_op jit(solution)/shard_map/ppermute | solution.py:296
  26.4 2.5 %collective-permute-start.2 = (bf16[2,512,256]{2,1,0:T(8,128)(2,1)}, bf16[2,512,256]{2,1,0:T(8,128)(2,1)S(1)}, u32[]{:S(2)}, u32[]{:S(2)}) collective-permute-start(bf16[2,512,256]{2,1,0:T(8,128)(2,1)} %get-tuple-element.16.w_0), channel_id=1, source_target_pairs={{0,128},{128,256},{256,384},{384,0},{1,129},{129,257},{257,385},{3... | collective-permute-start | bytes 1572872 | tf_op jit(solution)/shard_map/ppermute | solution.py:296
  28.9 0.0 all-to-all-done.parts
  28.9 0.7 plane_sum.1.after
  29.6 15.6 %all-to-all-start.1 = ((f32[16,16,128]{2,1,0:T(8,128)}), f32[16,16,128]{2,1,0:T(8,128)S(1)}, u32[]{:S(2)}, u32[]{:S(2)}) async-start(f32[16,16,128]{2,1,0:T(8,128)} %plane_sum.1.after), calls=%async_computation.1 | async-start | bytes 262144 | tf_op jit(solution)/shard_map/all_to_all | solution.py:300
  45.2 0.0 collective-permute-done.1.kv_p1
  45.2 1.3 %collective-permute-start.6 = (bf16[2,256,512]{2,1,0:T(8,128)(2,1)S(1)}, bf16[2,256,512]{2,1,0:T(8,128)(2,1)S(1)}, u32[]{:S(2)}, u32[]{:S(2)}) collective-permute-start(bf16[2,256,512]{2,1,0:T(8,128)(2,1)S(1)} %collective-permute-done.1.kv_p1), channel_id=1, source_target_pairs={{1,0},{2,1},{3,2},{4,3},{5,4},{6,5},{7,6},{8,7},{9,8},{10,9},{11,1... | collective-permute-start | bytes 1572872 | tf_op jit(solution)/shard_map/ppermute | solution.py:291
  46.5 0.0 collective-permute-done.kv_m1
  46.5 4.8 %collective-permute-start.5 = (bf16[2,256,512]{2,1,0:T(8,128)(2,1)S(1)}, bf16[2,256,512]{2,1,0:T(8,128)(2,1)}, u32[]{:S(2)}, u32[]{:S(2)}) collective-permute-start(bf16[2,256,512]{2,1,0:T(8,128)(2,1)S(1)} %collective-permute-done.kv_m1), channel_id=1, source_target_pairs={{0,1},{1,2},{2,3},{3,4},{4,5},{5,6},{6,7},{7,8},{8,9},{9,10},{10,1... | collective-permute-start | bytes 1572872 | tf_op jit(solution)/shard_map/ppermute | solution.py:291
  51.3 0.0 copy-done
  51.4 5.3 %near.1 = (f32[256,512]{1,0:T(8,128)}, f32[256,512]{1,0:T(8,128)}, f32[256,512]{1,0:T(8,128)}) custom-call(s32[2,6]{1,0:T(2,128)S(1)} %copy-done, f32[16,16,128]{2,1,0:T(8,128)} %plane_sum.1.after, bf16[256,512]{1,0:T(8,128)(2,1)} %queries_in.3, bf16[256,512]{1,0:T(8,128)(2,1)} %keys.1, bf16[256,512]{1,0:T(8,128)(2,1)} %values.1, ...), custom_call_target="tpu_custom_call" | custom-call | flops 4000000000 | bytes 6000000 | tf_op jit(solution)/shard_map/near/pallas_call | solution.py:376
  56.7 0.0 collective-permute-done.4.after_3.w_3
  56.7 0.0 collective-permute-done.3.after_2.w_2
  56.7 0.0 collective-permute-done.2.after_1.w_1
  56.7 0.6 all-to-all-done.1.parts
  57.2 0.7 pooled.1.after
  57.9 9.1 %all-to-all-start.2 = ((bf16[32,16,128]{2,1,0:T(8,128)(2,1)}), bf16[32,16,128]{2,1,0:T(8,128)(2,1)S(1)}, u32[]{:S(2)}, u32[]{:S(2)}) async-start(bf16[32,16,128]{2,1,0:T(8,128)(2,1)} %pooled.1.after), calls=%async_computation.2 | async-start | bytes 262144 | tf_op jit(solution)/shard_map/all_to_all | solution.py:300
  67.0 2.5 %stack.1.w_near_in = bf16[4,2,512,256]{3,2,1,0:T(8,128)(2,1)} custom-call(bf16[32,16,128]{2,1,0:T(8,128)(2,1)} %pooled.1.after, bf16[2,512,256]{2,1,0:T(8,128)(2,1)} %get-tuple-element.16.w_0, bf16[2,512,256]{2,1,0:T(8,128)(2,1)S(1)} %collective-permute-done.2.after_1.w_1, bf16[2,512,256]{2,1,0:T(8,128)(2,1)S(1)} %collective-permute-done.3.after_2.w_2, ...), custom_call_target="tpu_custom_call" | custom-call | tf_op jit(solution)/shard_map/stack/pallas_call | solution.py:404
  69.6 2.1 %collective-permute-start.7 = (bf16[4,2,512,256]{3,2,1,0:T(8,128)(2,1)}, bf16[4,2,512,256]{3,2,1,0:T(8,128)(2,1)}, u32[]{:S(2)}, u32[]{:S(2)}) collective-permute-start(bf16[4,2,512,256]{3,2,1,0:T(8,128)(2,1)} %stack.1.w_near_in), channel_id=1, source_target_pairs={{0,64},{64,0},{1,65},{65,1},{2,66},{66,2},{3,67},{67,3},{4,68},{68... | collective-permute-start | bytes 6291464 | tf_op jit(solution)/shard_map/ppermute | solution.py:296
  71.7 2.9 %all-to-all-done.2.virtual_kv = bf16[32,16,128]{2,1,0:T(8,128)(2,1)S(1)} async-done(((bf16[32,16,128]{2,1,0:T(8,128)(2,1)}), bf16[32,16,128]{2,1,0:T(8,128)(2,1)S(1)}, u32[]{:S(2)}, u32[]{:S(2)}) %all-to-all-start.2) | async-done | bytes 131104 | tf_op jit(solution)/shard_map/all_to_all | solution.py:300
  74.6 0.0 collective-permute-done.6.kv_p2
  74.6 0.0 collective-permute-done.5.kv_m2
  74.6 7.3 %layer.1 = (f32[256,512]{1,0:T(8,128)}, bf16[256,512]{1,0:T(8,128)(2,1)S(1)}) custom-call(s32[2,6]{1,0:T(2,128)S(1)} %copy-done, bf16[32,16,128]{2,1,0:T(8,128)(2,1)S(1)} %all-to-all-done.2.virtual_kv, f32[256,512]{1,0:T(8,128)} %get-tuple-element.17.numerators_in, f32[256,512]{1,0:T(8,128)} %get-tuple-element.18.denominators_in, ...), custom_call_target="tpu_custom_call" | custom-call | flops 399999991808 | bytes 6000000 | tf_op jit(solution)/shard_map/layer/pallas_call | solution.py:414
  81.9 0.0 collective-permute-done.7.weights
  81.9 3.5 %finish.1 = bf16[256,512]{1,0:T(8,128)(2,1)} custom-call(f32[256,512]{1,0:T(8,128)} %get-tuple-element.19.partial, bf16[256,512]{1,0:T(8,128)(2,1)S(1)} %get-tuple-element.20.normed, bf16[4,2,512,256]{3,2,1,0:T(8,128)(2,1)} %collective-permute-done.7.weights), custom_call_target="tpu_custom_call" | custom-call | tf_op jit(solution)/shard_map/finish/pallas_call | solution.py:449
Async XLA Ops:
  0.0 51.3 %copy-start = (s32[2,6]{1,0:T(2,128)S(1)}, s32[2,6]{1,0:T(2,128)}, u32[]{:S(2)}) copy-start(s32[2,6]{1,0:T(2,128)} %tile_lists.3) | copy-start | bytes 148
  2.4 42.8 %collective-permute-start.1 = (bf16[2,256,512]{2,1,0:T(8,128)(2,1)}, bf16[2,256,512]{2,1,0:T(8,128)(2,1)S(1)}, u32[]{:S(2)}, u32[]{:S(2)}) collective-permute-start(bf16[2,256,512]{2,1,0:T(8,128)(2,1)} %get-tuple-element.14), channel_id=1, source_target_pairs={{1,0},{2,1},{3,2},{4,3},{5,4},{6,5},{7,6},{8,7},{9,8},{10,9},{11,1... | collective-permute-start | bytes 1572872 | tf_op jit(solution)/shard_map/ppermute | solution.py:291
  3.7 42.8 %collective-permute-start = (bf16[2,256,512]{2,1,0:T(8,128)(2,1)}, bf16[2,256,512]{2,1,0:T(8,128)(2,1)S(1)}, u32[]{:S(2)}, u32[]{:S(2)}) collective-permute-start(bf16[2,256,512]{2,1,0:T(8,128)(2,1)} %get-tuple-element.14), channel_id=1, source_target_pairs={{0,1},{1,2},{2,3},{3,4},{4,5},{5,6},{6,7},{7,8},{8,9},{9,10},{10,1... | collective-permute-start | bytes 1572872 | tf_op jit(solution)/shard_map/ppermute | solution.py:291
  8.4 20.5 %all-to-all-start = ((f32[32,16,128]{2,1,0:T(8,128)}), f32[32,16,128]{2,1,0:T(8,128)S(1)}, u32[]{:S(2)}, u32[]{:S(2)}) async-start(f32[32,16,128]{2,1,0:T(8,128)} %get-tuple-element.13), calls=%async_computation | async-start | bytes 524288 | tf_op jit(solution)/shard_map/all_to_all | solution.py:300
  18.8 37.9 %collective-permute-start.4 = (bf16[2,512,256]{2,1,0:T(8,128)(2,1)}, bf16[2,512,256]{2,1,0:T(8,128)(2,1)S(1)}, u32[]{:S(2)}, u32[]{:S(2)}) collective-permute-start(bf16[2,512,256]{2,1,0:T(8,128)(2,1)} %get-tuple-element.16.w_0), channel_id=1, source_target_pairs={{0,256},{128,384},{256,0},{384,128},{1,257},{129,385},{257,1},{385... | collective-permute-start | bytes 1572872 | tf_op jit(solution)/shard_map/ppermute | solution.py:296
  23.6 33.1 %collective-permute-start.3 = (bf16[2,512,256]{2,1,0:T(8,128)(2,1)}, bf16[2,512,256]{2,1,0:T(8,128)(2,1)S(1)}, u32[]{:S(2)}, u32[]{:S(2)}) collective-permute-start(bf16[2,512,256]{2,1,0:T(8,128)(2,1)} %get-tuple-element.16.w_0), channel_id=1, source_target_pairs={{0,384},{128,0},{256,128},{384,256},{1,385},{129,1},{257,129},{385... | collective-permute-start | bytes 1572872 | tf_op jit(solution)/shard_map/ppermute | solution.py:296
  26.4 30.3 %collective-permute-start.2 = (bf16[2,512,256]{2,1,0:T(8,128)(2,1)}, bf16[2,512,256]{2,1,0:T(8,128)(2,1)S(1)}, u32[]{:S(2)}, u32[]{:S(2)}) collective-permute-start(bf16[2,512,256]{2,1,0:T(8,128)(2,1)} %get-tuple-element.16.w_0), channel_id=1, source_target_pairs={{0,128},{128,256},{256,384},{384,0},{1,129},{129,257},{257,385},{3... | collective-permute-start | bytes 1572872 | tf_op jit(solution)/shard_map/ppermute | solution.py:296
  29.6 27.6 %all-to-all-start.1 = ((f32[16,16,128]{2,1,0:T(8,128)}), f32[16,16,128]{2,1,0:T(8,128)S(1)}, u32[]{:S(2)}, u32[]{:S(2)}) async-start(f32[16,16,128]{2,1,0:T(8,128)} %plane_sum.1.after), calls=%async_computation.1 | async-start | bytes 262144 | tf_op jit(solution)/shard_map/all_to_all | solution.py:300
  45.2 29.4 %collective-permute-start.6 = (bf16[2,256,512]{2,1,0:T(8,128)(2,1)S(1)}, bf16[2,256,512]{2,1,0:T(8,128)(2,1)S(1)}, u32[]{:S(2)}, u32[]{:S(2)}) collective-permute-start(bf16[2,256,512]{2,1,0:T(8,128)(2,1)S(1)} %collective-permute-done.1.kv_p1), channel_id=1, source_target_pairs={{1,0},{2,1},{3,2},{4,3},{5,4},{6,5},{7,6},{8,7},{9,8},{10,9},{11,1... | collective-permute-start | bytes 1572872 | tf_op jit(solution)/shard_map/ppermute | solution.py:291
  46.5 28.1 %collective-permute-start.5 = (bf16[2,256,512]{2,1,0:T(8,128)(2,1)S(1)}, bf16[2,256,512]{2,1,0:T(8,128)(2,1)}, u32[]{:S(2)}, u32[]{:S(2)}) collective-permute-start(bf16[2,256,512]{2,1,0:T(8,128)(2,1)S(1)} %collective-permute-done.kv_m1), channel_id=1, source_target_pairs={{0,1},{1,2},{2,3},{3,4},{4,5},{5,6},{6,7},{7,8},{8,9},{9,10},{10,1... | collective-permute-start | bytes 1572872 | tf_op jit(solution)/shard_map/ppermute | solution.py:291
  57.9 16.7 %all-to-all-start.2 = ((bf16[32,16,128]{2,1,0:T(8,128)(2,1)}), bf16[32,16,128]{2,1,0:T(8,128)(2,1)S(1)}, u32[]{:S(2)}, u32[]{:S(2)}) async-start(bf16[32,16,128]{2,1,0:T(8,128)(2,1)} %pooled.1.after), calls=%async_computation.2 | async-start | bytes 262144 | tf_op jit(solution)/shard_map/all_to_all | solution.py:300
  69.6 12.4 %collective-permute-start.7 = (bf16[4,2,512,256]{3,2,1,0:T(8,128)(2,1)}, bf16[4,2,512,256]{3,2,1,0:T(8,128)(2,1)}, u32[]{:S(2)}, u32[]{:S(2)}) collective-permute-start(bf16[4,2,512,256]{3,2,1,0:T(8,128)(2,1)} %stack.1.w_near_in), channel_id=1, source_target_pairs={{0,64},{64,0},{1,65},{65,1},{2,66},{66,2},{3,67},{67,3},{4,68},{68... | collective-permute-start | bytes 6291464 | tf_op jit(solution)/shard_map/ppermute | solution.py:296

commit v4 on v3

v4 whole, which is shorter than its diff:
```python
import functools
import math

import jax
import jax.numpy as jnp
from jax import lax
from jax.experimental import pallas as pl
from jax.experimental.pallas import tpu as pltpu
from jax.sharding import Mesh
from jax.sharding import PartitionSpec as P

HEADS = 8
BLOCK = 128
VIRTUAL = 64
REACH = 2
TMAX = 6
LANES = 128
LOG2E = 1.4426950408889634
AXES = ("x", "c", "z", "y")
DOM = ("z", "y")
PLANE = ("x", "c", "y")
VMEM = pltpu.VMEM
F32 = jnp.float32
BF16 = jnp.bfloat16


def pool_kernel(
    virtual_of_in, keys_in, values_in, up_in, down_in, sums, key_value, weights, virtual_of, sem
):
    copies = [
        pltpu.make_async_copy(source, target, sem.at[i])
        for i, (source, target) in enumerate(
            (
                (virtual_of_in, virtual_of),
                (keys_in, key_value.at[0]),
                (values_in, key_value.at[1]),
                (up_in, weights.at[0]),
                (down_in, weights.at[1]),
            )
        )
    ]
    for copy in copies:
        copy.start()
    for copy in copies[:3]:
        copy.wait()
    node_rows, feat_width = key_value.shape[1:]
    ids = lax.broadcasted_iota(jnp.int32, (VIRTUAL, node_rows), 0)
    members = jnp.where(virtual_of[...] == ids, 1.0, 0.0).astype(BF16)
    per_part = sums.shape[1]
    lane_parts = feat_width // LANES
    rows_parts = VIRTUAL // per_part
    for which in range(2):
        pooled = jnp.dot(members, key_value[which], preferred_element_type=F32)
        for row in range(rows_parts):
            for lane in range(lane_parts):
                sums[(which * rows_parts + row) * lane_parts + lane] = pooled[
                    row * per_part : (row + 1) * per_part, lane * LANES : (lane + 1) * LANES
                ]
    for copy in copies[3:]:
        copy.wait()


def plane_sum_kernel(parts, total):
    total[...] = jnp.broadcast_to(jnp.sum(parts[...], axis=0, keepdims=True), total.shape)


def pooled_kernel(scale, parts, after, after_1, after_2, pooled):
    mean = (jnp.sum(parts[...], axis=0, keepdims=True) * scale).astype(BF16)
    pooled[...] = jnp.broadcast_to(mean, pooled.shape)


def stack_kernel(after, w_0, w_1, w_2, w_3, stacked):
    for i, piece in enumerate((w_0, w_1, w_2, w_3)):
        stacked[i] = piece[...]


def named(tile_lists, block, wanted):
    found = tile_lists[block, 0] == wanted
    for slot in range(1, TMAX):
        found = jnp.logical_or(found, tile_lists[block, slot] == wanted)
    return jnp.logical_and(found, wanted >= 0)


def gate_kernel(after, left, right, token):
    token[...] = jnp.zeros_like(token)


def layer_kernel(
    tile_lists,
    virtual_kv,
    queries_in,
    keys,
    values,
    kv_m1,
    kv_p1,
    kv_m2,
    kv_p2,
    out_weight_in,
    node_feats_in,
    norm_gain_in,
    w_near_in,
    partial_out,
    normed_out,
    queries,
    window,
    out_weight,
    node_feats,
    norm_gain,
    w_near,
    attended,
    sem,
):
    rows, feat_width = queries.shape
    near = w_near.shape[0]
    middle = REACH * rows
    moves = [
        (queries_in, queries),
        (keys, window.at[0, pl.ds(middle, rows)]),
        (values, window.at[1, pl.ds(middle, rows)]),
        (kv_m1, window.at[:, pl.ds(rows, rows)]),
        (kv_p1, window.at[:, pl.ds(3 * rows, rows)]),
        (kv_m2, window.at[:, pl.ds(0, rows)]),
        (kv_p2, window.at[:, pl.ds(4 * rows, rows)]),
        (out_weight_in, out_weight),
        (node_feats_in, node_feats),
        (norm_gain_in, norm_gain),
    ]
    moves += [(w_near_in.at[shard], w_near.at[shard]) for shard in range(near)]
    copies = [
        pltpu.make_async_copy(source, target, sem.at[i])
        for i, (source, target) in enumerate(moves)
    ]
    for copy in copies:
        copy.start()
    head_dim = feat_width // HEADS
    scale = LOG2E / math.sqrt(head_dim)
    lane_parts = feat_width // LANES
    rows_parts = VIRTUAL // virtual_kv.shape[1]
    blocks = rows // BLOCK
    places = (2 * REACH + 1) * blocks
    low = lax.broadcasted_iota(jnp.int32, (BLOCK, LANES), 1) < head_dim
    ones = jnp.ones((places * BLOCK + VIRTUAL, LANES), BF16)
    first_block = tile_lists[0, 0] - REACH * blocks
    bias = [
        jnp.concatenate(
            [
                jnp.full(
                    (1, BLOCK),
                    jnp.where(named(tile_lists, block, first_block + place), 0.0, -jnp.inf),
                    F32,
                )
                for place in range(places)
            ]
            + [jnp.zeros((1, VIRTUAL), F32)],
            axis=1,
        )
        for block in range(blocks)
    ]
    for copy in copies[:7]:
        copy.wait()
    for part in range(lane_parts):
        lanes = slice(part * LANES, (part + 1) * LANES)
        pooled = [virtual_kv[r * lane_parts + part] for r in range(2 * rows_parts)]
        all_keys = jnp.concatenate([window[0, :, lanes]] + pooled[:rows_parts], axis=0)
        all_values = jnp.concatenate([window[1, :, lanes]] + pooled[rows_parts:], axis=0)
        right = jnp.concatenate([all_values, ones], axis=1)
        for block in range(blocks):
            here = slice(block * BLOCK, (block + 1) * BLOCK)
            pair = queries[here, lanes]
            zero = jnp.zeros_like(pair)
            both = jnp.concatenate(
                [jnp.where(low, pair, zero), jnp.where(low, zero, pair)], axis=0
            )
            scores = lax.dot_general(
                both, all_keys, (((1,), (1,)), ((), ())), preferred_element_type=F32
            )
            scores = scores * scale + bias[block]
            row_max = jnp.max(scores, axis=-1, keepdims=True)
            exponent = jnp.exp2(scores - row_max).astype(BF16)
            summed = jnp.dot(exponent, right, preferred_element_type=F32)
            result = summed[:, :LANES] / summed[:, LANES:]
            attended[here, lanes] = jnp.where(low, result[:BLOCK], result[BLOCK:]).astype(BF16)

    for copy in copies[7:10]:
        copy.wait()
    residual = node_feats[...].astype(F32) + jnp.dot(
        attended[...], out_weight[...], preferred_element_type=F32
    )
    row_mean = jnp.mean(residual, axis=-1, keepdims=True)
    centered = residual - row_mean
    variance = jnp.mean(centered * centered, axis=-1, keepdims=True)
    normed = (centered * lax.rsqrt(variance + 1e-05) * norm_gain[...]).astype(BF16)
    normed_out[...] = normed
    partial_out[...] = residual + hidden_sum(normed, w_near, copies[10:])


def hidden_sum(normed, weights, copies):
    total = 0.0
    for shard, copy in enumerate(copies):
        copy.wait()
        hidden = jnp.dot(normed, weights[shard, 0], preferred_element_type=F32)
        hidden = jnp.maximum(hidden, 0.0).astype(BF16)
        total = total + lax.dot_general(
            hidden, weights[shard, 1], (((1,), (1,)), ((), ())), preferred_element_type=F32
        )
    return total


def finish_kernel(partial, normed, weights_in, layer_out, weights, sem):
    copies = [
        pltpu.make_async_copy(weights_in.at[shard], weights.at[shard], sem.at[shard])
        for shard in range(weights.shape[0])
    ]
    for copy in copies:
        copy.start()
    layer_out[...] = (partial[...] + hidden_sum(normed[...], weights, copies)).astype(BF16)


def along_dom(shard, by):
    length = lax.axis_size(DOM)
    pairs = [(i, i + by) for i in range(length) if 0 <= i + by < length]
    return lax.ppermute(shard, DOM, pairs)


def around(shard, axis, by):
    length = lax.axis_size(axis)
    return lax.ppermute(shard, axis, [(i, (i + by) % length) for i in range(length)])


def exchanged(parts, axes):
    return lax.all_to_all(parts, axes, 0, 0, tiled=True)


def local(
    node_feats,
    queries,
    keys,
    values,
    out_weight,
    up_weight,
    down_weight,
    norm_gain,
    tile_lists,
    virtual_of,
):
    node_rows, feat_width = queries.shape
    plane = lax.axis_size(PLANE)
    depth = lax.axis_size("z")
    near = lax.axis_size("x")
    per_part = 2 * VIRTUAL * feat_width // LANES // plane
    own_hidden = up_weight.shape[1]
    in_vmem = pl.BlockSpec(memory_space=VMEM)
    in_smem = pl.BlockSpec(memory_space=pltpu.SMEM)
    anywhere = pl.BlockSpec(memory_space=pl.ANY)
    shape = jax.ShapeDtypeStruct

    def grant(mib):
        return pltpu.CompilerParams(vmem_limit_bytes=mib * 1024 * 1024)

    def hbm(array):
        return pltpu.with_memory_space_constraint(array, pltpu.HBM)

    def vmem(array):
        return pltpu.with_memory_space_constraint(array, VMEM)

    def dma(count):
        return pltpu.SemaphoreType.DMA((count,))

    kv_shape = (2, node_rows, feat_width)
    w_shape = (2, feat_width, own_hidden)
    sums, key_value, w_0 = pl.pallas_call(
        pool_kernel,
        out_shape=(
            shape((plane, per_part, LANES), F32),
            pltpu.HBM(kv_shape, BF16),
            pltpu.HBM(w_shape, BF16),
        ),
        in_specs=[anywhere] * 5,
        out_specs=(in_vmem,) * 3,
        scratch_shapes=[VMEM((1, node_rows), jnp.int32), dma(5)],
        compiler_params=grant(6),
        name="pool",
    )(
        hbm(virtual_of.reshape(1, node_rows)),
        hbm(keys),
        hbm(values),
        hbm(up_weight),
        hbm(down_weight),
    )
    parts = exchanged(sums, PLANE)
    kv_m1 = along_dom(key_value, 1)
    kv_p1 = along_dom(key_value, -1)
    w_1 = around(w_0, "x", 1)
    w_2 = around(w_0, "x", -1)
    w_3 = around(w_0, "x", 2)

    plane_sum = pl.pallas_call(
        plane_sum_kernel,
        out_shape=shape((depth, per_part, LANES), F32),
        in_specs=[in_vmem],
        out_specs=in_vmem,
        compiler_params=grant(2),
        cost_estimate=pl.CostEstimate(
            flops=8_000_000_000, bytes_accessed=400_000, transcendentals=0
        ),
        name="plane_sum",
    )(parts)

    parts = exchanged(plane_sum, "z")
    kv_m2 = along_dom(kv_m1, 1)
    kv_p2 = along_dom(kv_p1, -1)
    token = pl.pallas_call(
        gate_kernel,
        out_shape=pltpu.HBM((8, LANES), F32),
        in_specs=[anywhere] * 3,
        out_specs=in_vmem,
        compiler_params=grant(2),
        cost_estimate=pl.CostEstimate(
            flops=4_000_000_000, bytes_accessed=6_000_000, transcendentals=2_000_000
        ),
        name="gate",
    )(plane_sum, kv_m1, kv_p1)

    pool_scale = math.sqrt(VIRTUAL / (node_rows * lax.axis_size(AXES)))
    pooled = pl.pallas_call(
        functools.partial(pooled_kernel, pool_scale),
        out_shape=shape((plane, per_part, LANES), BF16),
        in_specs=[in_vmem] + [anywhere] * 3,
        out_specs=in_vmem,
        compiler_params=grant(2),
        name="pooled",
    )(parts, hbm(token), w_1, w_2)

    virtual_kv = exchanged(pooled, PLANE)
    w_near = pl.pallas_call(
        stack_kernel,
        out_shape=pltpu.HBM((near, *w_shape), BF16),
        in_specs=[anywhere] + [in_vmem] * near,
        out_specs=in_vmem,
        compiler_params=grant(6),
        name="stack",
    )(pooled, hbm(w_0), w_1, w_2, w_3)
    w_far = around(w_near, "c", 1)

    partial, normed = pl.pallas_call(
        layer_kernel,
        out_shape=(VMEM((node_rows, feat_width), F32), VMEM((node_rows, feat_width), BF16)),
        in_specs=[in_smem, in_vmem] + [anywhere] * 11,
        out_specs=(in_vmem,) * 2,
        scratch_shapes=[
            VMEM((node_rows, feat_width), BF16),
            VMEM((2, (2 * REACH + 1) * node_rows, feat_width), BF16),
            VMEM(out_weight.shape, BF16),
            VMEM((node_rows, feat_width), BF16),
            VMEM((1, feat_width), F32),
            VMEM((near, *w_shape), BF16),
            VMEM((node_rows, feat_width), BF16),
            dma(10 + near),
        ],
        compiler_params=grant(20),
        cost_estimate=pl.CostEstimate(
            flops=400_000_000_000, bytes_accessed=6_000_000, transcendentals=2_000_000
        ),
        name="layer",
    )(
        tile_lists,
        virtual_kv,
        hbm(queries),
        hbm(keys),
        hbm(values),
        kv_m1,
        kv_p1,
        kv_m2,
        kv_p2,
        hbm(out_weight),
        hbm(node_feats),
        hbm(norm_gain.reshape(1, feat_width)),
        hbm(w_near),
    )
    return pl.pallas_call(
        finish_kernel,
        out_shape=shape((node_rows, feat_width), BF16),
        in_specs=[in_vmem, in_vmem, anywhere],
        out_specs=in_vmem,
        scratch_shapes=[VMEM((near, *w_shape), BF16), dma(near)],
        compiler_params=grant(10),
        name="finish",
    )(vmem(partial), vmem(normed), w_far)


def solution(mesh):
    group, dom = mesh.devices.shape
    fine = Mesh(mesh.devices.reshape(group // 2, 2, dom // 4, 4), AXES)
    placed = (
        P(AXES, None),
        P(AXES, None),
        P(AXES, None),
        P(AXES, None),
        P(),
        P(None, ("x", "c")),
        P(None, ("x", "c")),
        P(),
        P(AXES, None),
        P(AXES),
    )
    return jax.shard_map(
        local, mesh=fine, in_specs=placed, out_specs=P(AXES, None), check_vma=False
    )
```

time: 86.1 us -> 83.8 us (0.973)
  Pallas kernels: 22.4 us -> 19.1 us
  waiting for transfers between devices: 3.49 us -> 4.59 us
    pallas_call x2, Pallas kernels: 12.6 us -> 9.6 us  [the longest x1 9.01 us: local(): pl.pallas_call(layer_kernel, out_shape=(VMEM((node_rows, feat_width), F32...]
    all_to_all x3, waiting for transfers between devices: 3.47 us -> 4.57 us  [exchanged(): return lax.all_to_all(parts, axes, 0, 0, tiled=True)]
  transfers between devices with their start and end apart: 11 -> 11, of which waited for: 2 -> 2; matrix products, arithmetic and copies ran while one was open for 0% -> 0% of each run, Pallas kernels for 19% -> 16%
where the time goes in v4:
time: 83.8 us; the launch traced here: 83.2 us
  starting transfers between devices  59.4 us (71%)
  Pallas kernels  19.1 us (23%)
  waiting for transfers between devices  4.59 us (5%)
    all_to_all x3, starting transfers between devices, exchanged(): return lax.all_to_all(parts, axes, 0, 0, tiled=True)  35.7 us
    ppermute x4, starting transfers between devices, around(): lax.ppermute(shard, axis, [(i, (i + by) % length) for i in range(length)])  12.3 us
    ppermute x4, starting transfers between devices, along_dom(): return lax.ppermute(shard, DOM, pairs)  11.4 us
    pallas_call x1, Pallas kernels, local(): pl.pallas_call(layer_kernel, out_shape=(VMEM((node_rows, feat_width), F32...  9.01 us
    all_to_all x3, waiting for transfers between devices, exchanged(): return lax.all_to_all(parts, axes, 0, 0, tiled=True)  4.57 us
    pallas_call x1, Pallas kernels, local(): pl.pallas_call(finish_kernel, out_shape=shape((node_rows, feat_width), BF...  3.21 us
    pallas_call x1, Pallas kernels, local(): pl.pallas_call(stack_kernel, out_shape=pltpu.HBM((near, *w_shape), BF16),...  2.51 us
    pallas_call x1, Pallas kernels, local(): pl.pallas_call(pool_kernel, out_shape=(shape((plane, per_part, LANES), F3...  2.37 us
  transfers between devices with their start and end apart: 11, of which 2 were waited for; matrix products, arithmetic and copies ran while one was open for 0% of the time, Pallas kernels for 16%

profile of v4, /device:TPU:1, one launch (start us, length us, event | category | flops | bytes accessed | tf_op | source)
XLA Modules:
  0.0 83.2 jit_solution(11270764259057998108)
XLA Ops:
  0.0 2.4 %pool.1 = (f32[32,16,128]{2,1,0:T(8,128)}, bf16[2,256,512]{2,1,0:T(8,128)(2,1)}, bf16[2,512,256]{2,1,0:T(8,128)(2,1)}) custom-call(s32[1,256]{1,0:T(1,128)} %bitcast.2, bf16[256,512]{1,0:T(8,128)(2,1)} %keys.1, bf16[256,512]{1,0:T(8,128)(2,1)} %values.1, bf16[512,256]{1,0:T(8,128)(2,1)} %up_in.1, bf16[512,256]{1,0:T(8,128)(2,1)} %down_in.1), custom_call_target="tpu_custom_call" | custom-call | tf_op jit(solution)/shard_map/pool/pallas_call | solution.py:271
  2.4 10.4 %all-to-all-start = ((f32[32,16,128]{2,1,0:T(8,128)}), f32[32,16,128]{2,1,0:T(8,128)S(1)}, u32[]{:S(2)}, u32[]{:S(2)}) async-start(f32[32,16,128]{2,1,0:T(8,128)} %get-tuple-element.10), calls=%async_computation | async-start | bytes 524288 | tf_op jit(solution)/shard_map/all_to_all | solution.py:231
  12.8 1.3 %collective-permute-start.1 = (bf16[2,256,512]{2,1,0:T(8,128)(2,1)}, bf16[2,256,512]{2,1,0:T(8,128)(2,1)S(1)}, u32[]{:S(2)}, u32[]{:S(2)}) collective-permute-start(bf16[2,256,512]{2,1,0:T(8,128)(2,1)} %get-tuple-element.11), channel_id=1, source_target_pairs={{1,0},{2,1},{3,2},{4,3},{5,4},{6,5},{7,6},{8,7},{9,8},{10,9},{11,1... | collective-permute-start | bytes 1572872 | tf_op jit(solution)/shard_map/ppermute | solution.py:222
  14.1 4.0 %collective-permute-start = (bf16[2,256,512]{2,1,0:T(8,128)(2,1)}, bf16[2,256,512]{2,1,0:T(8,128)(2,1)S(1)}, u32[]{:S(2)}, u32[]{:S(2)}) collective-permute-start(bf16[2,256,512]{2,1,0:T(8,128)(2,1)} %get-tuple-element.11), channel_id=1, source_target_pairs={{0,1},{1,2},{2,3},{3,4},{4,5},{5,6},{6,7},{7,8},{8,9},{9,10},{10,1... | collective-permute-start | bytes 1572872 | tf_op jit(solution)/shard_map/ppermute | solution.py:222
  18.1 4.6 %collective-permute-start.3 = (bf16[2,512,256]{2,1,0:T(8,128)(2,1)}, bf16[2,512,256]{2,1,0:T(8,128)(2,1)S(1)}, u32[]{:S(2)}, u32[]{:S(2)}) collective-permute-start(bf16[2,512,256]{2,1,0:T(8,128)(2,1)} %get-tuple-element.12.w_0), channel_id=1, source_target_pairs={{0,384},{128,0},{256,128},{384,256},{1,385},{129,1},{257,129},{385... | collective-permute-start | bytes 1572872 | tf_op jit(solution)/shard_map/ppermute | solution.py:227
  22.8 1.9 %collective-permute-start.2 = (bf16[2,512,256]{2,1,0:T(8,128)(2,1)}, bf16[2,512,256]{2,1,0:T(8,128)(2,1)S(1)}, u32[]{:S(2)}, u32[]{:S(2)}) collective-permute-start(bf16[2,512,256]{2,1,0:T(8,128)(2,1)} %get-tuple-element.12.w_0), channel_id=1, source_target_pairs={{0,128},{128,256},{256,384},{384,0},{1,129},{129,257},{257,385},{3... | collective-permute-start | bytes 1572872 | tf_op jit(solution)/shard_map/ppermute | solution.py:227
  24.7 0.0 all-to-all-done.parts
  24.7 0.7 plane_sum.1.after
  25.4 13.9 %all-to-all-start.1 = ((f32[16,16,128]{2,1,0:T(8,128)}), f32[16,16,128]{2,1,0:T(8,128)S(1)}, u32[]{:S(2)}, u32[]{:S(2)}) async-start(f32[16,16,128]{2,1,0:T(8,128)} %plane_sum.1.after), calls=%async_computation.1 | async-start | bytes 262144 | tf_op jit(solution)/shard_map/all_to_all | solution.py:231
  39.4 3.6 %collective-permute-start.6 = (bf16[2,512,256]{2,1,0:T(8,128)(2,1)}, bf16[2,512,256]{2,1,0:T(8,128)(2,1)S(1)}, u32[]{:S(2)}, u32[]{:S(2)}) collective-permute-start(bf16[2,512,256]{2,1,0:T(8,128)(2,1)} %get-tuple-element.12.w_0), channel_id=1, source_target_pairs={{0,256},{128,384},{256,0},{384,128},{1,257},{129,385},{257,1},{385... | collective-permute-start | bytes 1572872 | tf_op jit(solution)/shard_map/ppermute | solution.py:227
  43.0 0.0 collective-permute-done.1.right.kv_p1
  43.0 1.3 %collective-permute-start.5 = (bf16[2,256,512]{2,1,0:T(8,128)(2,1)S(1)}, bf16[2,256,512]{2,1,0:T(8,128)(2,1)S(1)}, u32[]{:S(2)}, u32[]{:S(2)}) collective-permute-start(bf16[2,256,512]{2,1,0:T(8,128)(2,1)S(1)} %collective-permute-done.1.right.kv_p1), channel_id=1, source_target_pairs={{1,0},{2,1},{3,2},{4,3},{5,4},{6,5},{7,6},{8,7},{9,8},{10,9},{11,1... | collective-permute-start | bytes 1572872 | tf_op jit(solution)/shard_map/ppermute | solution.py:222
  44.3 0.0 collective-permute-done.left.kv_m1
  44.3 4.8 %collective-permute-start.4 = (bf16[2,256,512]{2,1,0:T(8,128)(2,1)S(1)}, bf16[2,256,512]{2,1,0:T(8,128)(2,1)}, u32[]{:S(2)}, u32[]{:S(2)}) collective-permute-start(bf16[2,256,512]{2,1,0:T(8,128)(2,1)S(1)} %collective-permute-done.left.kv_m1), channel_id=1, source_target_pairs={{0,1},{1,2},{2,3},{3,4},{4,5},{5,6},{6,7},{7,8},{8,9},{9,10},{10,1... | collective-permute-start | bytes 1572872 | tf_op jit(solution)/shard_map/ppermute | solution.py:222
  49.1 0.6 gate.1.after
  49.7 0.0 collective-permute-done.3.after_2.w_2
  49.7 0.0 collective-permute-done.2.after_1.w_1
  49.7 1.7 %all-to-all-done.1.parts = f32[16,16,128]{2,1,0:T(8,128)S(1)} async-done(((f32[16,16,128]{2,1,0:T(8,128)}), f32[16,16,128]{2,1,0:T(8,128)S(1)}, u32[]{:S(2)}, u32[]{:S(2)}) %all-to-all-start.1) | async-done | bytes 131104 | tf_op jit(solution)/shard_map/all_to_all | solution.py:231
  51.4 0.7 pooled.1.after
  52.0 11.3 %all-to-all-start.2 = ((bf16[32,16,128]{2,1,0:T(8,128)(2,1)}), bf16[32,16,128]{2,1,0:T(8,128)(2,1)S(1)}, u32[]{:S(2)}, u32[]{:S(2)}) async-start(bf16[32,16,128]{2,1,0:T(8,128)(2,1)} %pooled.1.after), calls=%async_computation.2 | async-start | bytes 262144 | tf_op jit(solution)/shard_map/all_to_all | solution.py:231
  63.4 0.0 copy-start
  63.4 0.0 collective-permute-done.6.w_3
  63.4 2.5 %stack.1.w_near_in = bf16[4,2,512,256]{3,2,1,0:T(8,128)(2,1)} custom-call(bf16[32,16,128]{2,1,0:T(8,128)(2,1)} %pooled.1.after, bf16[2,512,256]{2,1,0:T(8,128)(2,1)} %get-tuple-element.12.w_0, bf16[2,512,256]{2,1,0:T(8,128)(2,1)S(1)} %collective-permute-done.2.after_1.w_1, bf16[2,512,256]{2,1,0:T(8,128)(2,1)S(1)} %collective-permute-done.3.after_2.w_2, ...), custom_call_target="tpu_custom_call" | custom-call | tf_op jit(solution)/shard_map/stack/pallas_call | solution.py:335
  65.9 2.1 %collective-permute-start.7 = (bf16[4,2,512,256]{3,2,1,0:T(8,128)(2,1)}, bf16[4,2,512,256]{3,2,1,0:T(8,128)(2,1)}, u32[]{:S(2)}, u32[]{:S(2)}) collective-permute-start(bf16[4,2,512,256]{3,2,1,0:T(8,128)(2,1)} %stack.1.w_near_in), channel_id=1, source_target_pairs={{0,64},{64,0},{1,65},{65,1},{2,66},{66,2},{3,67},{67,3},{4,68},{68... | collective-permute-start | bytes 6291464 | tf_op jit(solution)/shard_map/ppermute | solution.py:227
  68.1 2.9 %all-to-all-done.2.virtual_kv = bf16[32,16,128]{2,1,0:T(8,128)(2,1)S(1)} async-done(((bf16[32,16,128]{2,1,0:T(8,128)(2,1)}), bf16[32,16,128]{2,1,0:T(8,128)(2,1)S(1)}, u32[]{:S(2)}, u32[]{:S(2)}) %all-to-all-start.2) | async-done | bytes 131104 | tf_op jit(solution)/shard_map/all_to_all | solution.py:231
  71.0 0.0 collective-permute-done.5.kv_p2
  71.0 0.0 collective-permute-done.4.kv_m2
  71.0 0.0 copy-done
  71.0 9.0 %layer.1 = (f32[256,512]{1,0:T(8,128)S(1)}, bf16[256,512]{1,0:T(8,128)(2,1)S(1)}) custom-call(s32[2,6]{1,0:T(2,128)S(1)} %copy-done, bf16[32,16,128]{2,1,0:T(8,128)(2,1)S(1)} %all-to-all-done.2.virtual_kv, bf16[256,512]{1,0:T(8,128)(2,1)} %queries_in.1, bf16[256,512]{1,0:T(8,128)(2,1)} %keys.1, bf16[256,512]{1,0:T(8,128)(2,1)} %values.1, ...), custom_call_target="tpu_custom_call" | custom-call | flops 399999991808 | bytes 6000000 | tf_op jit(solution)/shard_map/layer/pallas_call | solution.py:345
  80.0 0.0 collective-permute-done.7.weights_in
  80.0 3.2 %finish.1 = bf16[256,512]{1,0:T(8,128)(2,1)} custom-call(f32[256,512]{1,0:T(8,128)S(1)} %get-tuple-element.13.partial, bf16[256,512]{1,0:T(8,128)(2,1)S(1)} %get-tuple-element.14.normed, bf16[4,2,512,256]{3,2,1,0:T(8,128)(2,1)} %collective-permute-done.7.weights_in), custom_call_target="tpu_custom_call" | custom-call | tf_op jit(solution)/shard_map/finish/pallas_call | solution.py:380
Async XLA Ops:
  2.4 22.4 %all-to-all-start = ((f32[32,16,128]{2,1,0:T(8,128)}), f32[32,16,128]{2,1,0:T(8,128)S(1)}, u32[]{:S(2)}, u32[]{:S(2)}) async-start(f32[32,16,128]{2,1,0:T(8,128)} %get-tuple-element.10), calls=%async_computation | async-start | bytes 524288 | tf_op jit(solution)/shard_map/all_to_all | solution.py:231
  12.8 30.2 %collective-permute-start.1 = (bf16[2,256,512]{2,1,0:T(8,128)(2,1)}, bf16[2,256,512]{2,1,0:T(8,128)(2,1)S(1)}, u32[]{:S(2)}, u32[]{:S(2)}) collective-permute-start(bf16[2,256,512]{2,1,0:T(8,128)(2,1)} %get-tuple-element.11), channel_id=1, source_target_pairs={{1,0},{2,1},{3,2},{4,3},{5,4},{6,5},{7,6},{8,7},{9,8},{10,9},{11,1... | collective-permute-start | bytes 1572872 | tf_op jit(solution)/shard_map/ppermute | solution.py:222
  14.1 30.2 %collective-permute-start = (bf16[2,256,512]{2,1,0:T(8,128)(2,1)}, bf16[2,256,512]{2,1,0:T(8,128)(2,1)S(1)}, u32[]{:S(2)}, u32[]{:S(2)}) collective-permute-start(bf16[2,256,512]{2,1,0:T(8,128)(2,1)} %get-tuple-element.11), channel_id=1, source_target_pairs={{0,1},{1,2},{2,3},{3,4},{4,5},{5,6},{6,7},{7,8},{8,9},{9,10},{10,1... | collective-permute-start | bytes 1572872 | tf_op jit(solution)/shard_map/ppermute | solution.py:222
  18.1 31.5 %collective-permute-start.3 = (bf16[2,512,256]{2,1,0:T(8,128)(2,1)}, bf16[2,512,256]{2,1,0:T(8,128)(2,1)S(1)}, u32[]{:S(2)}, u32[]{:S(2)}) collective-permute-start(bf16[2,512,256]{2,1,0:T(8,128)(2,1)} %get-tuple-element.12.w_0), channel_id=1, source_target_pairs={{0,384},{128,0},{256,128},{384,256},{1,385},{129,1},{257,129},{385... | collective-permute-start | bytes 1572872 | tf_op jit(solution)/shard_map/ppermute | solution.py:227
  22.8 26.9 %collective-permute-start.2 = (bf16[2,512,256]{2,1,0:T(8,128)(2,1)}, bf16[2,512,256]{2,1,0:T(8,128)(2,1)S(1)}, u32[]{:S(2)}, u32[]{:S(2)}) collective-permute-start(bf16[2,512,256]{2,1,0:T(8,128)(2,1)} %get-tuple-element.12.w_0), channel_id=1, source_target_pairs={{0,128},{128,256},{256,384},{384,0},{1,129},{129,257},{257,385},{3... | collective-permute-start | bytes 1572872 | tf_op jit(solution)/shard_map/ppermute | solution.py:227
  25.4 25.9 %all-to-all-start.1 = ((f32[16,16,128]{2,1,0:T(8,128)}), f32[16,16,128]{2,1,0:T(8,128)S(1)}, u32[]{:S(2)}, u32[]{:S(2)}) async-start(f32[16,16,128]{2,1,0:T(8,128)} %plane_sum.1.after), calls=%async_computation.1 | async-start | bytes 262144 | tf_op jit(solution)/shard_map/all_to_all | solution.py:231
  39.4 24.0 %collective-permute-start.6 = (bf16[2,512,256]{2,1,0:T(8,128)(2,1)}, bf16[2,512,256]{2,1,0:T(8,128)(2,1)S(1)}, u32[]{:S(2)}, u32[]{:S(2)}) collective-permute-start(bf16[2,512,256]{2,1,0:T(8,128)(2,1)} %get-tuple-element.12.w_0), channel_id=1, source_target_pairs={{0,256},{128,384},{256,0},{384,128},{1,257},{129,385},{257,1},{385... | collective-permute-start | bytes 1572872 | tf_op jit(solution)/shard_map/ppermute | solution.py:227
  43.0 28.0 %collective-permute-start.5 = (bf16[2,256,512]{2,1,0:T(8,128)(2,1)S(1)}, bf16[2,256,512]{2,1,0:T(8,128)(2,1)S(1)}, u32[]{:S(2)}, u32[]{:S(2)}) collective-permute-start(bf16[2,256,512]{2,1,0:T(8,128)(2,1)S(1)} %collective-permute-done.1.right.kv_p1), channel_id=1, source_target_pairs={{1,0},{2,1},{3,2},{4,3},{5,4},{6,5},{7,6},{8,7},{9,8},{10,9},{11,1... | collective-permute-start | bytes 1572872 | tf_op jit(solution)/shard_map/ppermute | solution.py:222
  44.3 26.7 %collective-permute-start.4 = (bf16[2,256,512]{2,1,0:T(8,128)(2,1)S(1)}, bf16[2,256,512]{2,1,0:T(8,128)(2,1)}, u32[]{:S(2)}, u32[]{:S(2)}) collective-permute-start(bf16[2,256,512]{2,1,0:T(8,128)(2,1)S(1)} %collective-permute-done.left.kv_m1), channel_id=1, source_target_pairs={{0,1},{1,2},{2,3},{3,4},{4,5},{5,6},{6,7},{7,8},{8,9},{9,10},{10,1... | collective-permute-start | bytes 1572872 | tf_op jit(solution)/shard_map/ppermute | solution.py:222
  52.0 18.9 %all-to-all-start.2 = ((bf16[32,16,128]{2,1,0:T(8,128)(2,1)}), bf16[32,16,128]{2,1,0:T(8,128)(2,1)S(1)}, u32[]{:S(2)}, u32[]{:S(2)}) async-start(bf16[32,16,128]{2,1,0:T(8,128)(2,1)} %pooled.1.after), calls=%async_computation.2 | async-start | bytes 262144 | tf_op jit(solution)/shard_map/all_to_all | solution.py:231
  63.4 7.6 %copy-start = (s32[2,6]{1,0:T(2,128)S(1)}, s32[2,6]{1,0:T(2,128)}, u32[]{:S(2)}) copy-start(s32[2,6]{1,0:T(2,128)} %tile_lists.1) | copy-start | bytes 148
  65.9 14.1 %collective-permute-start.7 = (bf16[4,2,512,256]{3,2,1,0:T(8,128)(2,1)}, bf16[4,2,512,256]{3,2,1,0:T(8,128)(2,1)}, u32[]{:S(2)}, u32[]{:S(2)}) collective-permute-start(bf16[4,2,512,256]{3,2,1,0:T(8,128)(2,1)} %stack.1.w_near_in), channel_id=1, source_target_pairs={{0,64},{64,0},{1,65},{65,1},{2,66},{66,2},{3,67},{67,3},{4,68},{68... | collective-permute-start | bytes 6291464 | tf_op jit(solution)/shard_map/ppermute | solution.py:227

commit v5 on v4

--- a/solution.py
+++ b/solution.py
@@ -64,14 +64,9 @@
     total[...] = jnp.broadcast_to(jnp.sum(parts[...], axis=0, keepdims=True), total.shape)
 
 
-def pooled_kernel(scale, parts, after, after_1, after_2, pooled):
+def pooled_kernel(scale, parts, after, after_1, pooled):
     mean = (jnp.sum(parts[...], axis=0, keepdims=True) * scale).astype(BF16)
     pooled[...] = jnp.broadcast_to(mean, pooled.shape)
-
-
-def stack_kernel(after, w_0, w_1, w_2, w_3, stacked):
-    for i, piece in enumerate((w_0, w_1, w_2, w_3)):
-        stacked[i] = piece[...]
 
 
 def named(tile_lists, block, wanted):
@@ -81,20 +76,33 @@
     return jnp.logical_and(found, wanted >= 0)
 
 
+def stack_kernel(tile_lists, after, w_0, w_1, w_2, w_3, stacked, bias):
+    for i, piece in enumerate((w_0, w_1, w_2, w_3)):
+        stacked[i] = piece[...]
+    blocks, width = bias.shape
+    first_block = tile_lists[0, 0] - REACH * blocks
+    for block in range(blocks):
+        for place in range((2 * REACH + 1) * blocks):
+            here = pl.ds(place * BLOCK, BLOCK)
+            there = named(tile_lists, block, first_block + place)
+            bias[pl.ds(block, 1), here] = jnp.full((1, BLOCK), jnp.where(there, 0.0, -jnp.inf), F32)
+        bias[pl.ds(block, 1), pl.ds(width - VIRTUAL, VIRTUAL)] = jnp.zeros((1, VIRTUAL), F32)
+
+
 def gate_kernel(after, left, right, token):
     token[...] = jnp.zeros_like(token)
 
 
 def layer_kernel(
-    tile_lists,
     virtual_kv,
+    kv_m1,
+    kv_p1,
+    kv_p2,
+    kv_m2,
     queries_in,
     keys,
     values,
-    kv_m1,
-    kv_p1,
-    kv_m2,
-    kv_p2,
+    bias_in,
     out_weight_in,
     node_feats_in,
     norm_gain_in,
@@ -102,7 +110,9 @@
     partial_out,
     normed_out,
     queries,
-    window,
+    own,
+    left,
+    bias,
     out_weight,
     node_feats,
     norm_gain,
@@ -112,15 +122,12 @@
 ):
     rows, feat_width = queries.shape
     near = w_near.shape[0]
-    middle = REACH * rows
     moves = [
         (queries_in, queries),
-        (keys, window.at[0, pl.ds(middle, rows)]),
-        (values, window.at[1, pl.ds(middle, rows)]),
-        (kv_m1, window.at[:, pl.ds(rows, rows)]),
-        (kv_p1, window.at[:, pl.ds(3 * rows, rows)]),
-        (kv_m2, window.at[:, pl.ds(0, rows)]),
-        (kv_p2, window.at[:, pl.ds(4 * rows, rows)]),
+        (keys, own.at[0]),
+        (values, own.at[1]),
+        (kv_m2, left),
+        (bias_in, bias),
         (out_weight_in, out_weight),
         (node_feats_in, node_feats),
         (norm_gain_in, norm_gain),
@@ -137,32 +144,20 @@
     lane_parts = feat_width // LANES
     rows_parts = VIRTUAL // virtual_kv.shape[1]
     blocks = rows // BLOCK
-    places = (2 * REACH + 1) * blocks
     low = lax.broadcasted_iota(jnp.int32, (BLOCK, LANES), 1) < head_dim
-    ones = jnp.ones((places * BLOCK + VIRTUAL, LANES), BF16)
-    first_block = tile_lists[0, 0] - REACH * blocks
-    bias = [
-        jnp.concatenate(
-            [
-                jnp.full(
-                    (1, BLOCK),
-                    jnp.where(named(tile_lists, block, first_block + place), 0.0, -jnp.inf),
-                    F32,
-                )
-                for place in range(places)
-            ]
-            + [jnp.zeros((1, VIRTUAL), F32)],
-            axis=1,
-        )
-        for block in range(blocks)
-    ]
-    for copy in copies[:7]:
+    ones = jnp.ones((bias.shape[1], LANES), BF16)
+    for copy in copies[:5]:
         copy.wait()
+    pieces = (left, kv_m1, own, kv_p1, kv_p2)
     for part in range(lane_parts):
         lanes = slice(part * LANES, (part + 1) * LANES)
         pooled = [virtual_kv[r * lane_parts + part] for r in range(2 * rows_parts)]
-        all_keys = jnp.concatenate([window[0, :, lanes]] + pooled[:rows_parts], axis=0)
-        all_values = jnp.concatenate([window[1, :, lanes]] + pooled[rows_parts:], axis=0)
+        all_keys = jnp.concatenate(
+            [piece[0, :, lanes] for piece in pieces] + pooled[:rows_parts], axis=0
+        )
+        all_values = jnp.concatenate(
+            [piece[1, :, lanes] for piece in pieces] + pooled[rows_parts:], axis=0
+        )
         right = jnp.concatenate([all_values, ones], axis=1)
         for block in range(blocks):
             here = slice(block * BLOCK, (block + 1) * BLOCK)
@@ -174,14 +169,14 @@
             scores = lax.dot_general(
                 both, all_keys, (((1,), (1,)), ((), ())), preferred_element_type=F32
             )
-            scores = scores * scale + bias[block]
+            scores = scores * scale + bias[pl.ds(block, 1), :]
             row_max = jnp.max(scores, axis=-1, keepdims=True)
             exponent = jnp.exp2(scores - row_max).astype(BF16)
             summed = jnp.dot(exponent, right, preferred_element_type=F32)
             result = summed[:, :LANES] / summed[:, LANES:]
             attended[here, lanes] = jnp.where(low, result[:BLOCK], result[BLOCK:]).astype(BF16)
 
-    for copy in copies[7:10]:
+    for copy in copies[5:8]:
         copy.wait()
     residual = node_feats[...].astype(F32) + jnp.dot(
         attended[...], out_weight[...], preferred_element_type=F32
@@ -191,7 +186,7 @@
     variance = jnp.mean(centered * centered, axis=-1, keepdims=True)
     normed = (centered * lax.rsqrt(variance + 1e-05) * norm_gain[...]).astype(BF16)
     normed_out[...] = normed
-    partial_out[...] = residual + hidden_sum(normed, w_near, copies[10:])
+    partial_out[...] = residual + hidden_sum(normed, w_near, copies[8:])
 
 
 def hidden_sum(normed, weights, copies):
@@ -247,6 +242,7 @@
     plane = lax.axis_size(PLANE)
     depth = lax.axis_size("z")
     near = lax.axis_size("x")
+    blocks = node_rows // BLOCK
     per_part = 2 * VIRTUAL * feat_width // LANES // plane
     own_hidden = up_weight.shape[1]
     in_vmem = pl.BlockSpec(memory_space=VMEM)
@@ -325,37 +321,42 @@
     pooled = pl.pallas_call(
         functools.partial(pooled_kernel, pool_scale),
         out_shape=shape((plane, per_part, LANES), BF16),
-        in_specs=[in_vmem] + [anywhere] * 3,
+        in_specs=[in_vmem] + [anywhere] * 2,
         out_specs=in_vmem,
         compiler_params=grant(2),
         name="pooled",
-    )(parts, hbm(token), w_1, w_2)
+    )(parts, hbm(token), w_3)
 
     virtual_kv = exchanged(pooled, PLANE)
-    w_near = pl.pallas_call(
+    w_near, bias = pl.pallas_call(
         stack_kernel,
-        out_shape=pltpu.HBM((near, *w_shape), BF16),
-        in_specs=[anywhere] + [in_vmem] * near,
-        out_specs=in_vmem,
+        out_shape=(
+            pltpu.HBM((near, *w_shape), BF16),
+            pltpu.HBM((blocks, (2 * REACH + 1) * node_rows + VIRTUAL), F32),
+        ),
+        in_specs=[in_smem, anywhere] + [in_vmem] * near,
+        out_specs=(in_vmem,) * 2,
         compiler_params=grant(6),
         name="stack",
-    )(pooled, hbm(w_0), w_1, w_2, w_3)
+    )(tile_lists, pooled, hbm(w_0), w_1, w_2, w_3)
     w_far = around(w_near, "c", 1)
 
     partial, normed = pl.pallas_call(
         layer_kernel,
         out_shape=(VMEM((node_rows, feat_width), F32), VMEM((node_rows, feat_width), BF16)),
-        in_specs=[in_smem, in_vmem] + [anywhere] * 11,
+        in_specs=[in_vmem] * 4 + [anywhere] * 9,
         out_specs=(in_vmem,) * 2,
         scratch_shapes=[
             VMEM((node_rows, feat_width), BF16),
-            VMEM((2, (2 * REACH + 1) * node_rows, feat_width), BF16),
+            VMEM(kv_shape, BF16),
+            VMEM(kv_shape, BF16),
+            VMEM(bias.shape, F32),
             VMEM(out_weight.shape, BF16),
             VMEM((node_rows, feat_width), BF16),
             VMEM((1, feat_width), F32),
             VMEM((near, *w_shape), BF16),
             VMEM((node_rows, feat_width), BF16),
-            dma(10 + near),
+            dma(8 + near),
         ],
         compiler_params=grant(20),
         cost_estimate=pl.CostEstimate(
@@ -363,15 +364,15 @@
         ),
         name="layer",
     )(
-        tile_lists,
         virtual_kv,
+        kv_m1,
+        kv_p1,
+        kv_p2,
+        kv_m2,
         hbm(queries),
         hbm(keys),
         hbm(values),
-        kv_m1,
-        kv_p1,
-        kv_m2,
-        kv_p2,
+        hbm(bias),
         hbm(out_weight),
         hbm(node_feats),
         hbm(norm_gain.reshape(1, feat_width)),

time: 83.8 us -> 80.3 us (0.958)
  waiting for transfers between devices: 4.59 us -> 2.87 us
  starting transfers between devices: 59.4 us -> 57.9 us
    all_to_all x3, starting transfers between devices: 35.7 us -> 33.7 us  [exchanged(): return lax.all_to_all(parts, axes, 0, 0, tiled=True)]
    all_to_all x3, waiting for transfers between devices: 4.57 us -> 2.85 us  [exchanged(): return lax.all_to_all(parts, axes, 0, 0, tiled=True)]
    ppermute x4, starting transfers between devices: 12.3 us -> 13.4 us  [around(): lax.ppermute(shard, axis, [(i, (i + by) % length) for i in range(length)])]
  transfers between devices with their start and end apart: 11 -> 11, of which waited for: 2 -> 1; matrix products, arithmetic and copies ran while one was open for 0% -> 0% of each run, Pallas kernels for 16% -> 17%
where the time goes in v5:
time: 80.3 us; the launch traced here: 79.7 us
  starting transfers between devices  57.9 us (72%)
  Pallas kernels  18.8 us (23%)
  waiting for transfers between devices  2.87 us (4%)
    all_to_all x3, starting transfers between devices, exchanged(): return lax.all_to_all(parts, axes, 0, 0, tiled=True)  33.7 us
    ppermute x4, starting transfers between devices, around(): lax.ppermute(shard, axis, [(i, (i + by) % length) for i in range(length)])  13.4 us
    ppermute x4, starting transfers between devices, along_dom(): return lax.ppermute(shard, DOM, pairs)  10.7 us
    pallas_call x1, Pallas kernels, local(): pl.pallas_call(layer_kernel, out_shape=(VMEM((node_rows, feat_width), F32...  8.7 us
    pallas_call x1, Pallas kernels, local(): pl.pallas_call(finish_kernel, out_shape=shape((node_rows, feat_width), BF...  3.21 us
    all_to_all x3, waiting for transfers between devices, exchanged(): return lax.all_to_all(parts, axes, 0, 0, tiled=True)  2.85 us
    pallas_call x1, Pallas kernels, local(): pl.pallas_call(stack_kernel, out_shape=(pltpu.HBM((near, *w_shape), BF16)...  2.56 us
    pallas_call x1, Pallas kernels, local(): pl.pallas_call(pool_kernel, out_shape=(shape((plane, per_part, LANES), F3...  2.37 us
  transfers between devices with their start and end apart: 11, of which 1 were waited for; matrix products, arithmetic and copies ran while one was open for 0% of the time, Pallas kernels for 17%

profile of v5, /device:TPU:1, one launch (start us, length us, event | category | flops | bytes accessed | tf_op | source)
XLA Modules:
  0.0 79.7 jit_solution(4566115203468071536)
XLA Ops:
  0.0 2.4 %pool.1 = (f32[32,16,128]{2,1,0:T(8,128)}, bf16[2,256,512]{2,1,0:T(8,128)(2,1)}, bf16[2,512,256]{2,1,0:T(8,128)(2,1)}) custom-call(s32[1,256]{1,0:T(1,128)} %bitcast.2, bf16[256,512]{1,0:T(8,128)(2,1)} %keys.1, bf16[256,512]{1,0:T(8,128)(2,1)} %values.1, bf16[512,256]{1,0:T(8,128)(2,1)} %up_in.1, bf16[512,256]{1,0:T(8,128)(2,1)} %down_in.1), custom_call_target="tpu_custom_call" | custom-call | tf_op jit(solution)/shard_map/pool/pallas_call | solution.py:267
  2.4 10.4 %all-to-all-start = ((f32[32,16,128]{2,1,0:T(8,128)}), f32[32,16,128]{2,1,0:T(8,128)S(1)}, u32[]{:S(2)}, u32[]{:S(2)}) async-start(f32[32,16,128]{2,1,0:T(8,128)} %get-tuple-element.12), calls=%async_computation | async-start | bytes 524288 | tf_op jit(solution)/shard_map/all_to_all | solution.py:226
  12.8 3.3 %collective-permute-start = (bf16[2,256,512]{2,1,0:T(8,128)(2,1)}, bf16[2,256,512]{2,1,0:T(8,128)(2,1)S(1)}, u32[]{:S(2)}, u32[]{:S(2)}) collective-permute-start(bf16[2,256,512]{2,1,0:T(8,128)(2,1)} %get-tuple-element.13), channel_id=1, source_target_pairs={{0,1},{1,2},{2,3},{3,4},{4,5},{5,6},{6,7},{7,8},{8,9},{9,10},{10,1... | collective-permute-start | bytes 1572872 | tf_op jit(solution)/shard_map/ppermute | solution.py:217
  16.1 1.3 %collective-permute-start.1 = (bf16[2,256,512]{2,1,0:T(8,128)(2,1)}, bf16[2,256,512]{2,1,0:T(8,128)(2,1)S(1)}, u32[]{:S(2)}, u32[]{:S(2)}) collective-permute-start(bf16[2,256,512]{2,1,0:T(8,128)(2,1)} %get-tuple-element.13), channel_id=1, source_target_pairs={{1,0},{2,1},{3,2},{4,3},{5,4},{6,5},{7,6},{8,7},{9,8},{10,9},{11,1... | collective-permute-start | bytes 1572872 | tf_op jit(solution)/shard_map/ppermute | solution.py:217
  17.4 4.7 %collective-permute-start.2 = (bf16[2,512,256]{2,1,0:T(8,128)(2,1)}, bf16[2,512,256]{2,1,0:T(8,128)(2,1)S(1)}, u32[]{:S(2)}, u32[]{:S(2)}) collective-permute-start(bf16[2,512,256]{2,1,0:T(8,128)(2,1)} %get-tuple-element.14.w_0), channel_id=1, source_target_pairs={{0,256},{128,384},{256,0},{384,128},{1,257},{129,385},{257,1},{385... | collective-permute-start | bytes 1572872 | tf_op jit(solution)/shard_map/ppermute | solution.py:222
  22.1 0.0 all-to-all-done.parts
  22.2 0.7 plane_sum.1.after
  22.9 17.2 %all-to-all-start.1 = ((f32[16,16,128]{2,1,0:T(8,128)}), f32[16,16,128]{2,1,0:T(8,128)S(1)}, u32[]{:S(2)}, u32[]{:S(2)}) async-start(f32[16,16,128]{2,1,0:T(8,128)} %plane_sum.1.after), calls=%async_computation.1 | async-start | bytes 262144 | tf_op jit(solution)/shard_map/all_to_all | solution.py:226
  40.0 0.0 copy-start
  40.1 2.2 %collective-permute-start.5 = (bf16[2,512,256]{2,1,0:T(8,128)(2,1)}, bf16[2,512,256]{2,1,0:T(8,128)(2,1)S(1)}, u32[]{:S(2)}, u32[]{:S(2)}) collective-permute-start(bf16[2,512,256]{2,1,0:T(8,128)(2,1)} %get-tuple-element.14.w_0), channel_id=1, source_target_pairs={{0,128},{128,256},{256,384},{384,0},{1,129},{129,257},{257,385},{3... | collective-permute-start | bytes 1572872 | tf_op jit(solution)/shard_map/ppermute | solution.py:222
  42.3 4.3 %collective-permute-start.6 = (bf16[2,512,256]{2,1,0:T(8,128)(2,1)}, bf16[2,512,256]{2,1,0:T(8,128)(2,1)S(1)}, u32[]{:S(2)}, u32[]{:S(2)}) collective-permute-start(bf16[2,512,256]{2,1,0:T(8,128)(2,1)} %get-tuple-element.14.w_0), channel_id=1, source_target_pairs={{0,384},{128,0},{256,128},{384,256},{1,385},{129,1},{257,129},{385... | collective-permute-start | bytes 1572872 | tf_op jit(solution)/shard_map/ppermute | solution.py:222
  46.6 0.0 collective-permute-done.1.right.kv_p1
  46.6 1.3 %collective-permute-start.3 = (bf16[2,256,512]{2,1,0:T(8,128)(2,1)S(1)}, bf16[2,256,512]{2,1,0:T(8,128)(2,1)S(1)}, u32[]{:S(2)}, u32[]{:S(2)}) collective-permute-start(bf16[2,256,512]{2,1,0:T(8,128)(2,1)S(1)} %collective-permute-done.1.right.kv_p1), channel_id=1, source_target_pairs={{1,0},{2,1},{3,2},{4,3},{5,4},{6,5},{7,6},{8,7},{9,8},{10,9},{11,1... | collective-permute-start | bytes 1572872 | tf_op jit(solution)/shard_map/ppermute | solution.py:217
  47.9 0.0 collective-permute-done.left.kv_m1
  47.9 4.8 %collective-permute-start.4 = (bf16[2,256,512]{2,1,0:T(8,128)(2,1)S(1)}, bf16[2,256,512]{2,1,0:T(8,128)(2,1)}, u32[]{:S(2)}, u32[]{:S(2)}) collective-permute-start(bf16[2,256,512]{2,1,0:T(8,128)(2,1)S(1)} %collective-permute-done.left.kv_m1), channel_id=1, source_target_pairs={{0,1},{1,2},{2,3},{3,4},{4,5},{5,6},{6,7},{7,8},{8,9},{9,10},{10,1... | collective-permute-start | bytes 1572872 | tf_op jit(solution)/shard_map/ppermute | solution.py:217
  52.7 0.6 gate.1.after
  53.3 0.0 collective-permute-done.2.after_1.w_3
  53.3 0.0 all-to-all-done.1.parts
  53.3 0.7 pooled.1.after
  54.0 6.1 %all-to-all-start.2 = ((bf16[32,16,128]{2,1,0:T(8,128)(2,1)}), bf16[32,16,128]{2,1,0:T(8,128)(2,1)S(1)}, u32[]{:S(2)}, u32[]{:S(2)}) async-start(bf16[32,16,128]{2,1,0:T(8,128)(2,1)} %pooled.1.after), calls=%async_computation.2 | async-start | bytes 262144 | tf_op jit(solution)/shard_map/all_to_all | solution.py:226
  60.1 0.0 collective-permute-done.5.w_1
  60.1 0.0 collective-permute-done.6.w_2
  60.1 0.0 copy-done
  60.1 2.6 %stack.1 = (bf16[4,2,512,256]{3,2,1,0:T(8,128)(2,1)}, f32[2,1344]{1,0:T(2,128)}) custom-call(s32[2,6]{1,0:T(2,128)S(1)} %copy-done, bf16[32,16,128]{2,1,0:T(8,128)(2,1)} %pooled.1.after, bf16[2,512,256]{2,1,0:T(8,128)(2,1)} %get-tuple-element.14.w_0, bf16[2,512,256]{2,1,0:T(8,128)(2,1)S(1)} %collective-permute-done.5.w_1, ...), custom_call_target="tpu_custom_call" | custom-call | tf_op jit(solution)/shard_map/stack/pallas_call | solution.py:331
  62.7 2.2 %collective-permute-start.7 = (bf16[4,2,512,256]{3,2,1,0:T(8,128)(2,1)}, bf16[4,2,512,256]{3,2,1,0:T(8,128)(2,1)}, u32[]{:S(2)}, u32[]{:S(2)}) collective-permute-start(bf16[4,2,512,256]{3,2,1,0:T(8,128)(2,1)} %get-tuple-element.16.w_near_in), channel_id=1, source_target_pairs={{0,64},{64,0},{1,65},{65,1},{2,66},{66,2},{3,67},{67,3},{4,68},{68... | collective-permute-start | bytes 6291464 | tf_op jit(solution)/shard_map/ppermute | solution.py:222
  64.9 2.8 %all-to-all-done.2.virtual_kv = bf16[32,16,128]{2,1,0:T(8,128)(2,1)S(1)} async-done(((bf16[32,16,128]{2,1,0:T(8,128)(2,1)}), bf16[32,16,128]{2,1,0:T(8,128)(2,1)S(1)}, u32[]{:S(2)}, u32[]{:S(2)}) %all-to-all-start.2) | async-done | bytes 131104 | tf_op jit(solution)/shard_map/all_to_all | solution.py:226
  67.8 0.0 collective-permute-done.3.kv_p2
  67.8 0.0 collective-permute-done.4.kv_m2
  67.8 8.7 %layer.1 = (f32[256,512]{1,0:T(8,128)S(1)}, bf16[256,512]{1,0:T(8,128)(2,1)S(1)}) custom-call(bf16[32,16,128]{2,1,0:T(8,128)(2,1)S(1)} %all-to-all-done.2.virtual_kv, bf16[2,256,512]{2,1,0:T(8,128)(2,1)S(1)} %collective-permute-done.left.kv_m1, bf16[2,256,512]{2,1,0:T(8,128)(2,1)S(1)} %collective-permute-done.1.right.kv_p1, ...), custom_call_target="tpu_custom_call" | custom-call | flops 399999991808 | bytes 6000000 | tf_op jit(solution)/shard_map/layer/pallas_call | solution.py:344
  76.5 0.0 collective-permute-done.7.weights_in
  76.5 3.2 %finish.1 = bf16[256,512]{1,0:T(8,128)(2,1)} custom-call(f32[256,512]{1,0:T(8,128)S(1)} %get-tuple-element.17.partial, bf16[256,512]{1,0:T(8,128)(2,1)S(1)} %get-tuple-element.18.normed, bf16[4,2,512,256]{3,2,1,0:T(8,128)(2,1)} %collective-permute-done.7.weights_in), custom_call_target="tpu_custom_call" | custom-call | tf_op jit(solution)/shard_map/finish/pallas_call | solution.py:381
Async XLA Ops:
  2.4 19.8 %all-to-all-start = ((f32[32,16,128]{2,1,0:T(8,128)}), f32[32,16,128]{2,1,0:T(8,128)S(1)}, u32[]{:S(2)}, u32[]{:S(2)}) async-start(f32[32,16,128]{2,1,0:T(8,128)} %get-tuple-element.12), calls=%async_computation | async-start | bytes 524288 | tf_op jit(solution)/shard_map/all_to_all | solution.py:226
  12.8 35.1 %collective-permute-start = (bf16[2,256,512]{2,1,0:T(8,128)(2,1)}, bf16[2,256,512]{2,1,0:T(8,128)(2,1)S(1)}, u32[]{:S(2)}, u32[]{:S(2)}) collective-permute-start(bf16[2,256,512]{2,1,0:T(8,128)(2,1)} %get-tuple-element.13), channel_id=1, source_target_pairs={{0,1},{1,2},{2,3},{3,4},{4,5},{5,6},{6,7},{7,8},{8,9},{9,10},{10,1... | collective-permute-start | bytes 1572872 | tf_op jit(solution)/shard_map/ppermute | solution.py:217
  16.1 30.4 %collective-permute-start.1 = (bf16[2,256,512]{2,1,0:T(8,128)(2,1)}, bf16[2,256,512]{2,1,0:T(8,128)(2,1)S(1)}, u32[]{:S(2)}, u32[]{:S(2)}) collective-permute-start(bf16[2,256,512]{2,1,0:T(8,128)(2,1)} %get-tuple-element.13), channel_id=1, source_target_pairs={{1,0},{2,1},{3,2},{4,3},{5,4},{6,5},{7,6},{8,7},{9,8},{10,9},{11,1... | collective-permute-start | bytes 1572872 | tf_op jit(solution)/shard_map/ppermute | solution.py:217
  17.4 35.8 %collective-permute-start.2 = (bf16[2,512,256]{2,1,0:T(8,128)(2,1)}, bf16[2,512,256]{2,1,0:T(8,128)(2,1)S(1)}, u32[]{:S(2)}, u32[]{:S(2)}) collective-permute-start(bf16[2,512,256]{2,1,0:T(8,128)(2,1)} %get-tuple-element.14.w_0), channel_id=1, source_target_pairs={{0,256},{128,384},{256,0},{384,128},{1,257},{129,385},{257,1},{385... | collective-permute-start | bytes 1572872 | tf_op jit(solution)/shard_map/ppermute | solution.py:222
  22.9 30.4 %all-to-all-start.1 = ((f32[16,16,128]{2,1,0:T(8,128)}), f32[16,16,128]{2,1,0:T(8,128)S(1)}, u32[]{:S(2)}, u32[]{:S(2)}) async-start(f32[16,16,128]{2,1,0:T(8,128)} %plane_sum.1.after), calls=%async_computation.1 | async-start | bytes 262144 | tf_op jit(solution)/shard_map/all_to_all | solution.py:226
  40.0 20.1 %copy-start = (s32[2,6]{1,0:T(2,128)S(1)}, s32[2,6]{1,0:T(2,128)}, u32[]{:S(2)}) copy-start(s32[2,6]{1,0:T(2,128)} %tile_lists.1) | copy-start | bytes 148
  40.1 20.1 %collective-permute-start.5 = (bf16[2,512,256]{2,1,0:T(8,128)(2,1)}, bf16[2,512,256]{2,1,0:T(8,128)(2,1)S(1)}, u32[]{:S(2)}, u32[]{:S(2)}) collective-permute-start(bf16[2,512,256]{2,1,0:T(8,128)(2,1)} %get-tuple-element.14.w_0), channel_id=1, source_target_pairs={{0,128},{128,256},{256,384},{384,0},{1,129},{129,257},{257,385},{3... | collective-permute-start | bytes 1572872 | tf_op jit(solution)/shard_map/ppermute | solution.py:222
  42.3 17.8 %collective-permute-start.6 = (bf16[2,512,256]{2,1,0:T(8,128)(2,1)}, bf16[2,512,256]{2,1,0:T(8,128)(2,1)S(1)}, u32[]{:S(2)}, u32[]{:S(2)}) collective-permute-start(bf16[2,512,256]{2,1,0:T(8,128)(2,1)} %get-tuple-element.14.w_0), channel_id=1, source_target_pairs={{0,384},{128,0},{256,128},{384,256},{1,385},{129,1},{257,129},{385... | collective-permute-start | bytes 1572872 | tf_op jit(solution)/shard_map/ppermute | solution.py:222
  46.6 21.2 %collective-permute-start.3 = (bf16[2,256,512]{2,1,0:T(8,128)(2,1)S(1)}, bf16[2,256,512]{2,1,0:T(8,128)(2,1)S(1)}, u32[]{:S(2)}, u32[]{:S(2)}) collective-permute-start(bf16[2,256,512]{2,1,0:T(8,128)(2,1)S(1)} %collective-permute-done.1.right.kv_p1), channel_id=1, source_target_pairs={{1,0},{2,1},{3,2},{4,3},{5,4},{6,5},{7,6},{8,7},{9,8},{10,9},{11,1... | collective-permute-start | bytes 1572872 | tf_op jit(solution)/shard_map/ppermute | solution.py:217
  47.9 19.9 %collective-permute-start.4 = (bf16[2,256,512]{2,1,0:T(8,128)(2,1)S(1)}, bf16[2,256,512]{2,1,0:T(8,128)(2,1)}, u32[]{:S(2)}, u32[]{:S(2)}) collective-permute-start(bf16[2,256,512]{2,1,0:T(8,128)(2,1)S(1)} %collective-permute-done.left.kv_m1), channel_id=1, source_target_pairs={{0,1},{1,2},{2,3},{3,4},{4,5},{5,6},{6,7},{7,8},{8,9},{9,10},{10,1... | collective-permute-start | bytes 1572872 | tf_op jit(solution)/shard_map/ppermute | solution.py:217
  54.0 13.8 %all-to-all-start.2 = ((bf16[32,16,128]{2,1,0:T(8,128)(2,1)}), bf16[32,16,128]{2,1,0:T(8,128)(2,1)S(1)}, u32[]{:S(2)}, u32[]{:S(2)}) async-start(bf16[32,16,128]{2,1,0:T(8,128)(2,1)} %pooled.1.after), calls=%async_computation.2 | async-start | bytes 262144 | tf_op jit(solution)/shard_map/all_to_all | solution.py:226
  62.7 13.8 %collective-permute-start.7 = (bf16[4,2,512,256]{3,2,1,0:T(8,128)(2,1)}, bf16[4,2,512,256]{3,2,1,0:T(8,128)(2,1)}, u32[]{:S(2)}, u32[]{:S(2)}) collective-permute-start(bf16[4,2,512,256]{3,2,1,0:T(8,128)(2,1)} %get-tuple-element.16.w_near_in), channel_id=1, source_target_pairs={{0,64},{64,0},{1,65},{65,1},{2,66},{66,2},{3,67},{67,3},{4,68},{68... | collective-permute-start | bytes 6291464 | tf_op jit(solution)/shard_map/ppermute | solution.py:222

commit v6 on v4

--- a/solution.py
+++ b/solution.py
@@ -64,7 +64,7 @@
     total[...] = jnp.broadcast_to(jnp.sum(parts[...], axis=0, keepdims=True), total.shape)
 
 
-def pooled_kernel(scale, parts, after, after_1, after_2, pooled):
+def pooled_kernel(scale, parts, after, after_1, pooled):
     mean = (jnp.sum(parts[...], axis=0, keepdims=True) * scale).astype(BF16)
     pooled[...] = jnp.broadcast_to(mean, pooled.shape)
 
@@ -72,13 +72,6 @@
 def stack_kernel(after, w_0, w_1, w_2, w_3, stacked):
     for i, piece in enumerate((w_0, w_1, w_2, w_3)):
         stacked[i] = piece[...]
-
-
-def named(tile_lists, block, wanted):
-    found = tile_lists[block, 0] == wanted
-    for slot in range(1, TMAX):
-        found = jnp.logical_or(found, tile_lists[block, slot] == wanted)
-    return jnp.logical_and(found, wanted >= 0)
 
 
 def gate_kernel(after, left, right, token):
@@ -93,8 +86,8 @@
     values,
     kv_m1,
     kv_p1,
+    kv_p2,
     kv_m2,
-    kv_p2,
     out_weight_in,
     node_feats_in,
     norm_gain_in,
@@ -117,10 +110,10 @@
         (queries_in, queries),
         (keys, window.at[0, pl.ds(middle, rows)]),
         (values, window.at[1, pl.ds(middle, rows)]),
+        (kv_m2, window.at[:, pl.ds(0, rows)]),
+        (kv_p2, window.at[:, pl.ds(4 * rows, rows)]),
         (kv_m1, window.at[:, pl.ds(rows, rows)]),
         (kv_p1, window.at[:, pl.ds(3 * rows, rows)]),
-        (kv_m2, window.at[:, pl.ds(0, rows)]),
-        (kv_p2, window.at[:, pl.ds(4 * rows, rows)]),
         (out_weight_in, out_weight),
         (node_feats_in, node_feats),
         (norm_gain_in, norm_gain),
@@ -137,46 +130,53 @@
     lane_parts = feat_width // LANES
     rows_parts = VIRTUAL // virtual_kv.shape[1]
     blocks = rows // BLOCK
-    places = (2 * REACH + 1) * blocks
     low = lax.broadcasted_iota(jnp.int32, (BLOCK, LANES), 1) < head_dim
-    ones = jnp.ones((places * BLOCK + VIRTUAL, LANES), BF16)
     first_block = tile_lists[0, 0] - REACH * blocks
-    bias = [
-        jnp.concatenate(
-            [
-                jnp.full(
-                    (1, BLOCK),
-                    jnp.where(named(tile_lists, block, first_block + place), 0.0, -jnp.inf),
-                    F32,
-                )
-                for place in range(places)
-            ]
-            + [jnp.zeros((1, VIRTUAL), F32)],
-            axis=1,
-        )
-        for block in range(blocks)
-    ]
+    starts = []
+    shown = []
+    for block in range(blocks):
+        own = tile_lists[block, 0]
+        for slot in range(TMAX):
+            tile = tile_lists[block, slot]
+            there = tile >= 0
+            place = jnp.where(there, tile, own) - first_block
+            starts.append(pl.multiple_of(place * BLOCK, BLOCK))
+            shown.append(jnp.full((BLOCK, LANES), jnp.where(there, 1.0, 0.0), F32).astype(BF16))
     for copy in copies[:7]:
         copy.wait()
     for part in range(lane_parts):
         lanes = slice(part * LANES, (part + 1) * LANES)
         pooled = [virtual_kv[r * lane_parts + part] for r in range(2 * rows_parts)]
-        all_keys = jnp.concatenate([window[0, :, lanes]] + pooled[:rows_parts], axis=0)
-        all_values = jnp.concatenate([window[1, :, lanes]] + pooled[rows_parts:], axis=0)
-        right = jnp.concatenate([all_values, ones], axis=1)
         for block in range(blocks):
+            slots = range(block * TMAX, (block + 1) * TMAX)
             here = slice(block * BLOCK, (block + 1) * BLOCK)
             pair = queries[here, lanes]
             zero = jnp.zeros_like(pair)
             both = jnp.concatenate(
                 [jnp.where(low, pair, zero), jnp.where(low, zero, pair)], axis=0
             )
+            all_keys = jnp.concatenate(
+                [window[0, pl.ds(starts[s], BLOCK), lanes] for s in slots] + pooled[:rows_parts],
+                axis=0,
+            )
+            right = jnp.concatenate(
+                [
+                    jnp.concatenate(
+                        [window[1, pl.ds(starts[s], BLOCK), lanes] * shown[s], shown[s]], axis=1
+                    )
+                    for s in slots
+                ]
+                + [
+                    jnp.concatenate([piece, jnp.ones_like(piece)], axis=1)
+                    for piece in pooled[rows_parts:]
+                ],
+                axis=0,
+            )
             scores = lax.dot_general(
                 both, all_keys, (((1,), (1,)), ((), ())), preferred_element_type=F32
             )
-            scores = scores * scale + bias[block]
-            row_max = jnp.max(scores, axis=-1, keepdims=True)
-            exponent = jnp.exp2(scores - row_max).astype(BF16)
+            row_max = jnp.max(scores, axis=-1, keepdims=True) * scale
+            exponent = jnp.exp2(scores * scale - row_max).astype(BF16)
             summed = jnp.dot(exponent, right, preferred_element_type=F32)
             result = summed[:, :LANES] / summed[:, LANES:]
             attended[here, lanes] = jnp.where(low, result[:BLOCK], result[BLOCK:]).astype(BF16)
@@ -195,15 +195,14 @@
 
 
 def hidden_sum(normed, weights, copies):
-    total = 0.0
-    for shard, copy in enumerate(copies):
+    for copy in copies:
         copy.wait()
-        hidden = jnp.dot(normed, weights[shard, 0], preferred_element_type=F32)
-        hidden = jnp.maximum(hidden, 0.0).astype(BF16)
-        total = total + lax.dot_general(
-            hidden, weights[shard, 1], (((1,), (1,)), ((), ())), preferred_element_type=F32
-        )
-    return total
+    shards = range(weights.shape[0])
+    up = jnp.concatenate([weights[shard, 0] for shard in shards], axis=1)
+    down = jnp.concatenate([weights[shard, 1] for shard in shards], axis=1)
+    hidden = jnp.dot(normed, up, preferred_element_type=F32)
+    hidden = jnp.maximum(hidden, 0.0).astype(BF16)
+    return lax.dot_general(hidden, down, (((1,), (1,)), ((), ())), preferred_element_type=F32)
 
 
 def finish_kernel(partial, normed, weights_in, layer_out, weights, sem):
@@ -272,8 +271,8 @@
         pool_kernel,
         out_shape=(
             shape((plane, per_part, LANES), F32),
-            pltpu.HBM(kv_shape, BF16),
-            pltpu.HBM(w_shape, BF16),
+            VMEM(kv_shape, BF16),
+            VMEM(w_shape, BF16),
         ),
         in_specs=[anywhere] * 5,
         out_specs=(in_vmem,) * 3,
@@ -325,11 +324,11 @@
     pooled = pl.pallas_call(
         functools.partial(pooled_kernel, pool_scale),
         out_shape=shape((plane, per_part, LANES), BF16),
-        in_specs=[in_vmem] + [anywhere] * 3,
+        in_specs=[in_vmem] + [anywhere] * 2,
         out_specs=in_vmem,
         compiler_params=grant(2),
         name="pooled",
-    )(parts, hbm(token), w_1, w_2)
+    )(parts, hbm(token), w_3)
 
     virtual_kv = exchanged(pooled, PLANE)
     w_near = pl.pallas_call(
@@ -339,7 +338,7 @@
         out_specs=in_vmem,
         compiler_params=grant(6),
         name="stack",
-    )(pooled, hbm(w_0), w_1, w_2, w_3)
+    )(pooled, vmem(w_0), w_1, w_2, w_3)
     w_far = around(w_near, "c", 1)
 
     partial, normed = pl.pallas_call(
@@ -357,7 +356,7 @@
             VMEM((node_rows, feat_width), BF16),
             dma(10 + near),
         ],
-        compiler_params=grant(20),
+        compiler_params=grant(12),
         cost_estimate=pl.CostEstimate(
             flops=400_000_000_000, bytes_accessed=6_000_000, transcendentals=2_000_000
         ),
@@ -370,8 +369,8 @@
         hbm(values),
         kv_m1,
         kv_p1,
+        kv_p2,
         kv_m2,
-        kv_p2,
         hbm(out_weight),
         hbm(node_feats),
         hbm(norm_gain.reshape(1, feat_width)),

time: 83.8 us -> 78.2 us (0.933)
  Pallas kernels: 19.1 us -> 15.7 us
  starting transfers between devices: 59.4 us -> 57.9 us
    all_to_all x3, starting transfers between devices: 35.7 us -> 33.7 us  [exchanged(): return lax.all_to_all(parts, axes, 0, 0, tiled=True)]
    pallas_call x1, Pallas kernels: 9.01 us -> 7.09 us  [local(): pl.pallas_call(layer_kernel, out_shape=(VMEM((node_rows, feat_width), F32...]
    ppermute x4, starting transfers between devices: 12.3 us -> 13.4 us  [around(): lax.ppermute(shard, axis, [(i, (i + by) % length) for i in range(length)])]
    pallas_call x1, Pallas kernels: 2.51 us -> 1.47 us  [local(): pl.pallas_call(stack_kernel, out_shape=pltpu.HBM((near, *w_shape), BF16),...]
  transfers between devices with their start and end apart: 11 -> 11, of which waited for: 2 -> 1; matrix products, arithmetic and copies ran while one was open for 0% -> 0% of each run, Pallas kernels for 16% -> 14%
where the time goes in v6:
time: 78.2 us; the launch traced here: 77.7 us
  starting transfers between devices  57.9 us (74%)
  Pallas kernels  15.7 us (20%)
  waiting for transfers between devices  3.96 us (5%)
    all_to_all x3, starting transfers between devices, exchanged(): return lax.all_to_all(parts, axes, 0, 0, tiled=True)  33.7 us
    ppermute x4, starting transfers between devices, around(): lax.ppermute(shard, axis, [(i, (i + by) % length) for i in range(length)])  13.4 us
    ppermute x4, starting transfers between devices, along_dom(): return lax.ppermute(shard, DOM, pairs)  10.7 us
    pallas_call x1, Pallas kernels, local(): pl.pallas_call(layer_kernel, out_shape=(VMEM((node_rows, feat_width), F32...  7.09 us
    all_to_all x3, waiting for transfers between devices, exchanged(): return lax.all_to_all(parts, axes, 0, 0, tiled=True)  3.94 us
    pallas_call x1, Pallas kernels, local(): pl.pallas_call(finish_kernel, out_shape=shape((node_rows, feat_width), BF...  2.97 us
    pallas_call x1, Pallas kernels, local(): pl.pallas_call(pool_kernel, out_shape=(shape((plane, per_part, LANES), F3...  2.18 us
  transfers between devices with their start and end apart: 11, of which 1 were waited for; matrix products, arithmetic and copies ran while one was open for 0% of the time, Pallas kernels for 14%

profile of v6, /device:TPU:1, one launch (start us, length us, event | category | flops | bytes accessed | tf_op | source)
XLA Modules:
  0.0 77.7 jit_solution(1483985869529569954)
XLA Ops:
  0.0 2.2 %pool.1 = (f32[32,16,128]{2,1,0:T(8,128)}, bf16[2,256,512]{2,1,0:T(8,128)(2,1)}, bf16[2,512,256]{2,1,0:T(8,128)(2,1)S(1)}) custom-call(s32[1,256]{1,0:T(1,128)} %bitcast.2, bf16[256,512]{1,0:T(8,128)(2,1)} %keys.1, bf16[256,512]{1,0:T(8,128)(2,1)} %values.1, bf16[512,256]{1,0:T(8,128)(2,1)} %up_in.1, bf16[512,256]{1,0:T(8,128)(2,1)} %down_in.1), custom_call_target="tpu_custom_call" | custom-call | tf_op jit(solution)/shard_map/pool/pallas_call | solution.py:270
  2.2 10.4 %all-to-all-start = ((f32[32,16,128]{2,1,0:T(8,128)}), f32[32,16,128]{2,1,0:T(8,128)S(1)}, u32[]{:S(2)}, u32[]{:S(2)}) async-start(f32[32,16,128]{2,1,0:T(8,128)} %get-tuple-element.10), calls=%async_computation | async-start | bytes 524288 | tf_op jit(solution)/shard_map/all_to_all | solution.py:230
  12.6 3.3 %collective-permute-start = (bf16[2,256,512]{2,1,0:T(8,128)(2,1)}, bf16[2,256,512]{2,1,0:T(8,128)(2,1)S(1)}, u32[]{:S(2)}, u32[]{:S(2)}) collective-permute-start(bf16[2,256,512]{2,1,0:T(8,128)(2,1)} %get-tuple-element.11), channel_id=1, source_target_pairs={{0,1},{1,2},{2,3},{3,4},{4,5},{5,6},{6,7},{7,8},{8,9},{9,10},{10,1... | collective-permute-start | bytes 1572872 | tf_op jit(solution)/shard_map/ppermute | solution.py:221
  15.9 1.3 %collective-permute-start.1 = (bf16[2,256,512]{2,1,0:T(8,128)(2,1)}, bf16[2,256,512]{2,1,0:T(8,128)(2,1)S(1)}, u32[]{:S(2)}, u32[]{:S(2)}) collective-permute-start(bf16[2,256,512]{2,1,0:T(8,128)(2,1)} %get-tuple-element.11), channel_id=1, source_target_pairs={{1,0},{2,1},{3,2},{4,3},{5,4},{6,5},{7,6},{8,7},{9,8},{10,9},{11,1... | collective-permute-start | bytes 1572872 | tf_op jit(solution)/shard_map/ppermute | solution.py:221
  17.2 4.7 %collective-permute-start.2 = (bf16[2,512,256]{2,1,0:T(8,128)(2,1)S(1)}, bf16[2,512,256]{2,1,0:T(8,128)(2,1)S(1)}, u32[]{:S(2)}, u32[]{:S(2)}) collective-permute-start(bf16[2,512,256]{2,1,0:T(8,128)(2,1)S(1)} %get-tuple-element.12.w_0), channel_id=1, source_target_pairs={{0,256},{128,384},{256,0},{384,128},{1,257},{129,385},{257,1},{385... | collective-permute-start | bytes 1572872 | tf_op jit(solution)/shard_map/ppermute | solution.py:226
  22.0 0.0 all-to-all-done.parts
  22.0 0.7 plane_sum.1.after
  22.7 17.2 %all-to-all-start.1 = ((f32[16,16,128]{2,1,0:T(8,128)}), f32[16,16,128]{2,1,0:T(8,128)S(1)}, u32[]{:S(2)}, u32[]{:S(2)}) async-start(f32[16,16,128]{2,1,0:T(8,128)} %plane_sum.1.after), calls=%async_computation.1 | async-start | bytes 262144 | tf_op jit(solution)/shard_map/all_to_all | solution.py:230
  39.9 2.2 %collective-permute-start.5 = (bf16[2,512,256]{2,1,0:T(8,128)(2,1)S(1)}, bf16[2,512,256]{2,1,0:T(8,128)(2,1)S(1)}, u32[]{:S(2)}, u32[]{:S(2)}) collective-permute-start(bf16[2,512,256]{2,1,0:T(8,128)(2,1)S(1)} %get-tuple-element.12.w_0), channel_id=1, source_target_pairs={{0,128},{128,256},{256,384},{384,0},{1,129},{129,257},{257,385},{3... | collective-permute-start | bytes 1572872 | tf_op jit(solution)/shard_map/ppermute | solution.py:226
  42.1 4.3 %collective-permute-start.6 = (bf16[2,512,256]{2,1,0:T(8,128)(2,1)S(1)}, bf16[2,512,256]{2,1,0:T(8,128)(2,1)S(1)}, u32[]{:S(2)}, u32[]{:S(2)}) collective-permute-start(bf16[2,512,256]{2,1,0:T(8,128)(2,1)S(1)} %get-tuple-element.12.w_0), channel_id=1, source_target_pairs={{0,384},{128,0},{256,128},{384,256},{1,385},{129,1},{257,129},{385... | collective-permute-start | bytes 1572872 | tf_op jit(solution)/shard_map/ppermute | solution.py:226
  46.4 0.0 collective-permute-done.1.right.kv_p1
  46.4 1.3 %collective-permute-start.3 = (bf16[2,256,512]{2,1,0:T(8,128)(2,1)S(1)}, bf16[2,256,512]{2,1,0:T(8,128)(2,1)}, u32[]{:S(2)}, u32[]{:S(2)}) collective-permute-start(bf16[2,256,512]{2,1,0:T(8,128)(2,1)S(1)} %collective-permute-done.1.right.kv_p1), channel_id=1, source_target_pairs={{1,0},{2,1},{3,2},{4,3},{5,4},{6,5},{7,6},{8,7},{9,8},{10,9},{11,1... | collective-permute-start | bytes 1572872 | tf_op jit(solution)/shard_map/ppermute | solution.py:221
  47.7 0.0 collective-permute-done.left.kv_m1
  47.7 4.8 %collective-permute-start.4 = (bf16[2,256,512]{2,1,0:T(8,128)(2,1)S(1)}, bf16[2,256,512]{2,1,0:T(8,128)(2,1)}, u32[]{:S(2)}, u32[]{:S(2)}) collective-permute-start(bf16[2,256,512]{2,1,0:T(8,128)(2,1)S(1)} %collective-permute-done.left.kv_m1), channel_id=1, source_target_pairs={{0,1},{1,2},{2,3},{3,4},{4,5},{5,6},{6,7},{7,8},{8,9},{9,10},{10,1... | collective-permute-start | bytes 1572872 | tf_op jit(solution)/shard_map/ppermute | solution.py:221
  52.5 0.6 gate.1.after
  53.1 0.0 collective-permute-done.2.after_1.w_3
  53.1 0.0 all-to-all-done.1.parts
  53.1 0.7 pooled.1.after
  53.8 6.1 %all-to-all-start.2 = ((bf16[32,16,128]{2,1,0:T(8,128)(2,1)}), bf16[32,16,128]{2,1,0:T(8,128)(2,1)S(1)}, u32[]{:S(2)}, u32[]{:S(2)}) async-start(bf16[32,16,128]{2,1,0:T(8,128)(2,1)} %pooled.1.after), calls=%async_computation.2 | async-start | bytes 262144 | tf_op jit(solution)/shard_map/all_to_all | solution.py:230
  59.9 0.0 copy-start
  59.9 0.0 collective-permute-done.5.w_1
  59.9 0.0 collective-permute-done.6.w_2
  59.9 1.5 %stack.1.w_near_in = bf16[4,2,512,256]{3,2,1,0:T(8,128)(2,1)} custom-call(bf16[32,16,128]{2,1,0:T(8,128)(2,1)} %pooled.1.after, bf16[2,512,256]{2,1,0:T(8,128)(2,1)S(1)} %get-tuple-element.12.w_0, bf16[2,512,256]{2,1,0:T(8,128)(2,1)S(1)} %collective-permute-done.5.w_1, bf16[2,512,256]{2,1,0:T(8,128)(2,1)S(1)} %collective-permute-done.6.w_2, ...), custom_call_target="tpu_custom_call" | custom-call | tf_op jit(solution)/shard_map/stack/pallas_call | solution.py:334
  61.4 2.2 %collective-permute-start.7 = (bf16[4,2,512,256]{3,2,1,0:T(8,128)(2,1)}, bf16[4,2,512,256]{3,2,1,0:T(8,128)(2,1)}, u32[]{:S(2)}, u32[]{:S(2)}) collective-permute-start(bf16[4,2,512,256]{3,2,1,0:T(8,128)(2,1)} %stack.1.w_near_in), channel_id=1, source_target_pairs={{0,64},{64,0},{1,65},{65,1},{2,66},{66,2},{3,67},{67,3},{4,68},{68... | collective-permute-start | bytes 6291464 | tf_op jit(solution)/shard_map/ppermute | solution.py:226
  63.6 3.9 %all-to-all-done.2.virtual_kv = bf16[32,16,128]{2,1,0:T(8,128)(2,1)S(1)} async-done(((bf16[32,16,128]{2,1,0:T(8,128)(2,1)}), bf16[32,16,128]{2,1,0:T(8,128)(2,1)S(1)}, u32[]{:S(2)}, u32[]{:S(2)}) %all-to-all-start.2) | async-done | bytes 131104 | tf_op jit(solution)/shard_map/all_to_all | solution.py:230
  67.6 0.0 collective-permute-done.3.kv_p2
  67.6 0.0 collective-permute-done.4.kv_m2
  67.6 0.0 copy-done
  67.6 7.1 %layer.1 = (f32[256,512]{1,0:T(8,128)S(1)}, bf16[256,512]{1,0:T(8,128)(2,1)S(1)}) custom-call(s32[2,6]{1,0:T(2,128)S(1)} %copy-done, bf16[32,16,128]{2,1,0:T(8,128)(2,1)S(1)} %all-to-all-done.2.virtual_kv, bf16[256,512]{1,0:T(8,128)(2,1)} %queries_in.1, bf16[256,512]{1,0:T(8,128)(2,1)} %keys.1, bf16[256,512]{1,0:T(8,128)(2,1)} %values.1, ...), custom_call_target="tpu_custom_call" | custom-call | flops 399999991808 | bytes 6000000 | tf_op jit(solution)/shard_map/layer/pallas_call | solution.py:344
  74.7 0.0 collective-permute-done.7.weights_in
  74.7 3.0 %finish.1 = bf16[256,512]{1,0:T(8,128)(2,1)} custom-call(f32[256,512]{1,0:T(8,128)S(1)} %get-tuple-element.13.partial, bf16[256,512]{1,0:T(8,128)(2,1)S(1)} %get-tuple-element.14.normed, bf16[4,2,512,256]{3,2,1,0:T(8,128)(2,1)} %collective-permute-done.7.weights_in), custom_call_target="tpu_custom_call" | custom-call | tf_op jit(solution)/shard_map/finish/pallas_call | solution.py:379
Async XLA Ops:
  2.2 19.8 %all-to-all-start = ((f32[32,16,128]{2,1,0:T(8,128)}), f32[32,16,128]{2,1,0:T(8,128)S(1)}, u32[]{:S(2)}, u32[]{:S(2)}) async-start(f32[32,16,128]{2,1,0:T(8,128)} %get-tuple-element.10), calls=%async_computation | async-start | bytes 524288 | tf_op jit(solution)/shard_map/all_to_all | solution.py:230
  12.6 35.1 %collective-permute-start = (bf16[2,256,512]{2,1,0:T(8,128)(2,1)}, bf16[2,256,512]{2,1,0:T(8,128)(2,1)S(1)}, u32[]{:S(2)}, u32[]{:S(2)}) collective-permute-start(bf16[2,256,512]{2,1,0:T(8,128)(2,1)} %get-tuple-element.11), channel_id=1, source_target_pairs={{0,1},{1,2},{2,3},{3,4},{4,5},{5,6},{6,7},{7,8},{8,9},{9,10},{10,1... | collective-permute-start | bytes 1572872 | tf_op jit(solution)/shard_map/ppermute | solution.py:221
  15.9 30.4 %collective-permute-start.1 = (bf16[2,256,512]{2,1,0:T(8,128)(2,1)}, bf16[2,256,512]{2,1,0:T(8,128)(2,1)S(1)}, u32[]{:S(2)}, u32[]{:S(2)}) collective-permute-start(bf16[2,256,512]{2,1,0:T(8,128)(2,1)} %get-tuple-element.11), channel_id=1, source_target_pairs={{1,0},{2,1},{3,2},{4,3},{5,4},{6,5},{7,6},{8,7},{9,8},{10,9},{11,1... | collective-permute-start | bytes 1572872 | tf_op jit(solution)/shard_map/ppermute | solution.py:221
  17.2 35.8 %collective-permute-start.2 = (bf16[2,512,256]{2,1,0:T(8,128)(2,1)S(1)}, bf16[2,512,256]{2,1,0:T(8,128)(2,1)S(1)}, u32[]{:S(2)}, u32[]{:S(2)}) collective-permute-start(bf16[2,512,256]{2,1,0:T(8,128)(2,1)S(1)} %get-tuple-element.12.w_0), channel_id=1, source_target_pairs={{0,256},{128,384},{256,0},{384,128},{1,257},{129,385},{257,1},{385... | collective-permute-start | bytes 1572872 | tf_op jit(solution)/shard_map/ppermute | solution.py:226
  22.7 30.4 %all-to-all-start.1 = ((f32[16,16,128]{2,1,0:T(8,128)}), f32[16,16,128]{2,1,0:T(8,128)S(1)}, u32[]{:S(2)}, u32[]{:S(2)}) async-start(f32[16,16,128]{2,1,0:T(8,128)} %plane_sum.1.after), calls=%async_computation.1 | async-start | bytes 262144 | tf_op jit(solution)/shard_map/all_to_all | solution.py:230
  39.9 20.1 %collective-permute-start.5 = (bf16[2,512,256]{2,1,0:T(8,128)(2,1)S(1)}, bf16[2,512,256]{2,1,0:T(8,128)(2,1)S(1)}, u32[]{:S(2)}, u32[]{:S(2)}) collective-permute-start(bf16[2,512,256]{2,1,0:T(8,128)(2,1)S(1)} %get-tuple-element.12.w_0), channel_id=1, source_target_pairs={{0,128},{128,256},{256,384},{384,0},{1,129},{129,257},{257,385},{3... | collective-permute-start | bytes 1572872 | tf_op jit(solution)/shard_map/ppermute | solution.py:226
  42.1 17.8 %collective-permute-start.6 = (bf16[2,512,256]{2,1,0:T(8,128)(2,1)S(1)}, bf16[2,512,256]{2,1,0:T(8,128)(2,1)S(1)}, u32[]{:S(2)}, u32[]{:S(2)}) collective-permute-start(bf16[2,512,256]{2,1,0:T(8,128)(2,1)S(1)} %get-tuple-element.12.w_0), channel_id=1, source_target_pairs={{0,384},{128,0},{256,128},{384,256},{1,385},{129,1},{257,129},{385... | collective-permute-start | bytes 1572872 | tf_op jit(solution)/shard_map/ppermute | solution.py:226
  46.4 21.2 %collective-permute-start.3 = (bf16[2,256,512]{2,1,0:T(8,128)(2,1)S(1)}, bf16[2,256,512]{2,1,0:T(8,128)(2,1)}, u32[]{:S(2)}, u32[]{:S(2)}) collective-permute-start(bf16[2,256,512]{2,1,0:T(8,128)(2,1)S(1)} %collective-permute-done.1.right.kv_p1), channel_id=1, source_target_pairs={{1,0},{2,1},{3,2},{4,3},{5,4},{6,5},{7,6},{8,7},{9,8},{10,9},{11,1... | collective-permute-start | bytes 1572872 | tf_op jit(solution)/shard_map/ppermute | solution.py:221
  47.7 19.9 %collective-permute-start.4 = (bf16[2,256,512]{2,1,0:T(8,128)(2,1)S(1)}, bf16[2,256,512]{2,1,0:T(8,128)(2,1)}, u32[]{:S(2)}, u32[]{:S(2)}) collective-permute-start(bf16[2,256,512]{2,1,0:T(8,128)(2,1)S(1)} %collective-permute-done.left.kv_m1), channel_id=1, source_target_pairs={{0,1},{1,2},{2,3},{3,4},{4,5},{5,6},{6,7},{7,8},{8,9},{9,10},{10,1... | collective-permute-start | bytes 1572872 | tf_op jit(solution)/shard_map/ppermute | solution.py:221
  53.8 13.8 %all-to-all-start.2 = ((bf16[32,16,128]{2,1,0:T(8,128)(2,1)}), bf16[32,16,128]{2,1,0:T(8,128)(2,1)S(1)}, u32[]{:S(2)}, u32[]{:S(2)}) async-start(bf16[32,16,128]{2,1,0:T(8,128)(2,1)} %pooled.1.after), calls=%async_computation.2 | async-start | bytes 262144 | tf_op jit(solution)/shard_map/all_to_all | solution.py:230
  59.9 7.7 %copy-start = (s32[2,6]{1,0:T(2,128)S(1)}, s32[2,6]{1,0:T(2,128)}, u32[]{:S(2)}) copy-start(s32[2,6]{1,0:T(2,128)} %tile_lists.1) | copy-start | bytes 148
  61.4 13.3 %collective-permute-start.7 = (bf16[4,2,512,256]{3,2,1,0:T(8,128)(2,1)}, bf16[4,2,512,256]{3,2,1,0:T(8,128)(2,1)}, u32[]{:S(2)}, u32[]{:S(2)}) collective-permute-start(bf16[4,2,512,256]{3,2,1,0:T(8,128)(2,1)} %stack.1.w_near_in), channel_id=1, source_target_pairs={{0,64},{64,0},{1,65},{65,1},{2,66},{66,2},{3,67},{67,3},{4,68},{68... | collective-permute-start | bytes 6291464 | tf_op jit(solution)/shard_map/ppermute | solution.py:226

commit v7 on v6

--- a/solution.py
+++ b/solution.py
@@ -132,39 +132,30 @@
     blocks = rows // BLOCK
     low = lax.broadcasted_iota(jnp.int32, (BLOCK, LANES), 1) < head_dim
     first_block = tile_lists[0, 0] - REACH * blocks
-    starts = []
-    shown = []
-    for block in range(blocks):
-        own = tile_lists[block, 0]
-        for slot in range(TMAX):
-            tile = tile_lists[block, slot]
-            there = tile >= 0
-            place = jnp.where(there, tile, own) - first_block
-            starts.append(pl.multiple_of(place * BLOCK, BLOCK))
-            shown.append(jnp.full((BLOCK, LANES), jnp.where(there, 1.0, 0.0), F32).astype(BF16))
     for copy in copies[:7]:
         copy.wait()
-    for part in range(lane_parts):
-        lanes = slice(part * LANES, (part + 1) * LANES)
-        pooled = [virtual_kv[r * lane_parts + part] for r in range(2 * rows_parts)]
-        for block in range(blocks):
-            slots = range(block * TMAX, (block + 1) * TMAX)
-            here = slice(block * BLOCK, (block + 1) * BLOCK)
+
+    def attend(block, slots, starts, shown):
+        here = slice(block * BLOCK, (block + 1) * BLOCK)
+        for part in range(lane_parts):
+            lanes = slice(part * LANES, (part + 1) * LANES)
+            pooled = [virtual_kv[r * lane_parts + part] for r in range(2 * rows_parts)]
             pair = queries[here, lanes]
             zero = jnp.zeros_like(pair)
             both = jnp.concatenate(
                 [jnp.where(low, pair, zero), jnp.where(low, zero, pair)], axis=0
             )
             all_keys = jnp.concatenate(
-                [window[0, pl.ds(starts[s], BLOCK), lanes] for s in slots] + pooled[:rows_parts],
+                [window[0, pl.ds(start, BLOCK), lanes] for start in starts[:slots]]
+                + pooled[:rows_parts],
                 axis=0,
             )
             right = jnp.concatenate(
                 [
                     jnp.concatenate(
-                        [window[1, pl.ds(starts[s], BLOCK), lanes] * shown[s], shown[s]], axis=1
+                        [window[1, pl.ds(start, BLOCK), lanes] * there, there], axis=1
                     )
-                    for s in slots
+                    for start, there in zip(starts[:slots], shown)
                 ]
                 + [
                     jnp.concatenate([piece, jnp.ones_like(piece)], axis=1)
@@ -181,6 +172,22 @@
             result = summed[:, :LANES] / summed[:, LANES:]
             attended[here, lanes] = jnp.where(low, result[:BLOCK], result[BLOCK:]).astype(BF16)
 
+    for block in range(blocks):
+        own = tile_lists[block, 0]
+        starts = []
+        shown = []
+        for slot in range(TMAX):
+            tile = tile_lists[block, slot]
+            there = tile >= 0
+            place = jnp.where(there, tile, own) - first_block
+            starts.append(pl.multiple_of(place * BLOCK, BLOCK))
+            shown.append(jnp.full((BLOCK, LANES), jnp.where(there, 1.0, 0.0), F32).astype(BF16))
+        for slots in range(2, TMAX + 1, 2):
+            needed = tile_lists[block, slots - 2] >= 0
+            if slots < TMAX:
+                needed = jnp.logical_and(needed, tile_lists[block, slots] < 0)
+            pl.when(needed)(functools.partial(attend, block, slots, starts, shown))
+
     for copy in copies[7:10]:
         copy.wait()
     residual = node_feats[...].astype(F32) + jnp.dot(
@@ -205,14 +212,8 @@
     return lax.dot_general(hidden, down, (((1,), (1,)), ((), ())), preferred_element_type=F32)
 
 
-def finish_kernel(partial, normed, weights_in, layer_out, weights, sem):
-    copies = [
-        pltpu.make_async_copy(weights_in.at[shard], weights.at[shard], sem.at[shard])
-        for shard in range(weights.shape[0])
-    ]
-    for copy in copies:
-        copy.start()
-    layer_out[...] = (partial[...] + hidden_sum(normed[...], weights, copies)).astype(BF16)
+def finish_kernel(partial, normed, weights, layer_out):
+    layer_out[...] = (partial[...] + hidden_sum(normed[...], weights, ())).astype(BF16)
 
 
 def along_dom(shard, by):
@@ -270,7 +271,7 @@
     sums, key_value, w_0 = pl.pallas_call(
         pool_kernel,
         out_shape=(
-            shape((plane, per_part, LANES), F32),
+            VMEM((plane, per_part, LANES), F32),
             VMEM(kv_shape, BF16),
             VMEM(w_shape, BF16),
         ),
@@ -295,7 +296,7 @@
 
     plane_sum = pl.pallas_call(
         plane_sum_kernel,
-        out_shape=shape((depth, per_part, LANES), F32),
+        out_shape=VMEM((depth, per_part, LANES), F32),
         in_specs=[in_vmem],
         out_specs=in_vmem,
         compiler_params=grant(2),
@@ -310,7 +311,7 @@
     kv_p2 = along_dom(kv_p1, -1)
     token = pl.pallas_call(
         gate_kernel,
-        out_shape=pltpu.HBM((8, LANES), F32),
+        out_shape=VMEM((8, LANES), F32),
         in_specs=[anywhere] * 3,
         out_specs=in_vmem,
         compiler_params=grant(2),
@@ -323,12 +324,12 @@
     pool_scale = math.sqrt(VIRTUAL / (node_rows * lax.axis_size(AXES)))
     pooled = pl.pallas_call(
         functools.partial(pooled_kernel, pool_scale),
-        out_shape=shape((plane, per_part, LANES), BF16),
+        out_shape=VMEM((plane, per_part, LANES), BF16),
         in_specs=[in_vmem] + [anywhere] * 2,
         out_specs=in_vmem,
         compiler_params=grant(2),
         name="pooled",
-    )(parts, hbm(token), w_3)
+    )(parts, vmem(token), w_3)
 
     virtual_kv = exchanged(pooled, PLANE)
     w_near = pl.pallas_call(
@@ -379,12 +380,11 @@
     return pl.pallas_call(
         finish_kernel,
         out_shape=shape((node_rows, feat_width), BF16),
-        in_specs=[in_vmem, in_vmem, anywhere],
+        in_specs=[in_vmem] * 3,
         out_specs=in_vmem,
-        scratch_shapes=[VMEM((near, *w_shape), BF16), dma(near)],
-        compiler_params=grant(10),
+        compiler_params=grant(8),
         name="finish",
-    )(vmem(partial), vmem(normed), w_far)
+    )(vmem(partial), vmem(normed), vmem(w_far))
 
 
 def solution(mesh):

time: 78.2 us -> 76.9 us (0.983)
  Pallas kernels: 15.7 us -> 14 us
    pallas_call x1, Pallas kernels: 7.09 us -> 5.97 us  [local(): pl.pallas_call(layer_kernel, out_shape=(VMEM((node_rows, feat_width), F32...]
  transfers between devices with their start and end apart: 11 -> 11, of which waited for: 1 -> 1; matrix products, arithmetic and copies ran while one was open for 0% -> 0% of each run, Pallas kernels for 14% -> 12%
where the time goes in v7:
time: 76.9 us; the launch traced here: 76.4 us
  starting transfers between devices  58.2 us (76%)
  Pallas kernels  14 us (18%)
  waiting for transfers between devices  3.96 us (5%)
    all_to_all x3, starting transfers between devices, exchanged(): return lax.all_to_all(parts, axes, 0, 0, tiled=True)  34.1 us
    ppermute x4, starting transfers between devices, around(): lax.ppermute(shard, axis, [(i, (i + by) % length) for i in range(length)])  13.4 us
    ppermute x4, starting transfers between devices, along_dom(): return lax.ppermute(shard, DOM, pairs)  10.7 us
    pallas_call x1, Pallas kernels, local(): pl.pallas_call(layer_kernel, out_shape=(VMEM((node_rows, feat_width), F32...  5.97 us
    all_to_all x3, waiting for transfers between devices, exchanged(): return lax.all_to_all(parts, axes, 0, 0, tiled=True)  3.94 us
    pallas_call x1, Pallas kernels, local(): pl.pallas_call(finish_kernel, out_shape=shape((node_rows, feat_width), BF...  3.01 us
    pallas_call x1, Pallas kernels, local(): pl.pallas_call(pool_kernel, out_shape=(VMEM((plane, per_part, LANES), F32...  2.18 us
  transfers between devices with their start and end apart: 11, of which 1 were waited for; matrix products, arithmetic and copies ran while one was open for 0% of the time, Pallas kernels for 12%

profile of v7, /device:TPU:1, one launch (start us, length us, event | category | flops | bytes accessed | tf_op | source)
XLA Modules:
  0.0 76.4 jit_solution(13406607687495969221)
XLA Ops:
  0.0 2.2 %pool.1 = (f32[32,16,128]{2,1,0:T(8,128)}, bf16[2,256,512]{2,1,0:T(8,128)(2,1)}, bf16[2,512,256]{2,1,0:T(8,128)(2,1)S(1)}) custom-call(s32[1,256]{1,0:T(1,128)} %bitcast.2, bf16[256,512]{1,0:T(8,128)(2,1)} %keys.1, bf16[256,512]{1,0:T(8,128)(2,1)} %values.1, bf16[512,256]{1,0:T(8,128)(2,1)} %up_in.1, bf16[512,256]{1,0:T(8,128)(2,1)} %down_in.1), custom_call_target="tpu_custom_call" | custom-call | tf_op jit(solution)/shard_map/pool/pallas_call | solution.py:271
  2.2 10.4 %all-to-all-start = ((f32[32,16,128]{2,1,0:T(8,128)}), f32[32,16,128]{2,1,0:T(8,128)S(1)}, u32[]{:S(2)}, u32[]{:S(2)}) async-start(f32[32,16,128]{2,1,0:T(8,128)} %get-tuple-element.10), calls=%async_computation | async-start | bytes 524288 | tf_op jit(solution)/shard_map/all_to_all | solution.py:231
  12.6 3.3 %collective-permute-start = (bf16[2,256,512]{2,1,0:T(8,128)(2,1)}, bf16[2,256,512]{2,1,0:T(8,128)(2,1)S(1)}, u32[]{:S(2)}, u32[]{:S(2)}) collective-permute-start(bf16[2,256,512]{2,1,0:T(8,128)(2,1)} %get-tuple-element.11), channel_id=1, source_target_pairs={{0,1},{1,2},{2,3},{3,4},{4,5},{5,6},{6,7},{7,8},{8,9},{9,10},{10,1... | collective-permute-start | bytes 1572872 | tf_op jit(solution)/shard_map/ppermute | solution.py:222
  15.9 1.3 %collective-permute-start.1 = (bf16[2,256,512]{2,1,0:T(8,128)(2,1)}, bf16[2,256,512]{2,1,0:T(8,128)(2,1)S(1)}, u32[]{:S(2)}, u32[]{:S(2)}) collective-permute-start(bf16[2,256,512]{2,1,0:T(8,128)(2,1)} %get-tuple-element.11), channel_id=1, source_target_pairs={{1,0},{2,1},{3,2},{4,3},{5,4},{6,5},{7,6},{8,7},{9,8},{10,9},{11,1... | collective-permute-start | bytes 1572872 | tf_op jit(solution)/shard_map/ppermute | solution.py:222
  17.2 4.7 %collective-permute-start.2 = (bf16[2,512,256]{2,1,0:T(8,128)(2,1)S(1)}, bf16[2,512,256]{2,1,0:T(8,128)(2,1)S(1)}, u32[]{:S(2)}, u32[]{:S(2)}) collective-permute-start(bf16[2,512,256]{2,1,0:T(8,128)(2,1)S(1)} %get-tuple-element.12.w_0), channel_id=1, source_target_pairs={{0,256},{128,384},{256,0},{384,128},{1,257},{129,385},{257,1},{385... | collective-permute-start | bytes 1572872 | tf_op jit(solution)/shard_map/ppermute | solution.py:227
  22.0 0.0 all-to-all-done.parts
  22.0 0.7 plane_sum.1.after
  22.7 17.2 %all-to-all-start.1 = ((f32[16,16,128]{2,1,0:T(8,128)}), f32[16,16,128]{2,1,0:T(8,128)S(1)}, u32[]{:S(2)}, u32[]{:S(2)}) async-start(f32[16,16,128]{2,1,0:T(8,128)} %plane_sum.1.after), calls=%async_computation.1 | async-start | bytes 262144 | tf_op jit(solution)/shard_map/all_to_all | solution.py:231
  39.9 2.2 %collective-permute-start.5 = (bf16[2,512,256]{2,1,0:T(8,128)(2,1)S(1)}, bf16[2,512,256]{2,1,0:T(8,128)(2,1)S(1)}, u32[]{:S(2)}, u32[]{:S(2)}) collective-permute-start(bf16[2,512,256]{2,1,0:T(8,128)(2,1)S(1)} %get-tuple-element.12.w_0), channel_id=1, source_target_pairs={{0,128},{128,256},{256,384},{384,0},{1,129},{129,257},{257,385},{3... | collective-permute-start | bytes 1572872 | tf_op jit(solution)/shard_map/ppermute | solution.py:227
  42.1 4.3 %collective-permute-start.6 = (bf16[2,512,256]{2,1,0:T(8,128)(2,1)S(1)}, bf16[2,512,256]{2,1,0:T(8,128)(2,1)S(1)}, u32[]{:S(2)}, u32[]{:S(2)}) collective-permute-start(bf16[2,512,256]{2,1,0:T(8,128)(2,1)S(1)} %get-tuple-element.12.w_0), channel_id=1, source_target_pairs={{0,384},{128,0},{256,128},{384,256},{1,385},{129,1},{257,129},{385... | collective-permute-start | bytes 1572872 | tf_op jit(solution)/shard_map/ppermute | solution.py:227
  46.4 0.0 collective-permute-done.1.right.kv_p1
  46.4 1.3 %collective-permute-start.3 = (bf16[2,256,512]{2,1,0:T(8,128)(2,1)S(1)}, bf16[2,256,512]{2,1,0:T(8,128)(2,1)}, u32[]{:S(2)}, u32[]{:S(2)}) collective-permute-start(bf16[2,256,512]{2,1,0:T(8,128)(2,1)S(1)} %collective-permute-done.1.right.kv_p1), channel_id=1, source_target_pairs={{1,0},{2,1},{3,2},{4,3},{5,4},{6,5},{7,6},{8,7},{9,8},{10,9},{11,1... | collective-permute-start | bytes 1572872 | tf_op jit(solution)/shard_map/ppermute | solution.py:222
  47.7 0.0 collective-permute-done.left.kv_m1
  47.7 4.8 %collective-permute-start.4 = (bf16[2,256,512]{2,1,0:T(8,128)(2,1)S(1)}, bf16[2,256,512]{2,1,0:T(8,128)(2,1)}, u32[]{:S(2)}, u32[]{:S(2)}) collective-permute-start(bf16[2,256,512]{2,1,0:T(8,128)(2,1)S(1)} %collective-permute-done.left.kv_m1), channel_id=1, source_target_pairs={{0,1},{1,2},{2,3},{3,4},{4,5},{5,6},{6,7},{7,8},{8,9},{9,10},{10,1... | collective-permute-start | bytes 1572872 | tf_op jit(solution)/shard_map/ppermute | solution.py:222
  52.5 0.0 collective-permute-done.2.after_1.w_3
  52.5 0.0 all-to-all-done.1.parts
  52.5 0.7 pooled.1.after
  53.2 6.5 %all-to-all-start.2 = ((bf16[32,16,128]{2,1,0:T(8,128)(2,1)}), bf16[32,16,128]{2,1,0:T(8,128)(2,1)S(1)}, u32[]{:S(2)}, u32[]{:S(2)}) async-start(bf16[32,16,128]{2,1,0:T(8,128)(2,1)} %pooled.1.after), calls=%async_computation.2 | async-start | bytes 262144 | tf_op jit(solution)/shard_map/all_to_all | solution.py:231
  59.7 0.0 copy-start
  59.7 0.0 collective-permute-done.5.w_1
  59.7 0.0 collective-permute-done.6.w_2
  59.7 1.5 %stack.1.w_near_in = bf16[4,2,512,256]{3,2,1,0:T(8,128)(2,1)} custom-call(bf16[32,16,128]{2,1,0:T(8,128)(2,1)} %pooled.1.after, bf16[2,512,256]{2,1,0:T(8,128)(2,1)S(1)} %get-tuple-element.12.w_0, bf16[2,512,256]{2,1,0:T(8,128)(2,1)S(1)} %collective-permute-done.5.w_1, bf16[2,512,256]{2,1,0:T(8,128)(2,1)S(1)} %collective-permute-done.6.w_2, ...), custom_call_target="tpu_custom_call" | custom-call | tf_op jit(solution)/shard_map/stack/pallas_call | solution.py:335
  61.2 2.2 %collective-permute-start.7 = (bf16[4,2,512,256]{3,2,1,0:T(8,128)(2,1)}, bf16[4,2,512,256]{3,2,1,0:T(8,128)(2,1)}, u32[]{:S(2)}, u32[]{:S(2)}) collective-permute-start(bf16[4,2,512,256]{3,2,1,0:T(8,128)(2,1)} %stack.1.w_near_in), channel_id=1, source_target_pairs={{0,64},{64,0},{1,65},{65,1},{2,66},{66,2},{3,67},{67,3},{4,68},{68... | collective-permute-start | bytes 6291464 | tf_op jit(solution)/shard_map/ppermute | solution.py:227
  63.4 3.9 %all-to-all-done.2.virtual_kv = bf16[32,16,128]{2,1,0:T(8,128)(2,1)S(1)} async-done(((bf16[32,16,128]{2,1,0:T(8,128)(2,1)}), bf16[32,16,128]{2,1,0:T(8,128)(2,1)S(1)}, u32[]{:S(2)}, u32[]{:S(2)}) %all-to-all-start.2) | async-done | bytes 131104 | tf_op jit(solution)/shard_map/all_to_all | solution.py:231
  67.3 0.0 collective-permute-done.3.kv_p2
  67.3 0.0 collective-permute-done.4.kv_m2
  67.4 0.0 copy-done
  67.4 6.0 %layer.1 = (f32[256,512]{1,0:T(8,128)S(1)}, bf16[256,512]{1,0:T(8,128)(2,1)S(1)}) custom-call(s32[2,6]{1,0:T(2,128)S(1)} %copy-done, bf16[32,16,128]{2,1,0:T(8,128)(2,1)S(1)} %all-to-all-done.2.virtual_kv, bf16[256,512]{1,0:T(8,128)(2,1)} %queries_in.1, bf16[256,512]{1,0:T(8,128)(2,1)} %keys.1, bf16[256,512]{1,0:T(8,128)(2,1)} %values.1, ...), custom_call_target="tpu_custom_call" | custom-call | flops 399999991808 | bytes 6000000 | tf_op jit(solution)/shard_map/layer/pallas_call | solution.py:345
  73.3 0.0 collective-permute-done.7.weights
  73.3 3.0 %finish.1 = bf16[256,512]{1,0:T(8,128)(2,1)} custom-call(f32[256,512]{1,0:T(8,128)S(1)} %get-tuple-element.13.partial, bf16[256,512]{1,0:T(8,128)(2,1)S(1)} %get-tuple-element.14.normed, bf16[4,2,512,256]{3,2,1,0:T(8,128)(2,1)} %collective-permute-done.7.weights), custom_call_target="tpu_custom_call" | custom-call | tf_op jit(solution)/shard_map/finish/pallas_call | solution.py:380
  (1 shorter events, 0.0 us)
Async XLA Ops:
  2.2 19.8 %all-to-all-start = ((f32[32,16,128]{2,1,0:T(8,128)}), f32[32,16,128]{2,1,0:T(8,128)S(1)}, u32[]{:S(2)}, u32[]{:S(2)}) async-start(f32[32,16,128]{2,1,0:T(8,128)} %get-tuple-element.10), calls=%async_computation | async-start | bytes 524288 | tf_op jit(solution)/shard_map/all_to_all | solution.py:231
  12.6 35.1 %collective-permute-start = (bf16[2,256,512]{2,1,0:T(8,128)(2,1)}, bf16[2,256,512]{2,1,0:T(8,128)(2,1)S(1)}, u32[]{:S(2)}, u32[]{:S(2)}) collective-permute-start(bf16[2,256,512]{2,1,0:T(8,128)(2,1)} %get-tuple-element.11), channel_id=1, source_target_pairs={{0,1},{1,2},{2,3},{3,4},{4,5},{5,6},{6,7},{7,8},{8,9},{9,10},{10,1... | collective-permute-start | bytes 1572872 | tf_op jit(solution)/shard_map/ppermute | solution.py:222
  15.9 30.4 %collective-permute-start.1 = (bf16[2,256,512]{2,1,0:T(8,128)(2,1)}, bf16[2,256,512]{2,1,0:T(8,128)(2,1)S(1)}, u32[]{:S(2)}, u32[]{:S(2)}) collective-permute-start(bf16[2,256,512]{2,1,0:T(8,128)(2,1)} %get-tuple-element.11), channel_id=1, source_target_pairs={{1,0},{2,1},{3,2},{4,3},{5,4},{6,5},{7,6},{8,7},{9,8},{10,9},{11,1... | collective-permute-start | bytes 1572872 | tf_op jit(solution)/shard_map/ppermute | solution.py:222
  17.2 35.2 %collective-permute-start.2 = (bf16[2,512,256]{2,1,0:T(8,128)(2,1)S(1)}, bf16[2,512,256]{2,1,0:T(8,128)(2,1)S(1)}, u32[]{:S(2)}, u32[]{:S(2)}) collective-permute-start(bf16[2,512,256]{2,1,0:T(8,128)(2,1)S(1)} %get-tuple-element.12.w_0), channel_id=1, source_target_pairs={{0,256},{128,384},{256,0},{384,128},{1,257},{129,385},{257,1},{385... | collective-permute-start | bytes 1572872 | tf_op jit(solution)/shard_map/ppermute | solution.py:227
  22.7 29.8 %all-to-all-start.1 = ((f32[16,16,128]{2,1,0:T(8,128)}), f32[16,16,128]{2,1,0:T(8,128)S(1)}, u32[]{:S(2)}, u32[]{:S(2)}) async-start(f32[16,16,128]{2,1,0:T(8,128)} %plane_sum.1.after), calls=%async_computation.1 | async-start | bytes 262144 | tf_op jit(solution)/shard_map/all_to_all | solution.py:231
  39.9 19.8 %collective-permute-start.5 = (bf16[2,512,256]{2,1,0:T(8,128)(2,1)S(1)}, bf16[2,512,256]{2,1,0:T(8,128)(2,1)S(1)}, u32[]{:S(2)}, u32[]{:S(2)}) collective-permute-start(bf16[2,512,256]{2,1,0:T(8,128)(2,1)S(1)} %get-tuple-element.12.w_0), channel_id=1, source_target_pairs={{0,128},{128,256},{256,384},{384,0},{1,129},{129,257},{257,385},{3... | collective-permute-start | bytes 1572872 | tf_op jit(solution)/shard_map/ppermute | solution.py:227
  42.1 17.6 %collective-permute-start.6 = (bf16[2,512,256]{2,1,0:T(8,128)(2,1)S(1)}, bf16[2,512,256]{2,1,0:T(8,128)(2,1)S(1)}, u32[]{:S(2)}, u32[]{:S(2)}) collective-permute-start(bf16[2,512,256]{2,1,0:T(8,128)(2,1)S(1)} %get-tuple-element.12.w_0), channel_id=1, source_target_pairs={{0,384},{128,0},{256,128},{384,256},{1,385},{129,1},{257,129},{385... | collective-permute-start | bytes 1572872 | tf_op jit(solution)/shard_map/ppermute | solution.py:227
  46.4 21.0 %collective-permute-start.3 = (bf16[2,256,512]{2,1,0:T(8,128)(2,1)S(1)}, bf16[2,256,512]{2,1,0:T(8,128)(2,1)}, u32[]{:S(2)}, u32[]{:S(2)}) collective-permute-start(bf16[2,256,512]{2,1,0:T(8,128)(2,1)S(1)} %collective-permute-done.1.right.kv_p1), channel_id=1, source_target_pairs={{1,0},{2,1},{3,2},{4,3},{5,4},{6,5},{7,6},{8,7},{9,8},{10,9},{11,1... | collective-permute-start | bytes 1572872 | tf_op jit(solution)/shard_map/ppermute | solution.py:222
  47.7 19.7 %collective-permute-start.4 = (bf16[2,256,512]{2,1,0:T(8,128)(2,1)S(1)}, bf16[2,256,512]{2,1,0:T(8,128)(2,1)}, u32[]{:S(2)}, u32[]{:S(2)}) collective-permute-start(bf16[2,256,512]{2,1,0:T(8,128)(2,1)S(1)} %collective-permute-done.left.kv_m1), channel_id=1, source_target_pairs={{0,1},{1,2},{2,3},{3,4},{4,5},{5,6},{6,7},{7,8},{8,9},{9,10},{10,1... | collective-permute-start | bytes 1572872 | tf_op jit(solution)/shard_map/ppermute | solution.py:222
  53.2 14.2 %all-to-all-start.2 = ((bf16[32,16,128]{2,1,0:T(8,128)(2,1)}), bf16[32,16,128]{2,1,0:T(8,128)(2,1)S(1)}, u32[]{:S(2)}, u32[]{:S(2)}) async-start(bf16[32,16,128]{2,1,0:T(8,128)(2,1)} %pooled.1.after), calls=%async_computation.2 | async-start | bytes 262144 | tf_op jit(solution)/shard_map/all_to_all | solution.py:231
  59.7 7.7 %copy-start = (s32[2,6]{1,0:T(2,128)S(1)}, s32[2,6]{1,0:T(2,128)}, u32[]{:S(2)}) copy-start(s32[2,6]{1,0:T(2,128)} %tile_lists.1) | copy-start | bytes 148
  61.2 12.2 %collective-permute-start.7 = (bf16[4,2,512,256]{3,2,1,0:T(8,128)(2,1)}, bf16[4,2,512,256]{3,2,1,0:T(8,128)(2,1)}, u32[]{:S(2)}, u32[]{:S(2)}) collective-permute-start(bf16[4,2,512,256]{3,2,1,0:T(8,128)(2,1)} %stack.1.w_near_in), channel_id=1, source_target_pairs={{0,64},{64,0},{1,65},{65,1},{2,66},{66,2},{3,67},{67,3},{4,68},{68... | collective-permute-start | bytes 6291464 | tf_op jit(solution)/shard_map/ppermute | solution.py:227

commit v8 on v7

--- a/solution.py
+++ b/solution.py
@@ -292,7 +292,7 @@
     kv_p1 = along_dom(key_value, -1)
     w_1 = around(w_0, "x", 1)
     w_2 = around(w_0, "x", -1)
-    w_3 = around(w_0, "x", 2)
+    w_3 = around(w_1, "x", 1)
 
     plane_sum = pl.pallas_call(
         plane_sum_kernel,
@@ -329,7 +329,7 @@
         out_specs=in_vmem,
         compiler_params=grant(2),
         name="pooled",
-    )(parts, vmem(token), w_3)
+    )(parts, vmem(token), w_1)
 
     virtual_kv = exchanged(pooled, PLANE)
     w_near = pl.pallas_call(

time: 76.9 us -> 76.1 us (0.990)
  starting transfers between devices: 58.2 us -> 55.7 us
  waiting for transfers between devices: 3.96 us -> 5.65 us
    ppermute x4, starting transfers between devices: 13.4 us -> 10.6 us  [around(): lax.ppermute(shard, axis, [(i, (i + by) % length) for i in range(length)])]
    all_to_all x3, waiting for transfers between devices: 3.94 us -> 5.63 us  [exchanged(): return lax.all_to_all(parts, axes, 0, 0, tiled=True)]
  transfers between devices with their start and end apart: 11 -> 11, of which waited for: 1 -> 3; matrix products, arithmetic and copies ran while one was open for 0% -> 0% of each run, Pallas kernels for 12% -> 12%
where the time goes in v8:
time: 76.1 us; the launch traced here: 75.5 us
  starting transfers between devices  55.7 us (73%)
  Pallas kernels  14 us (18%)
  waiting for transfers between devices  5.65 us (7%)
    all_to_all x3, starting transfers between devices, exchanged(): return lax.all_to_all(parts, axes, 0, 0, tiled=True)  34.4 us
    ppermute x4, starting transfers between devices, along_dom(): return lax.ppermute(shard, DOM, pairs)  10.7 us
    ppermute x4, starting transfers between devices, around(): lax.ppermute(shard, axis, [(i, (i + by) % length) for i in range(length)])  10.6 us
    pallas_call x1, Pallas kernels, local(): pl.pallas_call(layer_kernel, out_shape=(VMEM((node_rows, feat_width), F32...  5.97 us
    all_to_all x3, waiting for transfers between devices, exchanged(): return lax.all_to_all(parts, axes, 0, 0, tiled=True)  5.63 us
    pallas_call x1, Pallas kernels, local(): pl.pallas_call(finish_kernel, out_shape=shape((node_rows, feat_width), BF...  3.01 us
    pallas_call x1, Pallas kernels, local(): pl.pallas_call(pool_kernel, out_shape=(VMEM((plane, per_part, LANES), F32...  2.18 us
  transfers between devices with their start and end apart: 11, of which 3 were waited for; matrix products, arithmetic and copies ran while one was open for 0% of the time, Pallas kernels for 12%

profile of v8, /device:TPU:1, one launch (start us, length us, event | category | flops | bytes accessed | tf_op | source)
XLA Modules:
  0.0 75.5 jit_solution(18440171967775140408)
XLA Ops:
  0.0 2.2 %pool.1 = (f32[32,16,128]{2,1,0:T(8,128)}, bf16[2,256,512]{2,1,0:T(8,128)(2,1)}, bf16[2,512,256]{2,1,0:T(8,128)(2,1)S(1)}) custom-call(s32[1,256]{1,0:T(1,128)} %bitcast.2, bf16[256,512]{1,0:T(8,128)(2,1)} %keys.1, bf16[256,512]{1,0:T(8,128)(2,1)} %values.1, bf16[512,256]{1,0:T(8,128)(2,1)} %up_in.1, bf16[512,256]{1,0:T(8,128)(2,1)} %down_in.1), custom_call_target="tpu_custom_call" | custom-call | tf_op jit(solution)/shard_map/pool/pallas_call | solution.py:271
  2.2 10.4 %all-to-all-start = ((f32[32,16,128]{2,1,0:T(8,128)}), f32[32,16,128]{2,1,0:T(8,128)S(1)}, u32[]{:S(2)}, u32[]{:S(2)}) async-start(f32[32,16,128]{2,1,0:T(8,128)} %get-tuple-element.10), calls=%async_computation | async-start | bytes 524288 | tf_op jit(solution)/shard_map/all_to_all | solution.py:231
  12.6 3.3 %collective-permute-start = (bf16[2,256,512]{2,1,0:T(8,128)(2,1)}, bf16[2,256,512]{2,1,0:T(8,128)(2,1)S(1)}, u32[]{:S(2)}, u32[]{:S(2)}) collective-permute-start(bf16[2,256,512]{2,1,0:T(8,128)(2,1)} %get-tuple-element.11), channel_id=1, source_target_pairs={{0,1},{1,2},{2,3},{3,4},{4,5},{5,6},{6,7},{7,8},{8,9},{9,10},{10,1... | collective-permute-start | bytes 1572872 | tf_op jit(solution)/shard_map/ppermute | solution.py:222
  15.9 1.3 %collective-permute-start.1 = (bf16[2,256,512]{2,1,0:T(8,128)(2,1)}, bf16[2,256,512]{2,1,0:T(8,128)(2,1)S(1)}, u32[]{:S(2)}, u32[]{:S(2)}) collective-permute-start(bf16[2,256,512]{2,1,0:T(8,128)(2,1)} %get-tuple-element.11), channel_id=1, source_target_pairs={{1,0},{2,1},{3,2},{4,3},{5,4},{6,5},{7,6},{8,7},{9,8},{10,9},{11,1... | collective-permute-start | bytes 1572872 | tf_op jit(solution)/shard_map/ppermute | solution.py:222
  17.2 3.1 %collective-permute-start.2 = (bf16[2,512,256]{2,1,0:T(8,128)(2,1)S(1)}, bf16[2,512,256]{2,1,0:T(8,128)(2,1)S(1)}, u32[]{:S(2)}, u32[]{:S(2)}) collective-permute-start(bf16[2,512,256]{2,1,0:T(8,128)(2,1)S(1)} %get-tuple-element.12.w_0), channel_id=1, source_target_pairs={{0,128},{128,256},{256,384},{384,0},{1,129},{129,257},{257,385},{3... | collective-permute-start | bytes 1572872 | tf_op jit(solution)/shard_map/ppermute | solution.py:227
  20.4 1.1 %all-to-all-done.parts = f32[32,16,128]{2,1,0:T(8,128)S(1)} async-done(((f32[32,16,128]{2,1,0:T(8,128)}), f32[32,16,128]{2,1,0:T(8,128)S(1)}, u32[]{:S(2)}, u32[]{:S(2)}) %all-to-all-start) | async-done | bytes 262176 | tf_op jit(solution)/shard_map/all_to_all | solution.py:231
  21.5 0.7 plane_sum.1.after
  22.2 16.1 %all-to-all-start.1 = ((f32[16,16,128]{2,1,0:T(8,128)}), f32[16,16,128]{2,1,0:T(8,128)S(1)}, u32[]{:S(2)}, u32[]{:S(2)}) async-start(f32[16,16,128]{2,1,0:T(8,128)} %plane_sum.1.after), calls=%async_computation.1 | async-start | bytes 262144 | tf_op jit(solution)/shard_map/all_to_all | solution.py:231
  38.3 3.2 %collective-permute-start.5 = (bf16[2,512,256]{2,1,0:T(8,128)(2,1)S(1)}, bf16[2,512,256]{2,1,0:T(8,128)(2,1)S(1)}, u32[]{:S(2)}, u32[]{:S(2)}) collective-permute-start(bf16[2,512,256]{2,1,0:T(8,128)(2,1)S(1)} %get-tuple-element.12.w_0), channel_id=1, source_target_pairs={{0,384},{128,0},{256,128},{384,256},{1,385},{129,1},{257,129},{385... | collective-permute-start | bytes 1572872 | tf_op jit(solution)/shard_map/ppermute | solution.py:227
  41.6 0.0 collective-permute-done.2.after_1.w_1
  41.6 2.1 %collective-permute-start.6 = (bf16[2,512,256]{2,1,0:T(8,128)(2,1)S(1)}, bf16[2,512,256]{2,1,0:T(8,128)(2,1)S(1)}, u32[]{:S(2)}, u32[]{:S(2)}) collective-permute-start(bf16[2,512,256]{2,1,0:T(8,128)(2,1)S(1)} %collective-permute-done.2.after_1.w_1), channel_id=1, source_target_pairs={{0,128},{128,256},{256,384},{384,0},{1,129},{129,257},{257,385},{3... | collective-permute-start | bytes 1572872 | tf_op jit(solution)/shard_map/ppermute | solution.py:227
  43.7 0.0 collective-permute-done.1.right.kv_p1
  43.7 1.3 %collective-permute-start.3 = (bf16[2,256,512]{2,1,0:T(8,128)(2,1)S(1)}, bf16[2,256,512]{2,1,0:T(8,128)(2,1)}, u32[]{:S(2)}, u32[]{:S(2)}) collective-permute-start(bf16[2,256,512]{2,1,0:T(8,128)(2,1)S(1)} %collective-permute-done.1.right.kv_p1), channel_id=1, source_target_pairs={{1,0},{2,1},{3,2},{4,3},{5,4},{6,5},{7,6},{8,7},{9,8},{10,9},{11,1... | collective-permute-start | bytes 1572872 | tf_op jit(solution)/shard_map/ppermute | solution.py:222
  45.0 0.0 collective-permute-done.left.kv_m1
  45.0 4.8 %collective-permute-start.4 = (bf16[2,256,512]{2,1,0:T(8,128)(2,1)S(1)}, bf16[2,256,512]{2,1,0:T(8,128)(2,1)}, u32[]{:S(2)}, u32[]{:S(2)}) collective-permute-start(bf16[2,256,512]{2,1,0:T(8,128)(2,1)S(1)} %collective-permute-done.left.kv_m1), channel_id=1, source_target_pairs={{0,1},{1,2},{2,3},{3,4},{4,5},{5,6},{6,7},{7,8},{8,9},{9,10},{10,1... | collective-permute-start | bytes 1572872 | tf_op jit(solution)/shard_map/ppermute | solution.py:222
  49.8 0.6 all-to-all-done.1.parts
  50.3 0.7 pooled.1.after
  51.0 7.9 %all-to-all-start.2 = ((bf16[32,16,128]{2,1,0:T(8,128)(2,1)}), bf16[32,16,128]{2,1,0:T(8,128)(2,1)S(1)}, u32[]{:S(2)}, u32[]{:S(2)}) async-start(bf16[32,16,128]{2,1,0:T(8,128)(2,1)} %pooled.1.after), calls=%async_computation.2 | async-start | bytes 262144 | tf_op jit(solution)/shard_map/all_to_all | solution.py:231
  58.9 0.0 copy-start
  58.9 0.0 collective-permute-done.5.w_2
  58.9 0.0 collective-permute-done.6.w_3
  59.0 1.5 %stack.1.w_near_in = bf16[4,2,512,256]{3,2,1,0:T(8,128)(2,1)} custom-call(bf16[32,16,128]{2,1,0:T(8,128)(2,1)} %pooled.1.after, bf16[2,512,256]{2,1,0:T(8,128)(2,1)S(1)} %get-tuple-element.12.w_0, bf16[2,512,256]{2,1,0:T(8,128)(2,1)S(1)} %collective-permute-done.2.after_1.w_1, bf16[2,512,256]{2,1,0:T(8,128)(2,1)S(1)} %collective-permute-done.5.w_2, ...), custom_call_target="tpu_custom_call" | custom-call | tf_op jit(solution)/shard_map/stack/pallas_call | solution.py:335
  60.4 2.1 %collective-permute-start.7 = (bf16[4,2,512,256]{3,2,1,0:T(8,128)(2,1)}, bf16[4,2,512,256]{3,2,1,0:T(8,128)(2,1)}, u32[]{:S(2)}, u32[]{:S(2)}) collective-permute-start(bf16[4,2,512,256]{3,2,1,0:T(8,128)(2,1)} %stack.1.w_near_in), channel_id=1, source_target_pairs={{0,64},{64,0},{1,65},{65,1},{2,66},{66,2},{3,67},{67,3},{4,68},{68... | collective-permute-start | bytes 6291464 | tf_op jit(solution)/shard_map/ppermute | solution.py:227
  62.6 3.9 %all-to-all-done.2.virtual_kv = bf16[32,16,128]{2,1,0:T(8,128)(2,1)S(1)} async-done(((bf16[32,16,128]{2,1,0:T(8,128)(2,1)}), bf16[32,16,128]{2,1,0:T(8,128)(2,1)S(1)}, u32[]{:S(2)}, u32[]{:S(2)}) %all-to-all-start.2) | async-done | bytes 131104 | tf_op jit(solution)/shard_map/all_to_all | solution.py:231
  66.5 0.0 collective-permute-done.3.kv_p2
  66.5 0.0 collective-permute-done.4.kv_m2
  66.5 0.0 copy-done
  66.5 6.0 %layer.1 = (f32[256,512]{1,0:T(8,128)S(1)}, bf16[256,512]{1,0:T(8,128)(2,1)S(1)}) custom-call(s32[2,6]{1,0:T(2,128)S(1)} %copy-done, bf16[32,16,128]{2,1,0:T(8,128)(2,1)S(1)} %all-to-all-done.2.virtual_kv, bf16[256,512]{1,0:T(8,128)(2,1)} %queries_in.1, bf16[256,512]{1,0:T(8,128)(2,1)} %keys.1, bf16[256,512]{1,0:T(8,128)(2,1)} %values.1, ...), custom_call_target="tpu_custom_call" | custom-call | flops 399999991808 | bytes 6000000 | tf_op jit(solution)/shard_map/layer/pallas_call | solution.py:345
  72.5 0.0 collective-permute-done.7.weights
  72.5 3.0 %finish.1 = bf16[256,512]{1,0:T(8,128)(2,1)} custom-call(f32[256,512]{1,0:T(8,128)S(1)} %get-tuple-element.13.partial, bf16[256,512]{1,0:T(8,128)(2,1)S(1)} %get-tuple-element.14.normed, bf16[4,2,512,256]{3,2,1,0:T(8,128)(2,1)} %collective-permute-done.7.weights), custom_call_target="tpu_custom_call" | custom-call | tf_op jit(solution)/shard_map/finish/pallas_call | solution.py:380
  (1 shorter events, 0.0 us)
Async XLA Ops:
  2.2 19.3 %all-to-all-start = ((f32[32,16,128]{2,1,0:T(8,128)}), f32[32,16,128]{2,1,0:T(8,128)S(1)}, u32[]{:S(2)}, u32[]{:S(2)}) async-start(f32[32,16,128]{2,1,0:T(8,128)} %get-tuple-element.10), calls=%async_computation | async-start | bytes 524288 | tf_op jit(solution)/shard_map/all_to_all | solution.py:231
  12.6 32.3 %collective-permute-start = (bf16[2,256,512]{2,1,0:T(8,128)(2,1)}, bf16[2,256,512]{2,1,0:T(8,128)(2,1)S(1)}, u32[]{:S(2)}, u32[]{:S(2)}) collective-permute-start(bf16[2,256,512]{2,1,0:T(8,128)(2,1)} %get-tuple-element.11), channel_id=1, source_target_pairs={{0,1},{1,2},{2,3},{3,4},{4,5},{5,6},{6,7},{7,8},{8,9},{9,10},{10,1... | collective-permute-start | bytes 1572872 | tf_op jit(solution)/shard_map/ppermute | solution.py:222
  15.9 27.7 %collective-permute-start.1 = (bf16[2,256,512]{2,1,0:T(8,128)(2,1)}, bf16[2,256,512]{2,1,0:T(8,128)(2,1)S(1)}, u32[]{:S(2)}, u32[]{:S(2)}) collective-permute-start(bf16[2,256,512]{2,1,0:T(8,128)(2,1)} %get-tuple-element.11), channel_id=1, source_target_pairs={{1,0},{2,1},{3,2},{4,3},{5,4},{6,5},{7,6},{8,7},{9,8},{10,9},{11,1... | collective-permute-start | bytes 1572872 | tf_op jit(solution)/shard_map/ppermute | solution.py:222
  17.2 24.3 %collective-permute-start.2 = (bf16[2,512,256]{2,1,0:T(8,128)(2,1)S(1)}, bf16[2,512,256]{2,1,0:T(8,128)(2,1)S(1)}, u32[]{:S(2)}, u32[]{:S(2)}) collective-permute-start(bf16[2,512,256]{2,1,0:T(8,128)(2,1)S(1)} %get-tuple-element.12.w_0), channel_id=1, source_target_pairs={{0,128},{128,256},{256,384},{384,0},{1,129},{129,257},{257,385},{3... | collective-permute-start | bytes 1572872 | tf_op jit(solution)/shard_map/ppermute | solution.py:227
  22.2 28.1 %all-to-all-start.1 = ((f32[16,16,128]{2,1,0:T(8,128)}), f32[16,16,128]{2,1,0:T(8,128)S(1)}, u32[]{:S(2)}, u32[]{:S(2)}) async-start(f32[16,16,128]{2,1,0:T(8,128)} %plane_sum.1.after), calls=%async_computation.1 | async-start | bytes 262144 | tf_op jit(solution)/shard_map/all_to_all | solution.py:231
  38.3 20.6 %collective-permute-start.5 = (bf16[2,512,256]{2,1,0:T(8,128)(2,1)S(1)}, bf16[2,512,256]{2,1,0:T(8,128)(2,1)S(1)}, u32[]{:S(2)}, u32[]{:S(2)}) collective-permute-start(bf16[2,512,256]{2,1,0:T(8,128)(2,1)S(1)} %get-tuple-element.12.w_0), channel_id=1, source_target_pairs={{0,384},{128,0},{256,128},{384,256},{1,385},{129,1},{257,129},{385... | collective-permute-start | bytes 1572872 | tf_op jit(solution)/shard_map/ppermute | solution.py:227
  41.6 17.4 %collective-permute-start.6 = (bf16[2,512,256]{2,1,0:T(8,128)(2,1)S(1)}, bf16[2,512,256]{2,1,0:T(8,128)(2,1)S(1)}, u32[]{:S(2)}, u32[]{:S(2)}) collective-permute-start(bf16[2,512,256]{2,1,0:T(8,128)(2,1)S(1)} %collective-permute-done.2.after_1.w_1), channel_id=1, source_target_pairs={{0,128},{128,256},{256,384},{384,0},{1,129},{129,257},{257,385},{3... | collective-permute-start | bytes 1572872 | tf_op jit(solution)/shard_map/ppermute | solution.py:227
  43.7 22.8 %collective-permute-start.3 = (bf16[2,256,512]{2,1,0:T(8,128)(2,1)S(1)}, bf16[2,256,512]{2,1,0:T(8,128)(2,1)}, u32[]{:S(2)}, u32[]{:S(2)}) collective-permute-start(bf16[2,256,512]{2,1,0:T(8,128)(2,1)S(1)} %collective-permute-done.1.right.kv_p1), channel_id=1, source_target_pairs={{1,0},{2,1},{3,2},{4,3},{5,4},{6,5},{7,6},{8,7},{9,8},{10,9},{11,1... | collective-permute-start | bytes 1572872 | tf_op jit(solution)/shard_map/ppermute | solution.py:222
  45.0 21.5 %collective-permute-start.4 = (bf16[2,256,512]{2,1,0:T(8,128)(2,1)S(1)}, bf16[2,256,512]{2,1,0:T(8,128)(2,1)}, u32[]{:S(2)}, u32[]{:S(2)}) collective-permute-start(bf16[2,256,512]{2,1,0:T(8,128)(2,1)S(1)} %collective-permute-done.left.kv_m1), channel_id=1, source_target_pairs={{0,1},{1,2},{2,3},{3,4},{4,5},{5,6},{6,7},{7,8},{8,9},{9,10},{10,1... | collective-permute-start | bytes 1572872 | tf_op jit(solution)/shard_map/ppermute | solution.py:222
  51.0 15.5 %all-to-all-start.2 = ((bf16[32,16,128]{2,1,0:T(8,128)(2,1)}), bf16[32,16,128]{2,1,0:T(8,128)(2,1)S(1)}, u32[]{:S(2)}, u32[]{:S(2)}) async-start(bf16[32,16,128]{2,1,0:T(8,128)(2,1)} %pooled.1.after), calls=%async_computation.2 | async-start | bytes 262144 | tf_op jit(solution)/shard_map/all_to_all | solution.py:231
  58.9 7.6 %copy-start = (s32[2,6]{1,0:T(2,128)S(1)}, s32[2,6]{1,0:T(2,128)}, u32[]{:S(2)}) copy-start(s32[2,6]{1,0:T(2,128)} %tile_lists.1) | copy-start | bytes 148
  60.4 12.1 %collective-permute-start.7 = (bf16[4,2,512,256]{3,2,1,0:T(8,128)(2,1)}, bf16[4,2,512,256]{3,2,1,0:T(8,128)(2,1)}, u32[]{:S(2)}, u32[]{:S(2)}) collective-permute-start(bf16[4,2,512,256]{3,2,1,0:T(8,128)(2,1)} %stack.1.w_near_in), channel_id=1, source_target_pairs={{0,64},{64,0},{1,65},{65,1},{2,66},{66,2},{3,67},{67,3},{4,68},{68... | collective-permute-start | bytes 6291464 | tf_op jit(solution)/shard_map/ppermute | solution.py:227

commit v9 on v8

--- a/solution.py
+++ b/solution.py
@@ -104,7 +104,6 @@
     sem,
 ):
     rows, feat_width = queries.shape
-    near = w_near.shape[0]
     middle = REACH * rows
     moves = [
         (queries_in, queries),
@@ -118,7 +117,7 @@
         (node_feats_in, node_feats),
         (norm_gain_in, norm_gain),
     ]
-    moves += [(w_near_in.at[shard], w_near.at[shard]) for shard in range(near)]
+    moves.append((w_near_in, w_near))
     copies = [
         pltpu.make_async_copy(source, target, sem.at[i])
         for i, (source, target) in enumerate(moves)
@@ -135,7 +134,10 @@
     for copy in copies[:7]:
         copy.wait()
 
+    ones = jnp.ones((BLOCK, LANES), BF16)
+
     def attend(block, slots, starts, shown):
+        last = jnp.full((BLOCK, LANES), jnp.where(shown[slots - 1], 1.0, 0.0), F32).astype(BF16)
         here = slice(block * BLOCK, (block + 1) * BLOCK)
         for part in range(lane_parts):
             lanes = slice(part * LANES, (part + 1) * LANES)
@@ -150,19 +152,10 @@
                 + pooled[:rows_parts],
                 axis=0,
             )
-            right = jnp.concatenate(
-                [
-                    jnp.concatenate(
-                        [window[1, pl.ds(start, BLOCK), lanes] * there, there], axis=1
-                    )
-                    for start, there in zip(starts[:slots], shown)
-                ]
-                + [
-                    jnp.concatenate([piece, jnp.ones_like(piece)], axis=1)
-                    for piece in pooled[rows_parts:]
-                ],
-                axis=0,
-            )
+            sides = [(window[1, pl.ds(start, BLOCK), lanes], ones) for start in starts[:slots]]
+            sides[-1] = (sides[-1][0] * last, last)
+            sides += [(piece, jnp.ones_like(piece)) for piece in pooled[rows_parts:]]
+            right = jnp.concatenate([jnp.concatenate(side, axis=1) for side in sides], axis=0)
             scores = lax.dot_general(
                 both, all_keys, (((1,), (1,)), ((), ())), preferred_element_type=F32
             )
@@ -181,7 +174,7 @@
             there = tile >= 0
             place = jnp.where(there, tile, own) - first_block
             starts.append(pl.multiple_of(place * BLOCK, BLOCK))
-            shown.append(jnp.full((BLOCK, LANES), jnp.where(there, 1.0, 0.0), F32).astype(BF16))
+            shown.append(there)
         for slots in range(2, TMAX + 1, 2):
             needed = tile_lists[block, slots - 2] >= 0
             if slots < TMAX:
@@ -198,22 +191,37 @@
     variance = jnp.mean(centered * centered, axis=-1, keepdims=True)
     normed = (centered * lax.rsqrt(variance + 1e-05) * norm_gain[...]).astype(BF16)
     normed_out[...] = normed
-    partial_out[...] = residual + hidden_sum(normed, w_near, copies[10:])
-
-
-def hidden_sum(normed, weights, copies):
+    copies[10].wait()
+    hidden = hidden_units(normed, w_near.at[:, 0])
+    partial_out[...] = residual + projected(hidden, w_near.at[:, 1])
+
+
+def side_by_side(shards):
+    return jnp.concatenate([shards[shard] for shard in range(shards.shape[0])], axis=1)
+
+
+def hidden_units(normed, up):
+    hidden = jnp.dot(normed, side_by_side(up), preferred_element_type=F32)
+    return jnp.maximum(hidden, 0.0).astype(BF16)
+
+
+def projected(hidden, down):
+    return lax.dot_general(
+        hidden, side_by_side(down), (((1,), (1,)), ((), ())), preferred_element_type=F32
+    )
+
+
+def finish_kernel(partial, normed, weights_in, layer_out, up, down, sem):
+    copies = [
+        pltpu.make_async_copy(weights_in.at[:, which], target, sem.at[which])
+        for which, target in enumerate((up, down))
+    ]
     for copy in copies:
-        copy.wait()
-    shards = range(weights.shape[0])
-    up = jnp.concatenate([weights[shard, 0] for shard in shards], axis=1)
-    down = jnp.concatenate([weights[shard, 1] for shard in shards], axis=1)
-    hidden = jnp.dot(normed, up, preferred_element_type=F32)
-    hidden = jnp.maximum(hidden, 0.0).astype(BF16)
-    return lax.dot_general(hidden, down, (((1,), (1,)), ((), ())), preferred_element_type=F32)
-
-
-def finish_kernel(partial, normed, weights, layer_out):
-    layer_out[...] = (partial[...] + hidden_sum(normed[...], weights, ())).astype(BF16)
+        copy.start()
+    copies[0].wait()
+    hidden = hidden_units(normed[...], up)
+    copies[1].wait()
+    layer_out[...] = (partial[...] + projected(hidden, down)).astype(BF16)
 
 
 def along_dom(shard, by):
@@ -355,9 +363,9 @@
             VMEM((1, feat_width), F32),
             VMEM((near, *w_shape), BF16),
             VMEM((node_rows, feat_width), BF16),
-            dma(10 + near),
+            dma(11),
         ],
-        compiler_params=grant(12),
+        compiler_params=grant(10),
         cost_estimate=pl.CostEstimate(
             flops=400_000_000_000, bytes_accessed=6_000_000, transcendentals=2_000_000
         ),
@@ -380,11 +388,16 @@
     return pl.pallas_call(
         finish_kernel,
         out_shape=shape((node_rows, feat_width), BF16),
-        in_specs=[in_vmem] * 3,
+        in_specs=[in_vmem, in_vmem, anywhere],
         out_specs=in_vmem,
+        scratch_shapes=[
+            VMEM((near, feat_width, own_hidden), BF16),
+            VMEM((near, feat_width, own_hidden), BF16),
+            dma(2),
+        ],
         compiler_params=grant(8),
         name="finish",
-    )(vmem(partial), vmem(normed), vmem(w_far))
+    )(vmem(partial), vmem(normed), w_far)
 
 
 def solution(mesh):

time: 76.1 us -> 75.9 us (level)
  no operation moved by 1% of the time
where the time goes in v9:
time: 75.9 us; the launch traced here: 75.3 us
  starting transfers between devices  55.7 us (73%)
  Pallas kernels  13.8 us (18%)
  waiting for transfers between devices  5.65 us (7%)
    all_to_all x3, starting transfers between devices, exchanged(): return lax.all_to_all(parts, axes, 0, 0, tiled=True)  34.4 us
    ppermute x4, starting transfers between devices, along_dom(): return lax.ppermute(shard, DOM, pairs)  10.7 us
    ppermute x4, starting transfers between devices, around(): lax.ppermute(shard, axis, [(i, (i + by) % length) for i in range(length)])  10.6 us
    pallas_call x1, Pallas kernels, local(): pl.pallas_call(layer_kernel, out_shape=(VMEM((node_rows, feat_width), F32...  5.93 us
    all_to_all x3, waiting for transfers between devices, exchanged(): return lax.all_to_all(parts, axes, 0, 0, tiled=True)  5.63 us
    pallas_call x1, Pallas kernels, local(): pl.pallas_call(finish_kernel, out_shape=shape((node_rows, feat_width), BF...  2.86 us
    pallas_call x1, Pallas kernels, local(): pl.pallas_call(pool_kernel, out_shape=(VMEM((plane, per_part, LANES), F32...  2.18 us
  transfers between devices with their start and end apart: 11, of which 3 were waited for; matrix products, arithmetic and copies ran while one was open for 0% of the time, Pallas kernels for 12%

profile of v9, /device:TPU:1, one launch (start us, length us, event | category | flops | bytes accessed | tf_op | source)
XLA Modules:
  0.0 75.3 jit_solution(11034662661647378920)
XLA Ops:
  0.0 2.2 %pool.1 = (f32[32,16,128]{2,1,0:T(8,128)}, bf16[2,256,512]{2,1,0:T(8,128)(2,1)}, bf16[2,512,256]{2,1,0:T(8,128)(2,1)S(1)}) custom-call(s32[1,256]{1,0:T(1,128)} %bitcast.2, bf16[256,512]{1,0:T(8,128)(2,1)} %keys.1, bf16[256,512]{1,0:T(8,128)(2,1)} %values.1, bf16[512,256]{1,0:T(8,128)(2,1)} %up_in.1, bf16[512,256]{1,0:T(8,128)(2,1)} %down_in.1), custom_call_target="tpu_custom_call" | custom-call | tf_op jit(solution)/shard_map/pool/pallas_call | solution.py:279
  2.2 10.4 %all-to-all-start = ((f32[32,16,128]{2,1,0:T(8,128)}), f32[32,16,128]{2,1,0:T(8,128)S(1)}, u32[]{:S(2)}, u32[]{:S(2)}) async-start(f32[32,16,128]{2,1,0:T(8,128)} %get-tuple-element.10), calls=%async_computation | async-start | bytes 524288 | tf_op jit(solution)/shard_map/all_to_all | solution.py:239
  12.6 3.3 %collective-permute-start = (bf16[2,256,512]{2,1,0:T(8,128)(2,1)}, bf16[2,256,512]{2,1,0:T(8,128)(2,1)S(1)}, u32[]{:S(2)}, u32[]{:S(2)}) collective-permute-start(bf16[2,256,512]{2,1,0:T(8,128)(2,1)} %get-tuple-element.11), channel_id=1, source_target_pairs={{0,1},{1,2},{2,3},{3,4},{4,5},{5,6},{6,7},{7,8},{8,9},{9,10},{10,1... | collective-permute-start | bytes 1572872 | tf_op jit(solution)/shard_map/ppermute | solution.py:230
  15.9 1.3 %collective-permute-start.1 = (bf16[2,256,512]{2,1,0:T(8,128)(2,1)}, bf16[2,256,512]{2,1,0:T(8,128)(2,1)S(1)}, u32[]{:S(2)}, u32[]{:S(2)}) collective-permute-start(bf16[2,256,512]{2,1,0:T(8,128)(2,1)} %get-tuple-element.11), channel_id=1, source_target_pairs={{1,0},{2,1},{3,2},{4,3},{5,4},{6,5},{7,6},{8,7},{9,8},{10,9},{11,1... | collective-permute-start | bytes 1572872 | tf_op jit(solution)/shard_map/ppermute | solution.py:230
  17.2 3.1 %collective-permute-start.2 = (bf16[2,512,256]{2,1,0:T(8,128)(2,1)S(1)}, bf16[2,512,256]{2,1,0:T(8,128)(2,1)S(1)}, u32[]{:S(2)}, u32[]{:S(2)}) collective-permute-start(bf16[2,512,256]{2,1,0:T(8,128)(2,1)S(1)} %get-tuple-element.12.w_0), channel_id=1, source_target_pairs={{0,128},{128,256},{256,384},{384,0},{1,129},{129,257},{257,385},{3... | collective-permute-start | bytes 1572872 | tf_op jit(solution)/shard_map/ppermute | solution.py:235
  20.4 1.1 %all-to-all-done.parts = f32[32,16,128]{2,1,0:T(8,128)S(1)} async-done(((f32[32,16,128]{2,1,0:T(8,128)}), f32[32,16,128]{2,1,0:T(8,128)S(1)}, u32[]{:S(2)}, u32[]{:S(2)}) %all-to-all-start) | async-done | bytes 262176 | tf_op jit(solution)/shard_map/all_to_all | solution.py:239
  21.5 0.7 plane_sum.1.after
  22.2 16.1 %all-to-all-start.1 = ((f32[16,16,128]{2,1,0:T(8,128)}), f32[16,16,128]{2,1,0:T(8,128)S(1)}, u32[]{:S(2)}, u32[]{:S(2)}) async-start(f32[16,16,128]{2,1,0:T(8,128)} %plane_sum.1.after), calls=%async_computation.1 | async-start | bytes 262144 | tf_op jit(solution)/shard_map/all_to_all | solution.py:239
  38.3 3.2 %collective-permute-start.5 = (bf16[2,512,256]{2,1,0:T(8,128)(2,1)S(1)}, bf16[2,512,256]{2,1,0:T(8,128)(2,1)S(1)}, u32[]{:S(2)}, u32[]{:S(2)}) collective-permute-start(bf16[2,512,256]{2,1,0:T(8,128)(2,1)S(1)} %get-tuple-element.12.w_0), channel_id=1, source_target_pairs={{0,384},{128,0},{256,128},{384,256},{1,385},{129,1},{257,129},{385... | collective-permute-start | bytes 1572872 | tf_op jit(solution)/shard_map/ppermute | solution.py:235
  41.6 0.0 collective-permute-done.2.after_1.w_1
  41.6 2.1 %collective-permute-start.6 = (bf16[2,512,256]{2,1,0:T(8,128)(2,1)S(1)}, bf16[2,512,256]{2,1,0:T(8,128)(2,1)S(1)}, u32[]{:S(2)}, u32[]{:S(2)}) collective-permute-start(bf16[2,512,256]{2,1,0:T(8,128)(2,1)S(1)} %collective-permute-done.2.after_1.w_1), channel_id=1, source_target_pairs={{0,128},{128,256},{256,384},{384,0},{1,129},{129,257},{257,385},{3... | collective-permute-start | bytes 1572872 | tf_op jit(solution)/shard_map/ppermute | solution.py:235
  43.7 0.0 collective-permute-done.1.right.kv_p1
  43.7 1.3 %collective-permute-start.3 = (bf16[2,256,512]{2,1,0:T(8,128)(2,1)S(1)}, bf16[2,256,512]{2,1,0:T(8,128)(2,1)}, u32[]{:S(2)}, u32[]{:S(2)}) collective-permute-start(bf16[2,256,512]{2,1,0:T(8,128)(2,1)S(1)} %collective-permute-done.1.right.kv_p1), channel_id=1, source_target_pairs={{1,0},{2,1},{3,2},{4,3},{5,4},{6,5},{7,6},{8,7},{9,8},{10,9},{11,1... | collective-permute-start | bytes 1572872 | tf_op jit(solution)/shard_map/ppermute | solution.py:230
  45.0 0.0 collective-permute-done.left.kv_m1
  45.0 4.8 %collective-permute-start.4 = (bf16[2,256,512]{2,1,0:T(8,128)(2,1)S(1)}, bf16[2,256,512]{2,1,0:T(8,128)(2,1)}, u32[]{:S(2)}, u32[]{:S(2)}) collective-permute-start(bf16[2,256,512]{2,1,0:T(8,128)(2,1)S(1)} %collective-permute-done.left.kv_m1), channel_id=1, source_target_pairs={{0,1},{1,2},{2,3},{3,4},{4,5},{5,6},{6,7},{7,8},{8,9},{9,10},{10,1... | collective-permute-start | bytes 1572872 | tf_op jit(solution)/shard_map/ppermute | solution.py:230
  49.8 0.6 all-to-all-done.1.parts
  50.3 0.7 pooled.1.after
  51.0 7.9 %all-to-all-start.2 = ((bf16[32,16,128]{2,1,0:T(8,128)(2,1)}), bf16[32,16,128]{2,1,0:T(8,128)(2,1)S(1)}, u32[]{:S(2)}, u32[]{:S(2)}) async-start(bf16[32,16,128]{2,1,0:T(8,128)(2,1)} %pooled.1.after), calls=%async_computation.2 | async-start | bytes 262144 | tf_op jit(solution)/shard_map/all_to_all | solution.py:239
  58.9 0.0 copy-start
  58.9 0.0 collective-permute-done.5.w_2
  58.9 0.0 collective-permute-done.6.w_3
  59.0 1.5 %stack.1.w_near_in = bf16[4,2,512,256]{3,2,1,0:T(8,128)(2,1)} custom-call(bf16[32,16,128]{2,1,0:T(8,128)(2,1)} %pooled.1.after, bf16[2,512,256]{2,1,0:T(8,128)(2,1)S(1)} %get-tuple-element.12.w_0, bf16[2,512,256]{2,1,0:T(8,128)(2,1)S(1)} %collective-permute-done.2.after_1.w_1, bf16[2,512,256]{2,1,0:T(8,128)(2,1)S(1)} %collective-permute-done.5.w_2, ...), custom_call_target="tpu_custom_call" | custom-call | tf_op jit(solution)/shard_map/stack/pallas_call | solution.py:343
  60.4 2.1 %collective-permute-start.7 = (bf16[4,2,512,256]{3,2,1,0:T(8,128)(2,1)}, bf16[4,2,512,256]{3,2,1,0:T(8,128)(2,1)}, u32[]{:S(2)}, u32[]{:S(2)}) collective-permute-start(bf16[4,2,512,256]{3,2,1,0:T(8,128)(2,1)} %stack.1.w_near_in), channel_id=1, source_target_pairs={{0,64},{64,0},{1,65},{65,1},{2,66},{66,2},{3,67},{67,3},{4,68},{68... | collective-permute-start | bytes 6291464 | tf_op jit(solution)/shard_map/ppermute | solution.py:235
  62.6 3.9 %all-to-all-done.2.virtual_kv = bf16[32,16,128]{2,1,0:T(8,128)(2,1)S(1)} async-done(((bf16[32,16,128]{2,1,0:T(8,128)(2,1)}), bf16[32,16,128]{2,1,0:T(8,128)(2,1)S(1)}, u32[]{:S(2)}, u32[]{:S(2)}) %all-to-all-start.2) | async-done | bytes 131104 | tf_op jit(solution)/shard_map/all_to_all | solution.py:239
  66.5 0.0 collective-permute-done.3.kv_p2
  66.5 0.0 collective-permute-done.4.kv_m2
  66.5 0.0 copy-done
  66.5 5.9 %layer.1 = (f32[256,512]{1,0:T(8,128)S(1)}, bf16[256,512]{1,0:T(8,128)(2,1)S(1)}) custom-call(s32[2,6]{1,0:T(2,128)S(1)} %copy-done, bf16[32,16,128]{2,1,0:T(8,128)(2,1)S(1)} %all-to-all-done.2.virtual_kv, bf16[256,512]{1,0:T(8,128)(2,1)} %queries_in.1, bf16[256,512]{1,0:T(8,128)(2,1)} %keys.1, bf16[256,512]{1,0:T(8,128)(2,1)} %values.1, ...), custom_call_target="tpu_custom_call" | custom-call | flops 399999991808 | bytes 6000000 | tf_op jit(solution)/shard_map/layer/pallas_call | solution.py:353
  72.4 0.0 collective-permute-done.7.weights_in
  72.5 2.9 %finish.1 = bf16[256,512]{1,0:T(8,128)(2,1)} custom-call(f32[256,512]{1,0:T(8,128)S(1)} %get-tuple-element.13.partial, bf16[256,512]{1,0:T(8,128)(2,1)S(1)} %get-tuple-element.14.normed, bf16[4,2,512,256]{3,2,1,0:T(8,128)(2,1)} %collective-permute-done.7.weights_in), custom_call_target="tpu_custom_call" | custom-call | tf_op jit(solution)/shard_map/finish/pallas_call | solution.py:388
  (1 shorter events, 0.0 us)
Async XLA Ops:
  2.2 19.3 %all-to-all-start = ((f32[32,16,128]{2,1,0:T(8,128)}), f32[32,16,128]{2,1,0:T(8,128)S(1)}, u32[]{:S(2)}, u32[]{:S(2)}) async-start(f32[32,16,128]{2,1,0:T(8,128)} %get-tuple-element.10), calls=%async_computation | async-start | bytes 524288 | tf_op jit(solution)/shard_map/all_to_all | solution.py:239
  12.6 32.3 %collective-permute-start = (bf16[2,256,512]{2,1,0:T(8,128)(2,1)}, bf16[2,256,512]{2,1,0:T(8,128)(2,1)S(1)}, u32[]{:S(2)}, u32[]{:S(2)}) collective-permute-start(bf16[2,256,512]{2,1,0:T(8,128)(2,1)} %get-tuple-element.11), channel_id=1, source_target_pairs={{0,1},{1,2},{2,3},{3,4},{4,5},{5,6},{6,7},{7,8},{8,9},{9,10},{10,1... | collective-permute-start | bytes 1572872 | tf_op jit(solution)/shard_map/ppermute | solution.py:230
  15.9 27.7 %collective-permute-start.1 = (bf16[2,256,512]{2,1,0:T(8,128)(2,1)}, bf16[2,256,512]{2,1,0:T(8,128)(2,1)S(1)}, u32[]{:S(2)}, u32[]{:S(2)}) collective-permute-start(bf16[2,256,512]{2,1,0:T(8,128)(2,1)} %get-tuple-element.11), channel_id=1, source_target_pairs={{1,0},{2,1},{3,2},{4,3},{5,4},{6,5},{7,6},{8,7},{9,8},{10,9},{11,1... | collective-permute-start | bytes 1572872 | tf_op jit(solution)/shard_map/ppermute | solution.py:230
  17.2 24.3 %collective-permute-start.2 = (bf16[2,512,256]{2,1,0:T(8,128)(2,1)S(1)}, bf16[2,512,256]{2,1,0:T(8,128)(2,1)S(1)}, u32[]{:S(2)}, u32[]{:S(2)}) collective-permute-start(bf16[2,512,256]{2,1,0:T(8,128)(2,1)S(1)} %get-tuple-element.12.w_0), channel_id=1, source_target_pairs={{0,128},{128,256},{256,384},{384,0},{1,129},{129,257},{257,385},{3... | collective-permute-start | bytes 1572872 | tf_op jit(solution)/shard_map/ppermute | solution.py:235
  22.2 28.1 %all-to-all-start.1 = ((f32[16,16,128]{2,1,0:T(8,128)}), f32[16,16,128]{2,1,0:T(8,128)S(1)}, u32[]{:S(2)}, u32[]{:S(2)}) async-start(f32[16,16,128]{2,1,0:T(8,128)} %plane_sum.1.after), calls=%async_computation.1 | async-start | bytes 262144 | tf_op jit(solution)/shard_map/all_to_all | solution.py:239
  38.3 20.6 %collective-permute-start.5 = (bf16[2,512,256]{2,1,0:T(8,128)(2,1)S(1)}, bf16[2,512,256]{2,1,0:T(8,128)(2,1)S(1)}, u32[]{:S(2)}, u32[]{:S(2)}) collective-permute-start(bf16[2,512,256]{2,1,0:T(8,128)(2,1)S(1)} %get-tuple-element.12.w_0), channel_id=1, source_target_pairs={{0,384},{128,0},{256,128},{384,256},{1,385},{129,1},{257,129},{385... | collective-permute-start | bytes 1572872 | tf_op jit(solution)/shard_map/ppermute | solution.py:235
  41.6 17.4 %collective-permute-start.6 = (bf16[2,512,256]{2,1,0:T(8,128)(2,1)S(1)}, bf16[2,512,256]{2,1,0:T(8,128)(2,1)S(1)}, u32[]{:S(2)}, u32[]{:S(2)}) collective-permute-start(bf16[2,512,256]{2,1,0:T(8,128)(2,1)S(1)} %collective-permute-done.2.after_1.w_1), channel_id=1, source_target_pairs={{0,128},{128,256},{256,384},{384,0},{1,129},{129,257},{257,385},{3... | collective-permute-start | bytes 1572872 | tf_op jit(solution)/shard_map/ppermute | solution.py:235
  43.7 22.8 %collective-permute-start.3 = (bf16[2,256,512]{2,1,0:T(8,128)(2,1)S(1)}, bf16[2,256,512]{2,1,0:T(8,128)(2,1)}, u32[]{:S(2)}, u32[]{:S(2)}) collective-permute-start(bf16[2,256,512]{2,1,0:T(8,128)(2,1)S(1)} %collective-permute-done.1.right.kv_p1), channel_id=1, source_target_pairs={{1,0},{2,1},{3,2},{4,3},{5,4},{6,5},{7,6},{8,7},{9,8},{10,9},{11,1... | collective-permute-start | bytes 1572872 | tf_op jit(solution)/shard_map/ppermute | solution.py:230
  45.0 21.5 %collective-permute-start.4 = (bf16[2,256,512]{2,1,0:T(8,128)(2,1)S(1)}, bf16[2,256,512]{2,1,0:T(8,128)(2,1)}, u32[]{:S(2)}, u32[]{:S(2)}) collective-permute-start(bf16[2,256,512]{2,1,0:T(8,128)(2,1)S(1)} %collective-permute-done.left.kv_m1), channel_id=1, source_target_pairs={{0,1},{1,2},{2,3},{3,4},{4,5},{5,6},{6,7},{7,8},{8,9},{9,10},{10,1... | collective-permute-start | bytes 1572872 | tf_op jit(solution)/shard_map/ppermute | solution.py:230
  51.0 15.5 %all-to-all-start.2 = ((bf16[32,16,128]{2,1,0:T(8,128)(2,1)}), bf16[32,16,128]{2,1,0:T(8,128)(2,1)S(1)}, u32[]{:S(2)}, u32[]{:S(2)}) async-start(bf16[32,16,128]{2,1,0:T(8,128)(2,1)} %pooled.1.after), calls=%async_computation.2 | async-start | bytes 262144 | tf_op jit(solution)/shard_map/all_to_all | solution.py:239
  58.9 7.6 %copy-start = (s32[2,6]{1,0:T(2,128)S(1)}, s32[2,6]{1,0:T(2,128)}, u32[]{:S(2)}) copy-start(s32[2,6]{1,0:T(2,128)} %tile_lists.1) | copy-start | bytes 148
  60.4 12.0 %collective-permute-start.7 = (bf16[4,2,512,256]{3,2,1,0:T(8,128)(2,1)}, bf16[4,2,512,256]{3,2,1,0:T(8,128)(2,1)}, u32[]{:S(2)}, u32[]{:S(2)}) collective-permute-start(bf16[4,2,512,256]{3,2,1,0:T(8,128)(2,1)} %stack.1.w_near_in), channel_id=1, source_target_pairs={{0,64},{64,0},{1,65},{65,1},{2,66},{66,2},{3,67},{67,3},{4,68},{68... | collective-permute-start | bytes 6291464 | tf_op jit(solution)/shard_map/ppermute | solution.py:235
